TPU v7x, 128 devices: a whole 4x4x4 slice. The times are simulated.
128 devices in a mesh: ens: 8 (over y, core), space: 16 (over z, x).
Axes of the slice: x: 4, y: 4, z: 4, core: 2. Of those that a mesh axis runs over, the one named last changes fastest.
Arguments:
- prior_profiles: bfloat16 [256, 128, 64, 128], P('ens', 'space'), may hold values from -6 to 6
- conductivity_profile: bfloat16 [256, 128, 64, 128], P('ens', 'space'), may hold values from 0.5 to 2
- sensor_position_flat: int32 [16384], P('space'), may hold values from 0 to 65535
- observation_slot_count: int32 [16], P('space'), may hold values from 1 to 1024, 10240 in all
- obs_values: float32 [16384], P('space'), may hold values from -6 to 6
- obs_std: float32 [16384], P('space'), may hold values from 0.3 to 3
- obs_noise: float32 [256, 16384], P('ens', 'space'), may hold values from -6 to 6
- params: float32 [256, 2048], P('ens', 'space'), may hold values from -6 to 6
Outputs:
- posterior_parameters: float32 [256, 2048], P('ens', 'space')
- predicted_states: float32 [256, 128, 64, 128], P('ens', 'space')
Inputs may be any that keep to these rules, and one draw needn't show every extreme that they name: The live slots of a slab are its first observation_slot_count ones.
All inputs are finite; a program needn't handle non-finite values. No bound on the sum of `observation_slot_count` on one device may be relied on, other than what follows from the above.
Results may differ from a plain program's by a relative error of at most 0.0003.
Values may be sent and summed in bfloat16 or wider, within the bound.
No kernel may reach another device: no remote copies, remote signals or barrier semaphores. Data moves between devices by JAX's collectives and lax.ppermute only.
A program may use at most 256 MiB of HBM per device.

v0:
```python
import math

import jax
import jax.numpy as jnp
from jax import lax
from jax.sharding import PartitionSpec as P

step_size = 0.08


def extended(cells, sides, width):
    for axis, dim in sides:
        count = lax.axis_size(axis)
        ends = count - 1
        head = lax.slice_in_dim(cells, 0, width, axis=dim)
        tail = lax.slice_in_dim(cells, cells.shape[dim] - width, cells.shape[dim], axis=dim)
        cells = jnp.concatenate(
            [
                lax.ppermute(tail, axis, [(i, (i + 1) % count) for i in range(ends)]),
                cells,
                lax.ppermute(head, axis, [((i + 1) % count, i) for i in range(ends)]),
            ],
            axis=dim,
        )
    return cells


def inner_window(array, starts):
    for dimension in range(3):
        which_axis = array.ndim - 3 + dimension
        extent = array.shape[which_axis] - 2
        array = lax.slice_in_dim(
            array, starts[dimension], starts[dimension] + extent, axis=which_axis
        )
    return array


def spread_heat_onestep(field, coeff):
    centre_u = inner_window(field, (1, 1, 1))
    centre_k = inner_window(coeff, (1, 1, 1))
    flux = jnp.zeros_like(centre_u)
    for dimension in range(3):
        for offset in (0, 2):
            starts = [1, 1, 1]
            starts[dimension] = offset
            neigh_u = inner_window(field, tuple(starts))
            neigh_k = inner_window(coeff, tuple(starts))
            flux = flux + 0.5 * (centre_k + neigh_k) * (neigh_u - centre_u)
    return centre_u + step_size * flux


def shards(
    prior_profiles,
    conductivity_profile,
    sensor_position_flat,
    observation_slot_count,
    obs_values,
    obs_std,
    obs_noise,
    params,
):
    stacked = jnp.stack([prior_profiles, conductivity_profile])
    bordered_profile = extended(stacked, (("space", 2),), 1)
    bordered_profile = jnp.pad(
        bordered_profile.astype(jnp.float32), ((0, 0), (0, 0), (0, 0), (1, 1), (1, 1))
    )
    predicted_states = spread_heat_onestep(bordered_profile[0], bordered_profile[1])
    resident_realizations = predicted_states.shape[0]
    sampled_readings = jnp.take(
        predicted_states.reshape(resident_realizations, -1), sensor_position_flat, axis=1
    )
    live_slots = (
        jnp.arange(sensor_position_flat.shape[0], dtype=jnp.int32) < observation_slot_count[0]
    )
    ensemble = resident_realizations * lax.axis_size("ens")
    ens_scale = math.sqrt(ensemble - 1.0)
    ens_rank = lax.axis_index("ens")
    all_picked, all_noise = (
        lax.all_gather(sampled_readings, "ens", axis=0, tiled=True),
        lax.all_gather(obs_noise, "ens", axis=0, tiled=True),
    )
    centre = jnp.mean(all_picked, axis=0)
    spread = jnp.where(live_slots, (all_picked - centre) / (obs_std * ens_scale), 0.0)
    misfit = jnp.where(live_slots, (obs_values - all_picked) / obs_std + all_noise, 0.0)
    cross_part = jnp.dot(spread, misfit.T, precision=lax.Precision.HIGHEST)
    gram_matrix = jnp.dot(spread, spread.T, precision=lax.Precision.HIGHEST)
    gram_matrix, cross_part = lax.psum((gram_matrix, cross_part), "space")
    factor = jnp.linalg.cholesky(gram_matrix + jnp.eye(ensemble, dtype=jnp.float32))
    solved = jax.scipy.linalg.cho_solve((factor, True), cross_part)
    all_params = lax.all_gather(params, "ens", axis=0, tiled=True)
    anomaly = (all_params - jnp.mean(all_params, axis=0)) / ens_scale
    own_weights = lax.dynamic_slice_in_dim(
        solved, ens_rank * resident_realizations, resident_realizations, 1
    )
    posterior_parameters = params + jnp.dot(own_weights.T, anomaly, precision=lax.Precision.HIGHEST)
    return (posterior_parameters, predicted_states)


def solution(mesh):
    in_specs = (
        P("ens", "space", None, None),
        P("ens", "space", None, None),
        P("space"),
        P("space"),
        P("space"),
        P("space"),
        P("ens", "space"),
        P("ens", "space"),
    )
    out_specs = (P("ens", "space"), P("ens", "space", None, None))
    return jax.shard_map(shards, mesh=mesh, in_specs=in_specs, out_specs=out_specs, check_vma=False)
```

profile of v0, /device:TPU:1, one launch (start us, length us, event | category | flops | bytes accessed | tf_op | source)
XLA Modules:
  0.0 421.7 jit_solution(3602188360894715256)
XLA Ops:
  7.2 0.0 all-gather.3.cloned.1.call-start
  7.2 1.9 pad_maximum_fusion.1
  9.1 4.3 %collective-permute-start = (bf16[2,32,1,64,128]{4,3,2,1,0:T(8,128)(2,1)S(1)}, bf16[2,32,1,64,128]{4,3,2,1,0:T(8,128)(2,1)S(1)}, u32[]{:S(2)}, u32[]{:S(2)}) collective-permute-start(bf16[2,32,1,64,128]{4,3,2,1,0:T(8,128)(2,1)S(1)} %get-tuple-element.24), channel_id=1, source_target_pairs={{0,1},{1,2},{2,3},{3,4},{4,5},{5,6},{6,7},{7,8},{8,9},{9,10},{10,1... | collective-permute-start | bytes 3145736 | tf_op jit(solution)/shard_map/ppermute | solution.py:19
  13.4 1.3 collective-permute-start.1
  14.7 20.4 %collective-permute-done = bf16[2,32,1,64,128]{4,3,2,1,0:T(8,128)(2,1)S(1)} collective-permute-done((bf16[2,32,1,64,128]{4,3,2,1,0:T(8,128)(2,1)S(1)}, bf16[2,32,1,64,128]{4,3,2,1,0:T(8,128)(2,1)S(1)}, u32[]{:S(2)}, u32[]{:S(2)}) %collective-permute-start) | collective-permute-done | bytes 1048608 | tf_op jit(solution)/shard_map/ppermute | solution.py:19
  35.1 3.9 collective-permute-done.1
  39.0 23.2 %fusion.3 = f32[2,32,10,66,130]{4,3,2,1,0:T(8,128)} fusion(bf16[2,32,1,64,128]{4,3,2,1,0:T(8,128)(2,1)S(1)} %collective-permute-done.1, bf16[2,32,1,64,128]{4,3,2,1,0:T(8,128)(2,1)S(1)} %collective-permute-done, bf16[1,32,8,64,128]{4,3,2,1,0:T(8,128)(2,1)S(1)} %bitcast.49, bf16[1,32,8,64,128]{4,3,2,1,0:T(8,128)(2,1)S(1)} %bitcast.51), kind=kLoop, calls=%fused_computation.13 | loop fusion | flops 126297600 | bytes 32450560 | tf_op jit(solution)/shard_map/jit(_pad)/pad | solution.py:64
  62.2 31.2 %slice_bitcast_fusion = (f32[32,10,66,130]{3,2,1,0:T(8,128)}, f32[32,10,66,130]{3,2,1,0:T(8,128)}) fusion(f32[2,32,10,66,130]{4,3,2,1,0:T(8,128)} %fusion.3), kind=kLoop, calls=%fused_computation.10 | loop fusion | bytes 43929600 | tf_op jit(solution)/shard_map/squeeze | solution.py:67
  93.4 79.4 %fusion.12 = f32[32,8,64,128]{3,2,1,0:T(8,128)} fusion(f32[32,10,66,130]{3,2,1,0:T(8,128)} %get-tuple-element.23, f32[32,10,66,130]{3,2,1,0:T(8,128)} %get-tuple-element.22), kind=kLoop, calls=%fused_computation.24 | loop fusion | flops 65011712 | bytes 125829120 | tf_op jit(solution)/shard_map/add | solution.py:49
  172.9 19.7 %copy.14 = f32[32,8,64,128]{0,3,2,1:T(8,128)} copy(f32[32,8,64,128]{3,2,1,0:T(8,128)} %fusion.12) | data formatting | bytes 16777216 | tf_op jit(solution)/shard_map/add | solution.py:49
  192.6 13.4 %gather_fusion = f32[1024,32]{1,0:T(8,128)S(1)} fusion(f32[32,65536]{0,1:T(8,128)} %bitcast.47, s32[1024]{0:T(1024)S(1)} %fusion.61), kind=kCustom, calls=%fused_computation | custom fusion | bytes 266240 | tf_op jit(solution)/shard_map/jit(_take)/gather | solution.py:69
  206.0 0.2 select_bitcast_fusion
  206.2 0.8 copy.15
  207.0 0.0 all-gather.3.cloned.1.call-update
  207.0 0.0 all-gather.5.cloned.1.call-start
  207.1 0.7 all-gather.5.cloned.1.call-update
  207.8 0.0 all-reduce.5.cloned.1.call-start
  208.5 27.7 %all-gather.3.cloned.1.call-done = f32[256,1024]{1,0:T(8,128)} async-done(((f32[32,1024]{1,0:T(8,128)}), f32[256,1024]{1,0:T(8,128)}) %all-gather.3.cloned.1.call-update) | async-done | bytes 1048592 | tf_op jit(solution)/shard_map/all_gather | solution.py:79
  236.2 1.3 reduce_sum.18
  237.6 3.5 fusion.33
  241.0 20.2 %all-gather.5.cloned.1.call-done = f32[256,1024]{1,0:T(8,128)} async-done(((f32[32,1024]{1,0:T(8,128)}), f32[256,1024]{1,0:T(8,128)}) %all-gather.5.cloned.1.call-update) | async-done | bytes 1048592 | tf_op jit(solution)/shard_map/all_gather | solution.py:80
  261.2 3.8 fusion.28
  265.0 0.0 all-reduce.5.cloned.1.call-update
  265.1 13.0 %all_gather.11 = f32[256,128]{1,0:T(8,128)S(1)} all-gather(f32[32,128]{1,0:T(8,128)S(1)} %copy-done.2), channel_id=1, replica_groups=mesh['ens'=8,'space'=16] {'ens'}, dimensions={0}, use_global_device_ids=true | all-gather | bytes 147456 | tf_op jit(solution)/shard_map/all_gather | solution.py:90
  278.1 70.5 %all-reduce.5.cloned.1.call-done = (f32[256,256]{1,0:T(8,128)}, f32[256,256]{0,1:T(8,128)}) async-done(((f32[256,256]{1,0:T(8,128)}, f32[256,256]{0,1:T(8,128)}), (f32[256,256]{1,0:T(8,128)}, f32[256,256]{0,1:T(8,128)})) %all-reduce.5.cloned.1.call-update) | async-done | bytes 524304 | tf_op jit(solution)/shard_map/psum | solution.py:87
  348.7 1.0 convert_add_fusion
  349.6 0.1 copy.17
  349.8 1.0 fusion.44
  350.8 11.7 %cholesky.50 = f32[128,128]{1,0:T(8,128)S(1)} custom-call(f32[128,128]{1,0:T(8,128)S(1)} %cholesky.118), custom_call_target="Cholesky" | custom-call | tf_op jit(solution)/shard_map/jit(cholesky)/cholesky | solution.py:88
  362.6 9.8 %custom-call.18 = f32[1,128,128]{1,2,0:T(8,128)S(1)} custom-call(f32[1,128,128]{2,1,0:T(8,128)S(1)} %get-tuple-element.29), custom_call_target="InvertDiagBlocksLowerTriangular" | custom-call | tf_op jit(solution)/shard_map/jit(cholesky)/cholesky | solution.py:88
  372.4 0.2 constant_dynamic-update-slice_fusion
  372.6 0.3 convolution_subtract_fusion.2
  372.8 11.7 %cholesky.105 = f32[128,128]{1,0:T(8,128)S(1)} custom-call(f32[128,128]{1,0:T(8,128)S(1)} %convolution_subtract_fusion.2), custom_call_target="Cholesky" | custom-call | tf_op jit(solution)/shard_map/jit(cholesky)/cholesky | solution.py:88
  384.6 0.7 compare_reduce_fusion
  386.6 0.1 triangular_solve.69
  386.7 4.1 while.1
  386.9 0.6 fusion.76
  387.5 1.3 bitcast_dynamic-update-slice_fusion.2
  388.9 0.6 fusion.76
  389.5 1.3 bitcast_dynamic-update-slice_fusion.2
  390.8 19.7 %custom-call.19 = f32[2,128,128]{1,2,0:T(8,128)S(1)} custom-call(f32[2,128,128]{2,1,0:T(8,128)S(1)} %get-tuple-element.9), custom_call_target="InvertDiagBlocksLowerTriangular" | custom-call | tf_op jit(solution)/shard_map/jit(_cho_solve)/triangular_solve | solution.py:89
  410.5 1.2 fusion.47
  411.7 1.2 convolution_subtract_fusion.1
  412.9 0.3 fusion.58
  413.2 0.3 fusion.57
  413.5 0.3 convolution_subtract_fusion
  413.8 0.3 fusion.56
  414.1 1.1 convolution_add_fusion
  (28 shorter events, 0.3 us)
Async XLA Ops:
  7.2 7.5 %copy-start.3 = (s32[1024]{0:T(1024)S(1)}, s32[1024]{0:T(1024)}, u32[]{:S(2)}) copy-start(s32[1024]{0:T(1024)} %param.10) | copy-start | bytes 12292
  7.2 229.1 %all-gather.3.cloned.1.call-start = ((), (), s32[]{:S(2)}) async-start(), calls=%async_computation | async-start | bytes 1179648 | tf_op jit(solution)/shard_map/all_gather | solution.py:79
  7.2 31.8 %copy-start = (bf16[32,8,64,128]{3,2,1,0:T(8,128)(2,1)S(1)}, bf16[32,8,64,128]{3,2,1,0:T(8,128)(2,1)}, u32[]{:S(2)}) copy-start(bf16[32,8,64,128]{3,2,1,0:T(8,128)(2,1)} %param.9) | copy-start | bytes 12582916
  7.2 31.8 %copy-start.1 = (bf16[32,8,64,128]{3,2,1,0:T(8,128)(2,1)S(1)}, bf16[32,8,64,128]{3,2,1,0:T(8,128)(2,1)}, u32[]{:S(2)}) copy-start(bf16[32,8,64,128]{3,2,1,0:T(8,128)(2,1)} %param.8) | copy-start | bytes 12582916
  9.1 26.0 %collective-permute-start = (bf16[2,32,1,64,128]{4,3,2,1,0:T(8,128)(2,1)S(1)}, bf16[2,32,1,64,128]{4,3,2,1,0:T(8,128)(2,1)S(1)}, u32[]{:S(2)}, u32[]{:S(2)}) collective-permute-start(bf16[2,32,1,64,128]{4,3,2,1,0:T(8,128)(2,1)S(1)} %get-tuple-element.24), channel_id=1, source_target_pairs={{0,1},{1,2},{2,3},{3,4},{4,5},{5,6},{6,7},{7,8},{8,9},{9,10},{10,1... | collective-permute-start | bytes 3145736 | tf_op jit(solution)/shard_map/ppermute | solution.py:19
  13.4 25.6 %collective-permute-start.1 = (bf16[2,32,1,64,128]{4,3,2,1,0:T(8,128)(2,1)S(1)}, bf16[2,32,1,64,128]{4,3,2,1,0:T(8,128)(2,1)S(1)}, u32[]{:S(2)}, u32[]{:S(2)}) collective-permute-start(bf16[2,32,1,64,128]{4,3,2,1,0:T(8,128)(2,1)S(1)} %get-tuple-element.25), channel_id=1, source_target_pairs={{1,0},{2,1},{3,2},{4,3},{5,4},{6,5},{7,6},{8,7},{9,8},{10,9},{11,1... | collective-permute-start | bytes 3145736 | tf_op jit(solution)/shard_map/ppermute | solution.py:21
  172.9 35.7 %copy-start.4 = (f32[1024]{0:T(1024)S(1)}, f32[1024]{0:T(1024)}, u32[]{:S(2)}) copy-start(f32[1024]{0:T(1024)} %param.13) | copy-start | bytes 12292
  192.6 68.6 %copy-start.5 = (f32[1024]{0:T(1024)S(1)}, f32[1024]{0:T(1024)}, u32[]{:S(2)}) copy-start(f32[1024]{0:T(1024)} %param.12) | copy-start | bytes 12292
  206.2 58.9 %copy-start.2 = (f32[32,128]{1,0:T(8,128)S(1)}, f32[32,128]{1,0:T(8,128)}, u32[]{:S(2)}) copy-start(f32[32,128]{1,0:T(8,128)} %param.15) | copy-start | bytes 49156
  207.0 54.2 %all-gather.5.cloned.1.call-start = ((), (), s32[]{:S(2)}) async-start(), calls=%async_computation.1 | async-start | bytes 1179648 | tf_op jit(solution)/shard_map/all_gather | solution.py:80
  207.8 140.9 %all-reduce.5.cloned.1.call-start = ((), (), s32[]{:S(2)}) async-start(), calls=%async_computation.2 | async-start | bytes 1048576 | tf_op jit(solution)/shard_map/psum | solution.py:87
Sparse Core Ops, SparseCore 0:
  207.2 29.0 all-gather.2
  238.0 23.2 all-gather.4
  265.2 83.4 all-reduce.4
where the time goes:
time: 423 us; the launch traced here: 422 us
  other arithmetic  162 us (38%)
  waiting for transfers between devices  143 us (34%)
  local copies, waits for them, and re-layouts  69.3 us (16%)
  between operations  15.9 us (4%)
  blocking collectives  13 us (3%)
  matrix products  12.4 us (3%)
  starting transfers between devices  5.68 us (1%)
    add x1, other arithmetic, spread_heat_onestep(): return centre_u + step_size * flux  79.4 us
    psum x1, waiting for transfers between devices, shards(): gram_matrix, cross_part = lax.psum((gram_matrix, cross_part), 'space')  70.5 us
    another operation x6, other arithmetic, shards(): jnp.linalg.cholesky(gram_matrix + jnp.eye(ensemble, dtype=jnp.float32))  34 us
    squeeze x1, local copies, waits for them, and re-layouts, shards(): bordered_profile[1]  31.2 us
    all_gather x1, waiting for transfers between devices, shards(): lax.all_gather(sampled_readings, 'ens', axis=0, tiled=True)  27.7 us
    pad x1, other arithmetic, shards(): jnp.pad(bordered_profile.astype(jnp.float32), ((0, 0), (0, 0), (0, 0), (1...  23.2 us
    ppermute x1, waiting for transfers between devices, extended(): lax.ppermute(tail, axis, [(i, (i + 1) % count) for i in range(ends)])  20.4 us
    all_gather x1, waiting for transfers between devices, shards(): lax.all_gather(obs_noise, 'ens', axis=0, tiled=True)  20.2 us
  transfers between devices with their start and end apart: 5, of which 5 were waited for; matrix products, arithmetic and copies ran while one was open for 1% of the time, Pallas kernels for 0%

commit v1 on v0

v1 whole, which is shorter than its diff:
```python
import math

import jax
import jax.numpy as jnp
from jax import lax
from jax.experimental import pallas as pl
from jax.experimental.pallas import tpu as pltpu
from jax.sharding import PartitionSpec as P

step_size = 0.08
HIGH = lax.Precision.HIGHEST
F32 = jnp.float32


def shift_down(a, first):
    return jnp.concatenate([first, a[:-1]], axis=0)


def shift_up(a):
    return jnp.concatenate([a[1:], jnp.zeros_like(a[:1])], axis=0)


def sample(pos_ref, src_ref, dst_ref, stride, place, initial=None):
    members, slots = dst_ref.shape
    groups = members // 8
    lane = lax.broadcasted_iota(jnp.int32, (8, 128), 1)

    def block(jb, _):
        def chunk(jc, accs):
            accs = list(accs)
            for t in range(8):
                j = jc * 8 + t
                p = pos_ref[jb * 128 + j]
                row, used = place(p)
                target = j if used is None else jnp.where(used, j, -1)
                turn = (j - p) & 127
                here = lane == target
                for g in range(groups):
                    v = src_ref[pl.ds(g * 8 * stride + row, 8, stride=stride), :]
                    accs[g] = jnp.where(here, pltpu.roll(v, turn, 1), accs[g])
            return tuple(accs)

        at = pl.ds(pl.multiple_of(jb * 128, 128), 128)
        if initial is None:
            start = tuple(jnp.zeros((8, 128), F32) for _ in range(groups))
        else:
            start = tuple(jnp.zeros((8, 128), F32) for _ in range(groups))
        accs = lax.fori_loop(0, 16, chunk, start)
        for g in range(groups):
            value = accs[g]
            if initial is not None:
                value = value + initial[g * 8 : g * 8 + 8, at]
            dst_ref[g * 8 : g * 8 + 8, at] = value
        return 0

    lax.fori_loop(0, slots // 128, block, 0)


def stencil_kernel(pos_ref, u_ref, k_ref, out_ref, picked_ref, state, sem):
    i = pl.program_id(0)
    members, layers, nx, ny = u_ref.shape
    lane = lax.broadcasted_iota(jnp.int32, (nx, ny), 1)
    first_lane, last_lane = lane == 0, lane == ny - 1
    half = step_size * 0.5

    def member(b, _):
        base = (i * members + b) * layers * nx
        u = u_ref[b, 0].astype(F32)
        k = k_ref[b, 0].astype(F32)
        below = None
        for z in range(layers):
            ku = k * u
            un = jnp.where(last_lane, 0.0, pltpu.roll(u, ny - 1, 1))
            kn = jnp.where(last_lane, 0.0, pltpu.roll(k, ny - 1, 1))
            f = (k + kn) * (un - u)
            acc = f - jnp.where(first_lane, ku, pltpu.roll(f, 1, 1))
            f = (k + shift_up(k)) * (shift_up(u) - u)
            acc = acc + (f - shift_down(f, ku[:1]))
            if below is not None:
                acc = acc - below
            u_now = u
            if z < layers - 1:
                u_next = u_ref[b, z + 1].astype(F32)
                k_next = k_ref[b, z + 1].astype(F32)
                below = (k + k_next) * (u_next - u)
                acc = acc + below
                u, k = u_next, k_next
            state[pl.ds(pl.multiple_of(base + z * nx, 8), nx), :] = u_now + half * acc
        return 0

    lax.fori_loop(0, members, member, 0)
    rows = members * layers * nx

    def push(step):
        part = pl.ds(pl.multiple_of(step * rows, 8), rows)
        return pltpu.make_async_copy(state.at[part, :], out_ref.at[part, :], sem.at[step])

    push(i).start()

    @pl.when(i == pl.num_programs(0) - 1)
    def _():
        sample(pos_ref, state, picked_ref, layers * nx, lambda p: (p >> 7, None))
        for step in range(state.shape[0] // rows):
            push(step).wait()


def stencil(pos, u, k):
    m, layers, nx, ny = u.shape
    per = 4
    block = pl.BlockSpec((per, layers, nx, ny), lambda i: (i, 0, 0, 0))
    rows = m * layers * nx
    return pl.pallas_call(
        stencil_kernel,
        grid=(m // per,),
        in_specs=[pl.BlockSpec(memory_space=pltpu.SMEM), block, block],
        out_specs=[
            pl.BlockSpec(memory_space=pl.ANY),
            pl.BlockSpec((m, pos.shape[0]), lambda i: (0, 0)),
        ],
        out_shape=[
            jax.ShapeDtypeStruct((rows, ny), F32),
            jax.ShapeDtypeStruct((m, pos.shape[0]), F32),
        ],
        scratch_shapes=[pltpu.VMEM((rows, ny), F32), pltpu.SemaphoreType.DMA((m // per,))],
        compiler_params=pltpu.CompilerParams(vmem_limit_bytes=32 << 20),
        cost_estimate=pl.CostEstimate(
            flops=40 * u.size, bytes_accessed=8 * u.size, transcendentals=0
        ),
    )(pos, u, k)


def faces_kernel(pos_ref, u_ref, k_ref, lo_ref, hi_ref, in_ref, partial_ref, out_ref, picked_ref, extra):
    g, side = pl.program_id(0), pl.program_id(1)
    members, _, nx, ny = u_ref.shape
    half = step_size * 0.5

    def apply(halo):
        def member(b, _):
            u = u_ref[b, 0].astype(F32)
            k = k_ref[b, 0].astype(F32)
            un = halo[0, b].astype(F32)
            kn = halo[1, b].astype(F32)
            d = half * ((k + kn) * (un - u))
            out_ref[b, 0] = in_ref[b, 0] + d
            at = ((g * members + b) * 2 + side) * nx
            extra[pl.ds(pl.multiple_of(at, 8), nx), :] = d
            return 0

        lax.fori_loop(0, members, member, 0)

    @pl.when(side == 0)
    def _():
        apply(lo_ref)

    @pl.when(side == 1)
    def _():
        apply(hi_ref)

    def place(p):
        z = p >> 13
        return ((z >> 2) << 6) + ((p >> 7) & 63), (z == 0) | (z == 7)

    @pl.when((g == pl.num_programs(0) - 1) & (side == 1))
    def _():
        sample(pos_ref, extra, picked_ref, 2 * nx, place, partial_ref)


def faces(pos, u, k, lo, hi, states, partial):
    m, layers, nx, ny = u.shape
    per = 8
    face = pl.BlockSpec((per, 1, nx, ny), lambda g, s: (g, s * (layers - 1), 0, 0))
    halo = pl.BlockSpec((2, per, nx, ny), lambda g, s: (0, g, 0, 0))
    flat = pl.BlockSpec(partial.shape, lambda g, s: (0, 0))
    return pl.pallas_call(
        faces_kernel,
        grid=(m // per, 2),
        in_specs=[pl.BlockSpec(memory_space=pltpu.SMEM), face, face, halo, halo, face, flat],
        out_specs=[face, flat],
        out_shape=[
            jax.ShapeDtypeStruct(states.shape, F32),
            jax.ShapeDtypeStruct(partial.shape, F32),
        ],
        scratch_shapes=[pltpu.VMEM((m * 2 * nx, ny), F32)],
        input_output_aliases={5: 0},
        compiler_params=pltpu.CompilerParams(vmem_limit_bytes=32 << 20),
        cost_estimate=pl.CostEstimate(
            flops=8 * m * nx * ny, bytes_accessed=24 * m * nx * ny, transcendentals=0
        ),
    )(pos, u, k, lo, hi, states, partial)


def contract(a, b, dims):
    return lax.dot_general(a, b, (dims, ((), ())), precision=HIGH, preferred_element_type=F32)


def gram_kernel(scale, count_ref, *refs):
    blocks, (noise, values, std, gram_ref, cross_ref) = refs[:8], refs[8:]
    rows = blocks[0].shape[0]
    own = blocks[0][...]
    total = own
    for b in blocks[1:]:
        total = total + b[...]
    centre = jnp.sum(total, axis=0, keepdims=True) * (1.0 / (8 * rows))
    live = lax.broadcasted_iota(jnp.int32, centre.shape, 1) < count_ref[0]
    weight = jnp.where(live, 1.0 / (std[...] * scale), 0.0)
    spread = jnp.concatenate([(b[...] - centre) * weight for b in blocks], axis=0)
    misfit = jnp.where(live, (values[...] - own) / std[...] + noise[...], 0.0)
    gram_ref[...] = contract(spread[: 4 * rows], spread, ((1,), (1,)))
    cross_ref[...] = contract(misfit, spread, ((1,), (1,)))


def gram(count, blocks, noise, values, std, ens_scale):
    rows = blocks[0].shape[0]
    vmem = pl.BlockSpec(memory_space=pltpu.VMEM)
    return pl.pallas_call(
        lambda *refs: gram_kernel(ens_scale, *refs),
        in_specs=[pl.BlockSpec(memory_space=pltpu.SMEM)] + [vmem] * 11,
        out_specs=[vmem, vmem],
        out_shape=[
            jax.ShapeDtypeStruct((4 * rows, 8 * rows), F32),
            jax.ShapeDtypeStruct((rows, 8 * rows), F32),
        ],
        compiler_params=pltpu.CompilerParams(vmem_limit_bytes=32 << 20),
    )(count, *blocks, noise, values.reshape(1, -1), std.reshape(1, -1))


def spd_inverse(p):
    n = p.shape[0]
    row_id = lax.broadcasted_iota(jnp.int32, (n, n), 0)
    lane_id = lax.broadcasted_iota(jnp.int32, (1, n), 1)
    for i in range(0, n, 2):
        row0, row1 = p[i : i + 1], p[i + 1 : i + 2]
        col0 = jnp.broadcast_to(p[:, i : i + 1], (n, n))
        col1 = jnp.broadcast_to(p[:, i + 1 : i + 2], (n, n))
        a, b, c = col0[i : i + 1], col0[i + 1 : i + 2], col1[i + 1 : i + 2]
        r = 1.0 / (a * c - b * b)
        at0, at1 = lane_id == i, lane_id == i + 1
        in_pair = at0 | at1
        e0 = jnp.where(in_pair, jnp.where(at0, 1.0, 0.0), row0)
        e1 = jnp.where(in_pair, jnp.where(at1, 1.0, 0.0), row1)
        new0 = (c * r) * e0 - (b * r) * e1
        new1 = (a * r) * e1 - (b * r) * e0
        rest = jnp.where(in_pair, 0.0, p) - col0 * new0 - col1 * new1
        p = jnp.where(row_id == i, new0, jnp.where(row_id == i + 1, new1, rest))
    return p


def solve_kernel(scale, *refs):
    tops, bottoms, (other,) = refs[:4], refs[4:8], refs[8:9]
    blocks, (x_ref,) = refs[9:17], refs[17:]
    top = tops[0][...] + tops[1][...] + tops[2][...] + tops[3][...]
    bottom = bottoms[0][...] + bottoms[1][...] + bottoms[2][...] + bottoms[3][...]
    rows = jnp.concatenate([top, bottom], axis=0)
    n = rows.shape[0]
    eye = jnp.where(
        lax.broadcasted_iota(jnp.int32, (n, n), 0) == lax.broadcasted_iota(jnp.int32, (n, n), 1),
        1.0,
        0.0,
    )
    params = jnp.concatenate([b[...] for b in blocks], axis=0)
    anomaly = (params - jnp.sum(params, axis=0, keepdims=True) * (1.0 / (2 * n))) * (1.0 / scale)
    ff, fs = rows[:, :n] + eye, rows[:, n:]
    first = spd_inverse(ff)
    right = contract(first, jnp.concatenate([fs, anomaly[:n]], axis=1), ((1,), (0,)))
    down = contract(fs, right, ((0,), (0,)))
    second = spd_inverse(other[...] + eye - down[:, :n])
    x_second = contract(second, anomaly[n:] - down[:, n:], ((1,), (0,)))
    x_ref[:n] = right[:, n:] - contract(right[:, :n], x_second, ((1,), (0,)))
    x_ref[n:] = x_second


def solve(tops, bottoms, other, blocks, ens_scale):
    n = other.shape[0]
    vmem = pl.BlockSpec(memory_space=pltpu.VMEM)
    return pl.pallas_call(
        lambda *refs: solve_kernel(ens_scale, *refs),
        in_specs=[vmem] * 17,
        out_specs=vmem,
        out_shape=jax.ShapeDtypeStruct((2 * n, blocks[0].shape[1]), F32),
        compiler_params=pltpu.CompilerParams(vmem_limit_bytes=32 << 20),
        cost_estimate=pl.CostEstimate(
            flops=8 << 30, bytes_accessed=1 << 20, transcendentals=0
        ),
    )(*tops, *bottoms, other, *blocks)


def final_kernel(*refs):
    parts, (params, x_ref, out_ref) = refs[:4], refs[4:]
    cross = parts[0][...] + parts[1][...] + parts[2][...] + parts[3][...]
    out_ref[...] = params[...] + contract(cross, x_ref[...], ((1,), (0,)))


def final(parts, params, x):
    vmem = pl.BlockSpec(memory_space=pltpu.VMEM)
    return pl.pallas_call(
        final_kernel,
        in_specs=[vmem] * 6,
        out_specs=vmem,
        out_shape=jax.ShapeDtypeStruct(params.shape, F32),
    )(*parts, params, x)


def around_x(a):
    return [a] + [
        lax.ppermute(
            a, "space", [(z * 4 + x, z * 4 + (x + s) % 4) for z in range(4) for x in range(4)]
        )
        for s in (1, 3, 2)
    ]


def around_z(a):
    return [a] + [
        lax.ppermute(
            a, "space", [(z * 4 + x, (z + s) % 4 * 4 + x) for z in range(4) for x in range(4)]
        )
        for s in (1, 3, 2)
    ]


def around_y(a):
    return [a] + [
        lax.ppermute(a, "ens", [(e, (e + 2 * s) % 8) for e in range(8)]) for s in (1, 3, 2)
    ]


def partner(a):
    return lax.ppermute(a, "ens", [(e, e ^ 1) for e in range(8)])


def total4(parts):
    return (parts[0] + parts[1]) + (parts[2] + parts[3])


def shards(u, k, pos, count, values, std, noise, params):
    spaces = lax.axis_size("space")
    ens_scale = math.sqrt(u.shape[0] * lax.axis_size("ens") - 1.0)
    last = jnp.stack([u[:, -1], k[:, -1]])
    head = jnp.stack([u[:, 0], k[:, 0]])
    lo = lax.ppermute(last, "space", [(i, i + 1) for i in range(spaces - 1)])
    hi = lax.ppermute(head, "space", [(i + 1, i) for i in range(spaces - 1)])
    states, partial = stencil(pos, u, k)
    states, picked = faces(pos, u, k, lo, hi, states.reshape(u.shape), partial)

    mine = around_y(picked)
    blocks = mine + [partner(a) for a in mine]
    mine = around_y(params)
    param_blocks = mine + [partner(a) for a in mine]

    gram_rows, cross = gram(count, blocks, noise, values, std, ens_scale)
    n = gram_rows.shape[0]
    tops = around_z(total4(around_x(gram_rows[: n // 2])))
    bottoms = around_x(total4(around_z(gram_rows[n // 2 :])))
    square = jnp.concatenate([total4(tops)[:, :n], total4(bottoms)[:, :n]], axis=0)
    other = partner(square)
    crosses = around_z(total4(around_x(cross)))
    x = solve(tops, bottoms, other, param_blocks, ens_scale)
    return final(crosses, params, x), states


def solution(mesh):
    in_specs = (
        P("ens", "space", None, None),
        P("ens", "space", None, None),
        P("space"),
        P("space"),
        P("space"),
        P("space"),
        P("ens", "space"),
        P("ens", "space"),
    )
    out_specs = (P("ens", "space"), P("ens", "space", None, None))
    return jax.shard_map(shards, mesh=mesh, in_specs=in_specs, out_specs=out_specs, check_vma=False)
```

time: 423 us -> 156 us (0.37)
  other arithmetic: 162 us -> 0.28 us
  waiting for transfers between devices: 143 us -> 4.52 us
  Pallas kernels: 0 us -> 89.1 us
  local copies, waits for them, and re-layouts: 69.3 us -> 3.78 us
  starting transfers between devices: 5.68 us -> 56.6 us
  between operations: 15.9 us -> 1.6 us
  blocking collectives: 13 us -> 0 us
  matrix products: 12.4 us -> 0 us
    pallas_call x0 -> x5, Pallas kernels: none -> 89.1 us  [the longest x1 37.7 us: stencil(): pl.pallas_call(stencil_kernel, grid=(m // per,), in_specs=[pl.BlockSpec(m...]
    add x2 -> x4, other arithmetic: 80.4 us -> 0.07 us  [total4(): return parts[0] + parts[1] + (parts[2] + parts[3])]
    psum x1 -> x0, waiting for transfers between devices: 70.5 us -> none  [shards(): gram_matrix, cross_part = lax.psum((gram_matrix, cross_part), 'space')]
    another operation x9 -> x2, other arithmetic: 53.7 us -> 0.2 us  [the longest x1 0.1 us: shards(): head = jnp.stack([u[:, 0], k[:, 0]])]
    ppermute x2 -> x35, starting transfers between devices: 5.57 us -> 56.6 us  [the longest x9 18 us: partner(): return lax.ppermute(a, 'ens', [(e, e ^ 1) for e in range(8)])]
    all_gather x2 -> x0, waiting for transfers between devices: 47.9 us -> none  [the longest x1 27.7 us: shards(): lax.all_gather(sampled_readings, 'ens', axis=0, tiled=True)]
    squeeze x1 -> x0, local copies, waits for them, and re-layouts: 31.2 us -> none  [shards(): bordered_profile[1]]
    pad x1 -> x0, other arithmetic: 23.2 us -> none  [shards(): jnp.pad(bordered_profile.astype(jnp.float32), ((0, 0), (0, 0), (0, 0), (1...]
  transfers between devices with their start and end apart: 5 -> 35, of which waited for: 5 -> 4; matrix products, arithmetic and copies ran while one was open for 1% -> 0% of each run, Pallas kernels for 0% -> 34%
where the time goes in v1:
time: 156 us
  Pallas kernels  89.1 us (57%)
  starting transfers between devices  56.6 us (36%)
  waiting for transfers between devices  4.52 us (3%)
  local copies, waits for them, and re-layouts  3.78 us (2%)
  between operations  1.6 us (1%)
    pallas_call x1, Pallas kernels, stencil(): pl.pallas_call(stencil_kernel, grid=(m // per,), in_specs=[pl.BlockSpec(m...  37.7 us
    pallas_call x1, Pallas kernels, faces(): pl.pallas_call(faces_kernel, grid=(m // per, 2), in_specs=[pl.BlockSpec(m...  32.5 us
    ppermute x9, starting transfers between devices, partner(): return lax.ppermute(a, 'ens', [(e, e ^ 1) for e in range(8)])  18 us
    pallas_call x1, Pallas kernels, solve(): pl.pallas_call(lambda *refs: solve_kernel(ens_scale, *refs), in_specs=[vm...  15.2 us
    ppermute x9, starting transfers between devices, around_x(): lax.ppermute(a, 'space', [(z * 4 + x, z * 4 + (x + s) % 4) for z in range...  12.7 us
    ppermute x9, starting transfers between devices, around_z(): lax.ppermute(a, 'space', [(z * 4 + x, (z + s) % 4 * 4 + x) for z in range...  12.1 us
    ppermute x6, starting transfers between devices, around_y(): lax.ppermute(a, 'ens', [(e, (e + 2 * s) % 8) for e in range(8)])  7.52 us
    ppermute x1, starting transfers between devices, shards(): lo = lax.ppermute(last, 'space', [(i, i + 1) for i in range(spaces - 1)])  4.64 us
  transfers between devices with their start and end apart: 35, of which 4 were waited for; matrix products, arithmetic and copies ran while one was open for 0% of the time, Pallas kernels for 34%

profile of v1, /device:TPU:1, one launch (start us, length us, event | category | flops | bytes accessed | tf_op | source)
XLA Modules:
  0.0 155.9 jit_solution(4654965877312942270)
XLA Ops:
  0.7 1.9 %slice_bitcast_fusion = (bf16[1,32,64,128]{3,2,1,0:T(8,128)(2,1)S(1)}, bf16[1,32,64,128]{3,2,1,0:T(8,128)(2,1)S(1)}, bf16[1,32,64,128]{3,2,1,0:T(8,128)(2,1)S(1)}, bf16[1,32,64,128]{3,2,1,0:T(8,128)(2,1)S(1)}) fusion(bf16[32,8,64,128]{3,2,1,0:T(8,128)(2,1)} %k_ref.3, bf16[32,8,64,128]{3,2,1,0:T(8,128)(2,1)} %u_ref.3), kind=kLoop, calls=%fused_computation.2 | loop fusion | bytes 4194304 | tf_op jit(solution)/shard_map/stack;squeeze | solution.py:339
  2.5 0.1 pad_maximum_fusion.1
  2.6 1.6 collective-permute-start.1
  4.3 4.6 %collective-permute-start = (bf16[2,32,64,128]{3,2,1,0:T(8,128)(2,1)S(1)}, bf16[2,32,64,128]{3,2,1,0:T(8,128)(2,1)S(1)}, u32[]{:S(2)}, u32[]{:S(2)}) collective-permute-start(bf16[2,32,64,128]{3,2,1,0:T(8,128)(2,1)S(1)} %pad_maximum_fusion), channel_id=1, source_target_pairs={{0,1},{1,2},{2,3},{3,4},{4,5},{5,6},{6,7},{7,8},{8,9},{9,10},{10,1... | collective-permute-start | bytes 3145736 | tf_op jit(solution)/shard_map/ppermute | solution.py:340
  9.0 37.7 %shard_map.95 = (f32[16384,128]{1,0:T(8,128)}, f32[32,1024]{1,0:T(8,128)S(1)}) custom-call(s32[1024]{0:T(1024)S(1)} %copy-done.5, bf16[32,8,64,128]{3,2,1,0:T(8,128)(2,1)S(1)} %copy-done, bf16[32,8,64,128]{3,2,1,0:T(8,128)(2,1)S(1)} %copy-done.1), custom_call_target="tpu_custom_call" | custom-call | flops 83886080 | bytes 16777216 | tf_op jit(solution)/shard_map/pallas_call | solution.py:112
  46.7 32.5 %shard_map.96 = (f32[32,8,64,128]{3,2,1,0:T(8,128)}, f32[32,1024]{1,0:T(8,128)S(1)}) custom-call(s32[1024]{0:T(1024)S(1)} %copy-done.5, bf16[32,8,64,128]{3,2,1,0:T(8,128)(2,1)S(1)} %copy-done, bf16[32,8,64,128]{3,2,1,0:T(8,128)(2,1)S(1)} %copy-done.1, bf16[2,32,64,128]{3,2,1,0:T(8,128)(2,1)S(1)} %collective-permute-done.lo_ref, ...), custom_call_target="tpu_custom_call", output_to_operand_aliasing={{0}: (5, {})} | custom-call | flops 2097152 | bytes 6291456 | tf_op jit(solution)/shard_map/pallas_call | solution.py:174
  79.2 1.5 collective-permute-start.2
  80.8 1.4 collective-permute-start.3
  82.2 1.6 %collective-permute-start.4 = (f32[32,1024]{1,0:T(8,128)S(1)}, f32[32,1024]{1,0:T(8,128)S(1)}, u32[]{:S(2)}, u32[]{:S(2)}) collective-permute-start(f32[32,1024]{1,0:T(8,128)S(1)} %get-tuple-element.10.refs_1_), channel_id=1, source_target_pairs={{0,64},{16,80},{32,96},{48,112},{64,0},{80,16},{96,32},{112,48},{1... | collective-permute-start | bytes 393224 | tf_op jit(solution)/shard_map/ppermute | solution.py:323
  83.8 2.1 %collective-permute-start.5 = (f32[32,1024]{1,0:T(8,128)S(1)}, f32[32,1024]{1,0:T(8,128)S(1)}, u32[]{:S(2)}, u32[]{:S(2)}) collective-permute-start(f32[32,1024]{1,0:T(8,128)S(1)} %get-tuple-element.10.refs_1_), channel_id=1, source_target_pairs={{0,16},{16,0},{32,48},{48,32},{64,80},{80,64},{96,112},{112,96},{1... | collective-permute-start | bytes 393224 | tf_op jit(solution)/shard_map/ppermute | solution.py:328
  85.9 0.9 collective-permute-start.6
  86.8 1.8 %collective-permute-start.7 = (f32[32,1024]{1,0:T(8,128)S(1)}, f32[32,1024]{1,0:T(8,128)S(1)}, u32[]{:S(2)}, u32[]{:S(2)}) collective-permute-start(f32[32,1024]{1,0:T(8,128)S(1)} %collective-permute-done.3.refs_3_), channel_id=1, source_target_pairs={{0,16},{16,0},{32,48},{48,32},{64,80},{80,64},{96,112},{112,96},{1... | collective-permute-start | bytes 393224 | tf_op jit(solution)/shard_map/ppermute | solution.py:328
  88.6 0.6 collective-permute-done.4.refs_4_
  89.2 1.7 %collective-permute-start.8 = (f32[32,1024]{1,0:T(8,128)S(1)}, f32[32,1024]{1,0:T(8,128)S(1)}, u32[]{:S(2)}, u32[]{:S(2)}) collective-permute-start(f32[32,1024]{1,0:T(8,128)S(1)} %collective-permute-done.4.refs_4_), channel_id=1, source_target_pairs={{0,16},{16,0},{32,48},{48,32},{64,80},{80,64},{96,112},{112,96},{1... | collective-permute-start | bytes 393224 | tf_op jit(solution)/shard_map/ppermute | solution.py:328
  91.6 0.3 collective-permute-done.8.refs_8_
  91.9 2.0 %shard_map.97 = (f32[128,256]{1,0:T(8,128)S(1)}, f32[32,256]{1,0:T(8,128)S(1)}) custom-call(s32[1]{0:T(128)S(6)} %copy.20.refs_0_, f32[32,1024]{1,0:T(8,128)S(1)} %get-tuple-element.10.refs_1_, f32[32,1024]{1,0:T(8,128)S(1)} %collective-permute-done.2.refs_2_, f32[32,1024]{1,0:T(8,128)S(1)} %collective-permute-done.3.refs_3_, ...), custom_call_target="tpu_custom_call" | custom-call | tf_op jit(solution)/shard_map/pallas_call | solution.py:215
  94.0 1.2 collective-permute-start.15
  95.2 3.5 %collective-permute-start.16 = (f32[64,256]{1,0:T(8,128)S(1)}, f32[64,256]{1,0:T(8,128)S(1)}, u32[]{:S(2)}, u32[]{:S(2)}) collective-permute-start(f32[64,256]{1,0:T(8,128)S(1)} %get-tuple-element.21), channel_id=1, source_target_pairs={{0,3},{1,0},{2,1},{3,2},{4,7},{5,4},{6,5},{7,6},{8,11},{9,8},{10,9... | collective-permute-start | bytes 196616 | tf_op jit(solution)/shard_map/ppermute | solution.py:305
  98.7 1.1 collective-permute-start.17
  99.8 1.6 %collective-permute-start.21 = (f32[64,256]{1,0:T(8,128)S(1)}, f32[64,256]{1,0:T(8,128)S(1)}, u32[]{:S(2)}, u32[]{:S(2)}) collective-permute-start(f32[64,256]{1,0:T(8,128)S(1)} %get-tuple-element.20), channel_id=1, source_target_pairs={{0,4},{1,5},{2,6},{3,7},{4,8},{5,9},{6,10},{7,11},{8,12},{9,13},{1... | collective-permute-start | bytes 196616 | tf_op jit(solution)/shard_map/ppermute | solution.py:314
  101.4 1.0 collective-permute-start.22
  102.4 2.4 %collective-permute-start.23 = (f32[64,256]{1,0:T(8,128)S(1)}, f32[64,256]{1,0:T(8,128)S(1)}, u32[]{:S(2)}, u32[]{:S(2)}) collective-permute-start(f32[64,256]{1,0:T(8,128)S(1)} %get-tuple-element.20), channel_id=1, source_target_pairs={{0,8},{1,9},{2,10},{3,11},{4,12},{5,13},{6,14},{7,15},{8,0},{9,1},... | collective-permute-start | bytes 196616 | tf_op jit(solution)/shard_map/ppermute | solution.py:314
  104.9 2.4 %collective-permute-done.23 = f32[64,256]{1,0:T(8,128)S(1)} collective-permute-done((f32[64,256]{1,0:T(8,128)S(1)}, f32[64,256]{1,0:T(8,128)S(1)}, u32[]{:S(2)}, u32[]{:S(2)}) %collective-permute-start.23) | collective-permute-done | bytes 65568 | tf_op jit(solution)/shard_map/ppermute | solution.py:314
  107.3 1.2 collective-permute-start.18
  108.5 1.5 collective-permute-start.19
  110.0 1.0 collective-permute-start.20
  111.0 0.6 collective-permute-start.28
  111.6 2.1 %collective-permute-start.29 = (f32[32,128]{1,0:T(8,128)S(1)}, f32[32,128]{1,0:T(8,128)S(1)}, u32[]{:S(2)}, u32[]{:S(2)}) collective-permute-start(f32[32,128]{1,0:T(8,128)S(1)} %copy-done.4), channel_id=1, source_target_pairs={{0,96},{16,112},{32,0},{48,16},{64,32},{80,48},{96,64},{112,80},{1... | collective-permute-start | bytes 49160 | tf_op jit(solution)/shard_map/ppermute | solution.py:323
  113.7 0.9 collective-permute-start.24
  114.6 1.8 %collective-permute-start.25 = (f32[64,256]{1,0:T(8,128)S(1)}, f32[64,256]{1,0:T(8,128)S(1)}, u32[]{:S(2)}, u32[]{:S(2)}) collective-permute-start(f32[64,256]{1,0:T(8,128)S(1)} %get-tuple-element.18.refs_4_), channel_id=1, source_target_pairs={{0,3},{1,0},{2,1},{3,2},{4,7},{5,4},{6,5},{7,6},{8,11},{9,8},{10,9... | collective-permute-start | bytes 196616 | tf_op jit(solution)/shard_map/ppermute | solution.py:305
  116.4 0.8 collective-permute-start.26
  117.2 1.2 collective-permute-done.24.refs_5_
  118.3 0.2 collective-permute-start.30
  118.6 2.9 %collective-permute-start.10 = (f32[32,256]{1,0:T(8,128)S(1)}, f32[32,256]{1,0:T(8,128)S(1)}, u32[]{:S(2)}, u32[]{:S(2)}) collective-permute-start(f32[32,256]{1,0:T(8,128)S(1)} %get-tuple-element.11), channel_id=1, source_target_pairs={{0,3},{1,0},{2,1},{3,2},{4,7},{5,4},{6,5},{7,6},{8,11},{9,8},{10,9... | collective-permute-start | bytes 98312 | tf_op jit(solution)/shard_map/ppermute | solution.py:305
  121.4 0.4 collective-permute-start.11
  121.8 0.3 collective-permute-start.9
  122.1 6.8 %collective-permute-start.31 = (f32[32,128]{1,0:T(8,128)S(1)}, f32[32,128]{1,0:T(8,128)S(1)}, u32[]{:S(2)}, u32[]{:S(2)}) collective-permute-start(f32[32,128]{1,0:T(8,128)S(1)} %copy-done.4), channel_id=1, source_target_pairs={{0,16},{16,0},{32,48},{48,32},{64,80},{80,64},{96,112},{112,96},{1... | collective-permute-start | bytes 49160 | tf_op jit(solution)/shard_map/ppermute | solution.py:328
  128.9 0.3 collective-permute-start.32
  129.2 0.3 collective-permute-start.33
  129.5 3.9 %collective-permute-start.34 = (f32[32,128]{1,0:T(8,128)S(1)}, f32[32,128]{1,0:T(8,128)S(1)}, u32[]{:S(2)}, u32[]{:S(2)}) collective-permute-start(f32[32,128]{1,0:T(8,128)S(1)} %collective-permute-done.30.refs_12_), channel_id=1, source_target_pairs={{0,16},{16,0},{32,48},{48,32},{64,80},{80,64},{96,112},{112,96},{1... | collective-permute-start | bytes 49160 | tf_op jit(solution)/shard_map/ppermute | solution.py:328
  133.3 0.3 collective-permute-start.27
  133.8 2.7 %collective-permute-start.13 = (f32[32,256]{1,0:T(8,128)S(1)}, f32[32,256]{1,0:T(8,128)S(1)}, u32[]{:S(2)}, u32[]{:S(2)}) collective-permute-start(f32[32,256]{1,0:T(8,128)S(1)} %add_add_fusion.2.refs_0_), channel_id=1, source_target_pairs={{0,12},{1,13},{2,14},{3,15},{4,0},{5,1},{6,2},{7,3},{8,4},{9,5},{1... | collective-permute-start | bytes 98312 | tf_op jit(solution)/shard_map/ppermute | solution.py:314
  136.4 0.6 collective-permute-start.14
  137.0 15.2 %shard_map.98.refs_5_ = f32[256,128]{1,0:T(8,128)S(1)} custom-call(f32[64,256]{1,0:T(8,128)S(1)} %get-tuple-element.19.refs_0_, f32[64,256]{1,0:T(8,128)S(1)} %collective-permute-done.18.refs_1_, f32[64,256]{1,0:T(8,128)S(1)} %collective-permute-done.19.refs_2_, f32[64,256]{1,0:T(8,128)S(1)} %collective-permute-done.20.refs_3_, ...), custom_call_target="tpu_custom_call" | custom-call | flops 8589934592 | bytes 1048576 | tf_op jit(solution)/shard_map/pallas_call | solution.py:275
  152.2 0.6 copy-done.3
  152.9 0.6 copy-done.9
  153.5 0.6 copy-done.11
  154.1 1.8 %shard_map.99 = f32[32,128]{1,0:T(8,128)} custom-call(f32[32,256]{1,0:T(8,128)} %copy-done.8, f32[32,256]{1,0:T(8,128)} %copy-done.9, f32[32,256]{1,0:T(8,128)} %copy-done.10, f32[32,256]{1,0:T(8,128)} %copy-done.11, f32[32,128]{1,0:T(8,128)} %refs_4_.1, f32[256,128]{1,0:T(8,128)} %copy-done.3), custom_call_target="tpu_custom_call" | custom-call | tf_op jit(solution)/shard_map/pallas_call | solution.py:295
  (60 shorter events, 0.4 us)
Async XLA Ops:
  0.6 8.3 %copy-start = (bf16[32,8,64,128]{3,2,1,0:T(8,128)(2,1)S(1)}, bf16[32,8,64,128]{3,2,1,0:T(8,128)(2,1)}, u32[]{:S(2)}) copy-start(bf16[32,8,64,128]{3,2,1,0:T(8,128)(2,1)} %u_ref.3) | copy-start | bytes 12582916
  0.6 8.3 %copy-start.1 = (bf16[32,8,64,128]{3,2,1,0:T(8,128)(2,1)S(1)}, bf16[32,8,64,128]{3,2,1,0:T(8,128)(2,1)}, u32[]{:S(2)}) copy-start(bf16[32,8,64,128]{3,2,1,0:T(8,128)(2,1)} %k_ref.3) | copy-start | bytes 12582916
  0.6 8.3 %copy-start.5 = (s32[1024]{0:T(1024)S(1)}, s32[1024]{0:T(1024)}, u32[]{:S(2)}) copy-start(s32[1024]{0:T(1024)} %pos_ref.3) | copy-start | bytes 12292
  2.6 44.0 %collective-permute-start.1 = (bf16[2,32,64,128]{3,2,1,0:T(8,128)(2,1)S(1)}, bf16[2,32,64,128]{3,2,1,0:T(8,128)(2,1)S(1)}, u32[]{:S(2)}, u32[]{:S(2)}) collective-permute-start(bf16[2,32,64,128]{3,2,1,0:T(8,128)(2,1)S(1)} %pad_maximum_fusion.1), channel_id=1, source_target_pairs={{1,0},{2,1},{3,2},{4,3},{5,4},{6,5},{7,6},{8,7},{9,8},{10,9},{11,1... | collective-permute-start | bytes 3145736 | tf_op jit(solution)/shard_map/ppermute | solution.py:341
  4.3 42.3 %collective-permute-start = (bf16[2,32,64,128]{3,2,1,0:T(8,128)(2,1)S(1)}, bf16[2,32,64,128]{3,2,1,0:T(8,128)(2,1)S(1)}, u32[]{:S(2)}, u32[]{:S(2)}) collective-permute-start(bf16[2,32,64,128]{3,2,1,0:T(8,128)(2,1)S(1)} %pad_maximum_fusion), channel_id=1, source_target_pairs={{0,1},{1,2},{2,3},{3,4},{4,5},{5,6},{6,7},{7,8},{8,9},{9,10},{10,1... | collective-permute-start | bytes 3145736 | tf_op jit(solution)/shard_map/ppermute | solution.py:340
  46.7 45.2 %copy-start.2 = (f32[32,1024]{1,0:T(8,128)S(1)}, f32[32,1024]{1,0:T(8,128)}, u32[]{:S(2)}) copy-start(f32[32,1024]{1,0:T(8,128)} %refs_9_.2) | copy-start | bytes 393220
  46.7 45.2 %copy-start.6 = (f32[1024]{0:T(1024)S(1)}, f32[1024]{0:T(1024)}, u32[]{:S(2)}) copy-start(f32[1024]{0:T(1024)} %param.12) | copy-start | bytes 12292
  46.7 45.2 %copy-start.7 = (f32[1024]{0:T(1024)S(1)}, f32[1024]{0:T(1024)}, u32[]{:S(2)}) copy-start(f32[1024]{0:T(1024)} %param.13) | copy-start | bytes 12292
  46.7 64.3 %copy-start.4 = (f32[32,128]{1,0:T(8,128)S(1)}, f32[32,128]{1,0:T(8,128)}, u32[]{:S(2)}) copy-start(f32[32,128]{1,0:T(8,128)} %refs_4_.1) | copy-start | bytes 49156
  79.2 6.7 %collective-permute-start.2 = (f32[32,1024]{1,0:T(8,128)S(1)}, f32[32,1024]{1,0:T(8,128)S(1)}, u32[]{:S(2)}, u32[]{:S(2)}) collective-permute-start(f32[32,1024]{1,0:T(8,128)S(1)} %get-tuple-element.10.refs_1_), channel_id=1, source_target_pairs={{0,32},{16,48},{32,64},{48,80},{64,96},{80,112},{96,0},{112,16},{1... | collective-permute-start | bytes 393224 | tf_op jit(solution)/shard_map/ppermute | solution.py:323
  80.8 6.0 %collective-permute-start.3 = (f32[32,1024]{1,0:T(8,128)S(1)}, f32[32,1024]{1,0:T(8,128)S(1)}, u32[]{:S(2)}, u32[]{:S(2)}) collective-permute-start(f32[32,1024]{1,0:T(8,128)S(1)} %get-tuple-element.10.refs_1_), channel_id=1, source_target_pairs={{0,96},{16,112},{32,0},{48,16},{64,32},{80,48},{96,64},{112,80},{1... | collective-permute-start | bytes 393224 | tf_op jit(solution)/shard_map/ppermute | solution.py:323
  82.2 7.0 %collective-permute-start.4 = (f32[32,1024]{1,0:T(8,128)S(1)}, f32[32,1024]{1,0:T(8,128)S(1)}, u32[]{:S(2)}, u32[]{:S(2)}) collective-permute-start(f32[32,1024]{1,0:T(8,128)S(1)} %get-tuple-element.10.refs_1_), channel_id=1, source_target_pairs={{0,64},{16,80},{32,96},{48,112},{64,0},{80,16},{96,32},{112,48},{1... | collective-permute-start | bytes 393224 | tf_op jit(solution)/shard_map/ppermute | solution.py:323
  83.8 7.7 %collective-permute-start.5 = (f32[32,1024]{1,0:T(8,128)S(1)}, f32[32,1024]{1,0:T(8,128)S(1)}, u32[]{:S(2)}, u32[]{:S(2)}) collective-permute-start(f32[32,1024]{1,0:T(8,128)S(1)} %get-tuple-element.10.refs_1_), channel_id=1, source_target_pairs={{0,16},{16,0},{32,48},{48,32},{64,80},{80,64},{96,112},{112,96},{1... | collective-permute-start | bytes 393224 | tf_op jit(solution)/shard_map/ppermute | solution.py:328
  85.9 5.7 %collective-permute-start.6 = (f32[32,1024]{1,0:T(8,128)S(1)}, f32[32,1024]{1,0:T(8,128)S(1)}, u32[]{:S(2)}, u32[]{:S(2)}) collective-permute-start(f32[32,1024]{1,0:T(8,128)S(1)} %collective-permute-done.2.refs_2_), channel_id=1, source_target_pairs={{0,16},{16,0},{32,48},{48,32},{64,80},{80,64},{96,112},{112,96},{1... | collective-permute-start | bytes 393224 | tf_op jit(solution)/shard_map/ppermute | solution.py:328
  86.8 4.8 %collective-permute-start.7 = (f32[32,1024]{1,0:T(8,128)S(1)}, f32[32,1024]{1,0:T(8,128)S(1)}, u32[]{:S(2)}, u32[]{:S(2)}) collective-permute-start(f32[32,1024]{1,0:T(8,128)S(1)} %collective-permute-done.3.refs_3_), channel_id=1, source_target_pairs={{0,16},{16,0},{32,48},{48,32},{64,80},{80,64},{96,112},{112,96},{1... | collective-permute-start | bytes 393224 | tf_op jit(solution)/shard_map/ppermute | solution.py:328
  89.2 2.7 %collective-permute-start.8 = (f32[32,1024]{1,0:T(8,128)S(1)}, f32[32,1024]{1,0:T(8,128)S(1)}, u32[]{:S(2)}, u32[]{:S(2)}) collective-permute-start(f32[32,1024]{1,0:T(8,128)S(1)} %collective-permute-done.4.refs_4_), channel_id=1, source_target_pairs={{0,16},{16,0},{32,48},{48,32},{64,80},{80,64},{96,112},{112,96},{1... | collective-permute-start | bytes 393224 | tf_op jit(solution)/shard_map/ppermute | solution.py:328
  94.0 8.5 %collective-permute-start.15 = (f32[64,256]{1,0:T(8,128)S(1)}, f32[64,256]{1,0:T(8,128)S(1)}, u32[]{:S(2)}, u32[]{:S(2)}) collective-permute-start(f32[64,256]{1,0:T(8,128)S(1)} %get-tuple-element.21), channel_id=1, source_target_pairs={{0,1},{1,2},{2,3},{3,0},{4,5},{5,6},{6,7},{7,4},{8,9},{9,10},{10,1... | collective-permute-start | bytes 196616 | tf_op jit(solution)/shard_map/ppermute | solution.py:305
  95.2 9.6 %collective-permute-start.16 = (f32[64,256]{1,0:T(8,128)S(1)}, f32[64,256]{1,0:T(8,128)S(1)}, u32[]{:S(2)}, u32[]{:S(2)}) collective-permute-start(f32[64,256]{1,0:T(8,128)S(1)} %get-tuple-element.21), channel_id=1, source_target_pairs={{0,3},{1,0},{2,1},{3,2},{4,7},{5,4},{6,5},{7,6},{8,11},{9,8},{10,9... | collective-permute-start | bytes 196616 | tf_op jit(solution)/shard_map/ppermute | solution.py:305
  98.7 6.2 %collective-permute-start.17 = (f32[64,256]{1,0:T(8,128)S(1)}, f32[64,256]{1,0:T(8,128)S(1)}, u32[]{:S(2)}, u32[]{:S(2)}) collective-permute-start(f32[64,256]{1,0:T(8,128)S(1)} %get-tuple-element.21), channel_id=1, source_target_pairs={{0,2},{1,3},{2,0},{3,1},{4,6},{5,7},{6,4},{7,5},{8,10},{9,11},{10,... | collective-permute-start | bytes 196616 | tf_op jit(solution)/shard_map/ppermute | solution.py:305
  99.8 5.1 %collective-permute-start.21 = (f32[64,256]{1,0:T(8,128)S(1)}, f32[64,256]{1,0:T(8,128)S(1)}, u32[]{:S(2)}, u32[]{:S(2)}) collective-permute-start(f32[64,256]{1,0:T(8,128)S(1)} %get-tuple-element.20), channel_id=1, source_target_pairs={{0,4},{1,5},{2,6},{3,7},{4,8},{5,9},{6,10},{7,11},{8,12},{9,13},{1... | collective-permute-start | bytes 196616 | tf_op jit(solution)/shard_map/ppermute | solution.py:314
  101.4 3.4 %collective-permute-start.22 = (f32[64,256]{1,0:T(8,128)S(1)}, f32[64,256]{1,0:T(8,128)S(1)}, u32[]{:S(2)}, u32[]{:S(2)}) collective-permute-start(f32[64,256]{1,0:T(8,128)S(1)} %get-tuple-element.20), channel_id=1, source_target_pairs={{0,12},{1,13},{2,14},{3,15},{4,0},{5,1},{6,2},{7,3},{8,4},{9,5},{1... | collective-permute-start | bytes 196616 | tf_op jit(solution)/shard_map/ppermute | solution.py:314
  102.4 4.8 %collective-permute-start.23 = (f32[64,256]{1,0:T(8,128)S(1)}, f32[64,256]{1,0:T(8,128)S(1)}, u32[]{:S(2)}, u32[]{:S(2)}) collective-permute-start(f32[64,256]{1,0:T(8,128)S(1)} %get-tuple-element.20), channel_id=1, source_target_pairs={{0,8},{1,9},{2,10},{3,11},{4,12},{5,13},{6,14},{7,15},{8,0},{9,1},... | collective-permute-start | bytes 196616 | tf_op jit(solution)/shard_map/ppermute | solution.py:314
  107.3 6.4 %collective-permute-start.18 = (f32[64,256]{1,0:T(8,128)S(1)}, f32[64,256]{1,0:T(8,128)S(1)}, u32[]{:S(2)}, u32[]{:S(2)}) collective-permute-start(f32[64,256]{1,0:T(8,128)S(1)} %get-tuple-element.19.refs_0_), channel_id=1, source_target_pairs={{0,4},{1,5},{2,6},{3,7},{4,8},{5,9},{6,10},{7,11},{8,12},{9,13},{1... | collective-permute-start | bytes 196616 | tf_op jit(solution)/shard_map/ppermute | solution.py:314
  108.5 6.1 %collective-permute-start.19 = (f32[64,256]{1,0:T(8,128)S(1)}, f32[64,256]{1,0:T(8,128)S(1)}, u32[]{:S(2)}, u32[]{:S(2)}) collective-permute-start(f32[64,256]{1,0:T(8,128)S(1)} %get-tuple-element.19.refs_0_), channel_id=1, source_target_pairs={{0,12},{1,13},{2,14},{3,15},{4,0},{5,1},{6,2},{7,3},{8,4},{9,5},{1... | collective-permute-start | bytes 196616 | tf_op jit(solution)/shard_map/ppermute | solution.py:314
  110.0 6.4 %collective-permute-start.20 = (f32[64,256]{1,0:T(8,128)S(1)}, f32[64,256]{1,0:T(8,128)S(1)}, u32[]{:S(2)}, u32[]{:S(2)}) collective-permute-start(f32[64,256]{1,0:T(8,128)S(1)} %get-tuple-element.19.refs_0_), channel_id=1, source_target_pairs={{0,8},{1,9},{2,10},{3,11},{4,12},{5,13},{6,14},{7,15},{8,0},{9,1},... | collective-permute-start | bytes 196616 | tf_op jit(solution)/shard_map/ppermute | solution.py:314
  111.0 10.8 %collective-permute-start.28 = (f32[32,128]{1,0:T(8,128)S(1)}, f32[32,128]{1,0:T(8,128)S(1)}, u32[]{:S(2)}, u32[]{:S(2)}) collective-permute-start(f32[32,128]{1,0:T(8,128)S(1)} %copy-done.4), channel_id=1, source_target_pairs={{0,32},{16,48},{32,64},{48,80},{64,96},{80,112},{96,0},{112,16},{1... | collective-permute-start | bytes 49160 | tf_op jit(solution)/shard_map/ppermute | solution.py:323
  111.6 10.5 %collective-permute-start.29 = (f32[32,128]{1,0:T(8,128)S(1)}, f32[32,128]{1,0:T(8,128)S(1)}, u32[]{:S(2)}, u32[]{:S(2)}) collective-permute-start(f32[32,128]{1,0:T(8,128)S(1)} %copy-done.4), channel_id=1, source_target_pairs={{0,96},{16,112},{32,0},{48,16},{64,32},{80,48},{96,64},{112,80},{1... | collective-permute-start | bytes 49160 | tf_op jit(solution)/shard_map/ppermute | solution.py:323
  113.7 4.6 %collective-permute-start.24 = (f32[64,256]{1,0:T(8,128)S(1)}, f32[64,256]{1,0:T(8,128)S(1)}, u32[]{:S(2)}, u32[]{:S(2)}) collective-permute-start(f32[64,256]{1,0:T(8,128)S(1)} %get-tuple-element.18.refs_4_), channel_id=1, source_target_pairs={{0,1},{1,2},{2,3},{3,0},{4,5},{5,6},{6,7},{7,4},{8,9},{9,10},{10,1... | collective-permute-start | bytes 196616 | tf_op jit(solution)/shard_map/ppermute | solution.py:305
  114.6 4.0 %collective-permute-start.25 = (f32[64,256]{1,0:T(8,128)S(1)}, f32[64,256]{1,0:T(8,128)S(1)}, u32[]{:S(2)}, u32[]{:S(2)}) collective-permute-start(f32[64,256]{1,0:T(8,128)S(1)} %get-tuple-element.18.refs_4_), channel_id=1, source_target_pairs={{0,3},{1,0},{2,1},{3,2},{4,7},{5,4},{6,5},{7,6},{8,11},{9,8},{10,9... | collective-permute-start | bytes 196616 | tf_op jit(solution)/shard_map/ppermute | solution.py:305
  116.4 5.0 %collective-permute-start.26 = (f32[64,256]{1,0:T(8,128)S(1)}, f32[64,256]{1,0:T(8,128)S(1)}, u32[]{:S(2)}, u32[]{:S(2)}) collective-permute-start(f32[64,256]{1,0:T(8,128)S(1)} %get-tuple-element.18.refs_4_), channel_id=1, source_target_pairs={{0,2},{1,3},{2,0},{3,1},{4,6},{5,7},{6,4},{7,5},{8,10},{9,11},{10,... | collective-permute-start | bytes 196616 | tf_op jit(solution)/shard_map/ppermute | solution.py:305
  118.3 10.6 %collective-permute-start.30 = (f32[32,128]{1,0:T(8,128)S(1)}, f32[32,128]{1,0:T(8,128)S(1)}, u32[]{:S(2)}, u32[]{:S(2)}) collective-permute-start(f32[32,128]{1,0:T(8,128)S(1)} %copy-done.4), channel_id=1, source_target_pairs={{0,64},{16,80},{32,96},{48,112},{64,0},{80,16},{96,32},{112,48},{1... | collective-permute-start | bytes 49160 | tf_op jit(solution)/shard_map/ppermute | solution.py:323
  118.6 10.6 %collective-permute-start.10 = (f32[32,256]{1,0:T(8,128)S(1)}, f32[32,256]{1,0:T(8,128)S(1)}, u32[]{:S(2)}, u32[]{:S(2)}) collective-permute-start(f32[32,256]{1,0:T(8,128)S(1)} %get-tuple-element.11), channel_id=1, source_target_pairs={{0,3},{1,0},{2,1},{3,2},{4,7},{5,4},{6,5},{7,6},{8,11},{9,8},{10,9... | collective-permute-start | bytes 98312 | tf_op jit(solution)/shard_map/ppermute | solution.py:305
  121.4 8.0 %collective-permute-start.11 = (f32[32,256]{1,0:T(8,128)S(1)}, f32[32,256]{1,0:T(8,128)S(1)}, u32[]{:S(2)}, u32[]{:S(2)}) collective-permute-start(f32[32,256]{1,0:T(8,128)S(1)} %get-tuple-element.11), channel_id=1, source_target_pairs={{0,2},{1,3},{2,0},{3,1},{4,6},{5,7},{6,4},{7,5},{8,10},{9,11},{10,... | collective-permute-start | bytes 98312 | tf_op jit(solution)/shard_map/ppermute | solution.py:305
  121.8 11.5 %collective-permute-start.9 = (f32[32,256]{1,0:T(8,128)S(1)}, f32[32,256]{1,0:T(8,128)S(1)}, u32[]{:S(2)}, u32[]{:S(2)}) collective-permute-start(f32[32,256]{1,0:T(8,128)S(1)} %get-tuple-element.11), channel_id=1, source_target_pairs={{0,1},{1,2},{2,3},{3,0},{4,5},{5,6},{6,7},{7,4},{8,9},{9,10},{10,1... | collective-permute-start | bytes 98312 | tf_op jit(solution)/shard_map/ppermute | solution.py:305
  122.1 11.6 %collective-permute-start.31 = (f32[32,128]{1,0:T(8,128)S(1)}, f32[32,128]{1,0:T(8,128)S(1)}, u32[]{:S(2)}, u32[]{:S(2)}) collective-permute-start(f32[32,128]{1,0:T(8,128)S(1)} %copy-done.4), channel_id=1, source_target_pairs={{0,16},{16,0},{32,48},{48,32},{64,80},{80,64},{96,112},{112,96},{1... | collective-permute-start | bytes 49160 | tf_op jit(solution)/shard_map/ppermute | solution.py:328
  128.9 4.8 %collective-permute-start.32 = (f32[32,128]{1,0:T(8,128)S(1)}, f32[32,128]{1,0:T(8,128)S(1)}, u32[]{:S(2)}, u32[]{:S(2)}) collective-permute-start(f32[32,128]{1,0:T(8,128)S(1)} %collective-permute-done.28.refs_10_), channel_id=1, source_target_pairs={{0,16},{16,0},{32,48},{48,32},{64,80},{80,64},{96,112},{112,96},{1... | collective-permute-start | bytes 49160 | tf_op jit(solution)/shard_map/ppermute | solution.py:328
  129.2 7.2 %collective-permute-start.33 = (f32[32,128]{1,0:T(8,128)S(1)}, f32[32,128]{1,0:T(8,128)S(1)}, u32[]{:S(2)}, u32[]{:S(2)}) collective-permute-start(f32[32,128]{1,0:T(8,128)S(1)} %collective-permute-done.29.refs_11_), channel_id=1, source_target_pairs={{0,16},{16,0},{32,48},{48,32},{64,80},{80,64},{96,112},{112,96},{1... | collective-permute-start | bytes 49160 | tf_op jit(solution)/shard_map/ppermute | solution.py:328
  129.5 7.5 %collective-permute-start.34 = (f32[32,128]{1,0:T(8,128)S(1)}, f32[32,128]{1,0:T(8,128)S(1)}, u32[]{:S(2)}, u32[]{:S(2)}) collective-permute-start(f32[32,128]{1,0:T(8,128)S(1)} %collective-permute-done.30.refs_12_), channel_id=1, source_target_pairs={{0,16},{16,0},{32,48},{48,32},{64,80},{80,64},{96,112},{112,96},{1... | collective-permute-start | bytes 49160 | tf_op jit(solution)/shard_map/ppermute | solution.py:328
  133.3 3.7 %collective-permute-start.27 = (f32[128,128]{1,0:T(8,128)S(1)}, f32[128,128]{1,0:T(8,128)S(1)}, u32[]{:S(2)}, u32[]{:S(2)}) collective-permute-start(f32[128,128]{1,0:T(8,128)S(1)} %pad_maximum_fusion.2), channel_id=1, source_target_pairs={{0,16},{16,0},{32,48},{48,32},{64,80},{80,64},{96,112},{112,96},{1... | collective-permute-start | bytes 196616 | tf_op jit(solution)/shard_map/ppermute | solution.py:328
  133.7 18.5 %copy-start.8 = (f32[32,256]{1,0:T(8,128)}, f32[32,256]{1,0:T(8,128)S(1)}, u32[]{:S(2)}) copy-start(f32[32,256]{1,0:T(8,128)S(1)} %add_add_fusion.2.refs_0_) | copy-start | bytes 98308
  133.7 19.2 %collective-permute-start.12 = (f32[32,256]{1,0:T(8,128)S(1)}, f32[32,256]{1,0:T(8,128)S(1)}, u32[]{:S(2)}, u32[]{:S(2)}) collective-permute-start(f32[32,256]{1,0:T(8,128)S(1)} %add_add_fusion.2.refs_0_), channel_id=1, source_target_pairs={{0,4},{1,5},{2,6},{3,7},{4,8},{5,9},{6,10},{7,11},{8,12},{9,13},{1... | collective-permute-start | bytes 98312 | tf_op jit(solution)/shard_map/ppermute | solution.py:314
  133.8 19.1 %collective-permute-start.13 = (f32[32,256]{1,0:T(8,128)S(1)}, f32[32,256]{1,0:T(8,128)S(1)}, u32[]{:S(2)}, u32[]{:S(2)}) collective-permute-start(f32[32,256]{1,0:T(8,128)S(1)} %add_add_fusion.2.refs_0_), channel_id=1, source_target_pairs={{0,12},{1,13},{2,14},{3,15},{4,0},{5,1},{6,2},{7,3},{8,4},{9,5},{1... | collective-permute-start | bytes 98312 | tf_op jit(solution)/shard_map/ppermute | solution.py:314
  136.4 16.4 %collective-permute-start.14 = (f32[32,256]{1,0:T(8,128)S(1)}, f32[32,256]{1,0:T(8,128)S(1)}, u32[]{:S(2)}, u32[]{:S(2)}) collective-permute-start(f32[32,256]{1,0:T(8,128)S(1)} %add_add_fusion.2.refs_0_), channel_id=1, source_target_pairs={{0,8},{1,9},{2,10},{3,11},{4,12},{5,13},{6,14},{7,15},{8,0},{9,1},... | collective-permute-start | bytes 98312 | tf_op jit(solution)/shard_map/ppermute | solution.py:314
  152.2 0.7 copy-start.3
  152.9 0.6 copy-start.9
  152.9 0.6 copy-start.10
  153.5 0.6 copy-start.11

commit v2 on v1

v2 whole, which is shorter than its diff:
```python
import math

import jax
import jax.numpy as jnp
from jax import lax
from jax.experimental import pallas as pl
from jax.experimental.pallas import tpu as pltpu
from jax.sharding import PartitionSpec as P

step_size = 0.08
HIGH = lax.Precision.HIGHEST
F32 = jnp.float32


def shift_down(a, first):
    return jnp.concatenate([first, a[:-1]], axis=0)


def shift_up(a):
    return jnp.concatenate([a[1:], jnp.zeros_like(a[:1])], axis=0)


PAD = 8


def boundary(p, layers):
    z = p >> 13
    return (z == 0) | (z == layers - 1)


def sample_all(pos_ref, src_ref, dst_ref, list_ref, count_ref, stride, layers):
    members, slots = dst_ref.shape
    groups = members // 8
    lane = lax.broadcasted_iota(jnp.int32, (8, 128), 1)

    def block(jb, found):
        def chunk(jc, carry):
            found, accs = carry[0], list(carry[1:])
            for t in range(8):
                j = jc * 8 + t
                p = pos_ref[jb * 128 + j]
                list_ref[found] = jb * 128 + j
                found = found + boundary(p, layers).astype(jnp.int32)
                here = lane == j
                for g in range(groups):
                    v = src_ref[pl.ds(g * 8 * stride + (p >> 7), 8, stride=stride), :]
                    accs[g] = jnp.where(here, pltpu.roll(v, (j - p) & 127, 1), accs[g])
            return (found, *accs)

        start = (found,) + tuple(jnp.zeros((8, 128), F32) for _ in range(groups))
        found, *accs = lax.fori_loop(0, 16, chunk, start)
        at = pl.ds(pl.multiple_of(jb * 128, 128), 128)
        for g in range(groups):
            dst_ref[g * 8 : g * 8 + 8, at] = accs[g]
        return found

    count_ref[0] = lax.fori_loop(0, slots // 128, block, jnp.int32(0))


def sample_listed(pos_ref, list_ref, count_ref, src_ref, dst_ref, stride, nx):
    groups = dst_ref.shape[0] // 8
    lane = lax.broadcasted_iota(jnp.int32, (8, 128), 1)
    count, unroll = count_ref[0], 8

    def chunk(c, _):
        held = []
        for t in range(unroll):
            n = jnp.minimum(c * unroll + t, count - 1)
            j = list_ref[n]
            p = pos_ref[j]
            row = ((p >> 15) & 1) * nx + ((p >> 7) & (nx - 1))
            rolled = [
                pltpu.roll(
                    src_ref[pl.ds(g * 8 * stride + row, 8, stride=stride), :], (j - p) & 127, 1
                )
                for g in range(groups)
            ]
            held.append((j, rolled))
        for j, rolled in held:
            here = lane == (j & 127)
            at = pl.ds(pl.multiple_of((j >> 7) * 128, 128), 128)
            for g in range(groups):
                pltpu.store(dst_ref.at[g * 8 : g * 8 + 8, at], rolled[g], mask=here)
        return 0

    lax.fori_loop(0, (count + unroll - 1) // unroll, chunk, 0)


def stencil_kernel(
    pos_ref, u_ref, k_ref, out_ref, picked_ref, list_ref, count_ref, state, sem
):
    i = pl.program_id(0)
    members, layers, nx, ny = u_ref.shape
    lane = lax.broadcasted_iota(jnp.int32, (nx, ny), 1)
    first_lane, last_lane = lane == 0, lane == ny - 1
    half = step_size * 0.5

    def member(b, _):
        base = (i * members + b) * (layers * nx + PAD)
        u = u_ref[b, 0].astype(F32)
        k = k_ref[b, 0].astype(F32)
        below = None
        for z in range(layers):
            ku = k * u
            un = jnp.where(last_lane, 0.0, pltpu.roll(u, ny - 1, 1))
            kn = jnp.where(last_lane, 0.0, pltpu.roll(k, ny - 1, 1))
            f = (k + kn) * (un - u)
            acc = f - jnp.where(first_lane, ku, pltpu.roll(f, 1, 1))
            f = (k + shift_up(k)) * (shift_up(u) - u)
            acc = acc + (f - shift_down(f, ku[:1]))
            if below is not None:
                acc = acc - below
            u_now = u
            if z < layers - 1:
                u_next = u_ref[b, z + 1].astype(F32)
                k_next = k_ref[b, z + 1].astype(F32)
                below = (k + k_next) * (u_next - u)
                acc = acc + below
                u, k = u_next, k_next
            state[pl.ds(pl.multiple_of(base + z * nx, 8), nx), :] = u_now + half * acc
        return 0

    lax.fori_loop(0, members, member, 0)
    rows = layers * nx

    def push(m):
        return pltpu.make_async_copy(
            state.at[pl.ds(pl.multiple_of(m * (rows + PAD), 8), rows), :],
            out_ref.at[pl.ds(pl.multiple_of(m * rows, 8), rows), :],
            sem.at[m],
        )

    for b in range(members):
        push(i * members + b).start()

    @pl.when(i == pl.num_programs(0) - 1)
    def _():
        sample_all(pos_ref, state, picked_ref, list_ref, count_ref, rows + PAD, layers)
        for m in range(out_ref.shape[0] // rows):
            push(m).wait()


def stencil(pos, u, k):
    m, layers, nx, ny = u.shape
    per = 4
    block = pl.BlockSpec((per, layers, nx, ny), lambda i: (i, 0, 0, 0))
    rows = m * layers * nx
    return pl.pallas_call(
        stencil_kernel,
        grid=(m // per,),
        in_specs=[pl.BlockSpec(memory_space=pltpu.SMEM), block, block],
        out_specs=[
            pl.BlockSpec(memory_space=pl.ANY),
            pl.BlockSpec((m, pos.shape[0]), lambda i: (0, 0)),
            pl.BlockSpec(memory_space=pltpu.SMEM),
            pl.BlockSpec(memory_space=pltpu.SMEM),
        ],
        out_shape=[
            jax.ShapeDtypeStruct((rows, ny), F32),
            jax.ShapeDtypeStruct((m, pos.shape[0]), F32),
            jax.ShapeDtypeStruct((pos.shape[0] + 8,), jnp.int32),
            jax.ShapeDtypeStruct((1,), jnp.int32),
        ],
        scratch_shapes=[
            pltpu.VMEM((m * (layers * nx + PAD), ny), F32),
            pltpu.SemaphoreType.DMA((m,)),
        ],
        compiler_params=pltpu.CompilerParams(vmem_limit_bytes=32 << 20),
        cost_estimate=pl.CostEstimate(
            flops=40 * u.size, bytes_accessed=8 * u.size, transcendentals=0
        ),
    )(pos, u, k)


def faces_kernel(
    pos_ref, list_ref, count_ref, u_ref, k_ref, lo_ref, hi_ref, in_ref, partial_ref, params_ref, out_ref, picked_ref, extra, found
):
    g, side = pl.program_id(0), pl.program_id(1)
    members, _, nx, ny = u_ref.shape
    half = step_size * 0.5

    def apply(halo):
        def member(b, _):
            u = u_ref[b, 0].astype(F32)
            k = k_ref[b, 0].astype(F32)
            un = halo[0, b].astype(F32)
            kn = halo[1, b].astype(F32)
            d = half * ((k + kn) * (un - u))
            out_ref[b, 0] = in_ref[b, 0] + d
            at = (g * members + b) * (2 * nx + PAD) + side * nx
            extra[pl.ds(pl.multiple_of(at, 8), nx), :] = d
            return 0

        lax.fori_loop(0, members, member, 0)

    @pl.when(side == 0)
    def _():
        apply(lo_ref)

    @pl.when(side == 1)
    def _():
        apply(hi_ref)

    @pl.when((g == pl.num_programs(0) - 1) & (side == 1))
    def _():
        found[...] = jnp.zeros_like(found)
        sample_listed(pos_ref, list_ref, count_ref, extra, found, 2 * nx + PAD, nx)
        slots = found.shape[1]
        picked_ref[:, :slots] = partial_ref[...] + found[...]
        picked_ref[:, slots:] = params_ref[...]


def faces(pos, listed, count, u, k, lo, hi, states, partial, params):
    m, layers, nx, ny = u.shape
    per = 16
    face = pl.BlockSpec((per, 1, nx, ny), lambda g, s: (g, s * (layers - 1), 0, 0))
    halo = pl.BlockSpec((2, per, nx, ny), lambda g, s: (0, g, 0, 0))
    flat = pl.BlockSpec(partial.shape, lambda g, s: (0, 0))
    small = pl.BlockSpec(params.shape, lambda g, s: (0, 0))
    both = (m, partial.shape[1] + params.shape[1])
    return pl.pallas_call(
        faces_kernel,
        grid=(m // per, 2),
        in_specs=[pl.BlockSpec(memory_space=pltpu.SMEM)] * 3 + [face, face, halo, halo, face, flat, small],
        out_specs=[face, pl.BlockSpec(both, lambda g, s: (0, 0))],
        out_shape=[
            jax.ShapeDtypeStruct(states.shape, F32),
            jax.ShapeDtypeStruct(both, F32),
        ],
        scratch_shapes=[
            pltpu.VMEM((m * (2 * nx + PAD), ny), F32),
            pltpu.VMEM(partial.shape, F32),
        ],
        input_output_aliases={7: 0},
        compiler_params=pltpu.CompilerParams(vmem_limit_bytes=32 << 20),
        cost_estimate=pl.CostEstimate(
            flops=8 * m * nx * ny, bytes_accessed=24 * m * nx * ny, transcendentals=0
        ),
    )(pos, listed, count, u, k, lo, hi, states, partial, params)


def contract(a, b, dims):
    return lax.dot_general(a, b, (dims, ((), ())), precision=HIGH, preferred_element_type=F32)


def gram_kernel(scale, count_ref, core_ref, *refs):
    blocks, (noise, values, std, sum_ref) = refs[:8], refs[8:]
    rows = blocks[0].shape[0]
    n = 4 * rows
    slots = noise.shape[1]
    readings = [b[:, :slots] for b in blocks]
    own = readings[0]
    total = own
    for b in readings[1:]:
        total = total + b
    centre = jnp.sum(total, axis=0, keepdims=True) * (1.0 / (8 * rows))
    live = lax.broadcasted_iota(jnp.int32, centre.shape, 1) < count_ref[0]
    weight = jnp.where(live, 1.0 / (std[...] * scale), 0.0)
    first = jnp.concatenate([(b - centre) * weight for b in readings[:4]], axis=0)
    second = jnp.concatenate([(b - centre) * weight for b in readings[4:]], axis=0)
    misfit = jnp.where(live, (values[...] - own) / std[...] + noise[...], 0.0)
    on_first = contract(
        jnp.concatenate([first, second[: n // 2], misfit], axis=0), first, ((1,), (1,))
    )
    on_second = contract(
        jnp.concatenate([first[n // 2 :], misfit], axis=0), second, ((1,), (1,))
    )
    is_first = core_ref[0] == 0
    sum_ref[:n] = on_first[:n]
    sum_ref[n : n + n // 2] = jnp.where(is_first, on_first[n : n + n // 2], on_second[: n // 2])
    sum_ref[n + n // 2 : n + n // 2 + rows] = on_first[n + n // 2 :]
    sum_ref[n + n // 2 + rows :] = on_second[n // 2 :]


def gram(count, core, blocks, noise, values, std, ens_scale):
    rows = blocks[0].shape[0]
    vmem = pl.BlockSpec(memory_space=pltpu.VMEM)
    return pl.pallas_call(
        lambda *refs: gram_kernel(ens_scale, *refs),
        in_specs=[pl.BlockSpec(memory_space=pltpu.SMEM)] * 2 + [vmem] * 11,
        out_specs=vmem,
        out_shape=jax.ShapeDtypeStruct((8 * rows, 4 * rows), F32),
        compiler_params=pltpu.CompilerParams(vmem_limit_bytes=16 << 20),
    )(count, core, *blocks, noise, values.reshape(1, -1), std.reshape(1, -1))


def inverse4(k):
    r = 1.0 / (k[0][0] * k[1][1] - k[0][1] * k[0][1])
    a00, a01, a11 = k[1][1] * r, -k[0][1] * r, k[0][0] * r
    t00, t01 = a00 * k[0][2] + a01 * k[1][2], a00 * k[0][3] + a01 * k[1][3]
    t10, t11 = a01 * k[0][2] + a11 * k[1][2], a01 * k[0][3] + a11 * k[1][3]
    s00 = k[2][2] - (k[0][2] * t00 + k[1][2] * t10)
    s01 = k[2][3] - (k[0][2] * t01 + k[1][2] * t11)
    s11 = k[3][3] - (k[0][3] * t01 + k[1][3] * t11)
    q = 1.0 / (s00 * s11 - s01 * s01)
    i00, i01, i11 = s11 * q, -s01 * q, s00 * q
    v00, v01 = t00 * i00 + t01 * i01, t00 * i01 + t01 * i11
    v10, v11 = t10 * i00 + t11 * i01, t10 * i01 + t11 * i11
    b00 = a00 + v00 * t00 + v01 * t01
    b01 = a01 + v00 * t10 + v01 * t11
    b11 = a11 + v10 * t10 + v11 * t11
    return [
        [b00, b01, -v00, -v01],
        [b01, b11, -v10, -v11],
        [-v00, -v10, i00, i01],
        [-v01, -v11, i01, i11],
    ]


def pivoted_inverse(p):
    n = p.shape[0]
    tiles = [p[t : t + 8] for t in range(0, n, 8)]
    row = lax.broadcasted_iota(jnp.int32, (8, n), 0)
    lane = lax.broadcasted_iota(jnp.int32, (8, n), 1)
    lane1 = lax.broadcasted_iota(jnp.int32, (1, n), 1)

    def spread(tile, at):
        return jnp.broadcast_to(tile[:, at : at + 1], (8, n))

    def entries(tile, at):
        columns = [spread(tile, at + b) for b in range(4)]
        return [[columns[b][at % 8 + a : at % 8 + a + 1] for b in range(4)] for a in range(4)]

    def dot4(x, y):
        return (x[0] * y[0] + x[1] * y[1]) + (x[2] * y[2] + x[3] * y[3])

    inv = inverse4(entries(tiles[0], 0))
    for i in range(0, n, 4):
        here, off = i // 8, i % 8
        cols = [[spread(t, i + b) for t in tiles] for b in range(4)]
        ahead = None
        if i + 4 < n:
            there, shift = (i + 4) // 8, (i + 4) % 8
            q = entries(tiles[there], i + 4)
            c = [[cols[m][there][shift + a : shift + a + 1] for m in range(4)] for a in range(4)]
            w = [[dot4(inv[m], c[b]) for m in range(4)] for b in range(4)]
            ahead = inverse4(
                [[q[a][b] - dot4(c[a], w[b]) if a <= b else None for b in range(4)] for a in range(4)]
            )
        inside1 = (lane1 >= i) & (lane1 < i + 4)
        e = [
            jnp.where(
                inside1, jnp.where(lane1 == i + a, 1.0, 0.0), tiles[here][off + a : off + a + 1]
            )
            for a in range(4)
        ]
        new = [dot4(inv[a], e) for a in range(4)]
        inside = (lane >= i) & (lane < i + 4)
        for t in range(n // 8):
            rest = jnp.where(inside, 0.0, tiles[t])
            tiles[t] = rest - (
                (cols[0][t] * new[0] + cols[1][t] * new[1])
                + (cols[2][t] * new[2] + cols[3][t] * new[3])
            )
        for a in range(4):
            tiles[here] = jnp.where(row == off + a, new[a], tiles[here])
        inv = ahead
    return jnp.concatenate(tiles, axis=0)


def spd_inverse(p):
    n = p.shape[0]
    if n <= 64:
        return pivoted_inverse(p)
    h = n // 2
    corner, side = p[:h, :h], p[:h, h:]
    first = spd_inverse(corner)
    ahead = contract(first, side, ((1,), (0,)))
    second = spd_inverse(p[h:, h:] - contract(side, ahead, ((0,), (0,))))
    mixed = contract(ahead, second, ((1,), (0,)))
    top = jnp.concatenate([first + contract(mixed, ahead, ((1,), (1,))), -mixed], axis=1)
    return jnp.concatenate([top, jnp.concatenate([-mixed.T, second], axis=1)], axis=0)


def identity(n):
    return jnp.where(
        lax.broadcasted_iota(jnp.int32, (n, n), 0) == lax.broadcasted_iota(jnp.int32, (n, n), 1),
        1.0,
        0.0,
    )


def inverse_kernel(sum_ref, out_ref):
    n = out_ref.shape[0]
    out_ref[...] = spd_inverse(sum_ref[:n] + identity(n))


def inverse(sums):
    n = sums.shape[1]
    vmem = pl.BlockSpec(memory_space=pltpu.VMEM)
    return pl.pallas_call(
        inverse_kernel,
        in_specs=[vmem],
        out_specs=vmem,
        out_shape=jax.ShapeDtypeStruct((n, n), F32),
        compiler_params=pltpu.CompilerParams(vmem_limit_bytes=4 << 20),
        cost_estimate=pl.CostEstimate(flops=4 << 30, bytes_accessed=1 << 20, transcendentals=0),
    )(sums)


def update_kernel(scale, core_ref, inv_ref, sum_ref, other_ref, *refs):
    blocks, out_ref = refs[:8], refs[8]
    n = inv_ref.shape[0]
    half, rows = n // 2, blocks[0].shape[0]
    width = out_ref.shape[1]
    params = jnp.concatenate([b[:, -width:] for b in blocks], axis=0)
    anomaly = (params - jnp.sum(params, axis=0, keepdims=True) * (1.0 / (2 * n))) * (1.0 / scale)
    is_first = core_ref[0] == 0
    mine, theirs = sum_ref[n : n + half], other_ref[n : n + half]
    product = jnp.concatenate(
        [jnp.where(is_first, mine, theirs), jnp.where(is_first, theirs, mine)], axis=0
    )
    fs = jnp.where(is_first, product.T, product)
    right = contract(inv_ref[...], jnp.concatenate([fs, anomaly[:n]], axis=1), ((1,), (0,)))
    down = contract(fs, right, ((0,), (0,)))
    second = spd_inverse(other_ref[:n] + identity(n) - down[:, :n])
    x_second = contract(second, anomaly[n:] - down[:, n:], ((1,), (0,)))
    x_first = right[:, n:] - contract(right[:, :n], x_second, ((1,), (0,)))
    cross_first, cross_second = sum_ref[n + half : n + half + rows], sum_ref[n + half + rows :]
    out_ref[...] = params[:rows] + (
        contract(cross_first, x_first, ((1,), (0,))) + contract(cross_second, x_second, ((1,), (0,)))
    )


def update(core, inv, sums, other, blocks, width, ens_scale):
    vmem = pl.BlockSpec(memory_space=pltpu.VMEM)
    return pl.pallas_call(
        lambda *refs: update_kernel(ens_scale, *refs),
        in_specs=[pl.BlockSpec(memory_space=pltpu.SMEM)] + [vmem] * 11,
        out_specs=vmem,
        out_shape=jax.ShapeDtypeStruct((blocks[0].shape[0], width), F32),
        compiler_params=pltpu.CompilerParams(vmem_limit_bytes=16 << 20),
    )(core, inv, sums, other, *blocks)


def around_x(a):
    return [a] + [
        lax.ppermute(
            a, "space", [(z * 4 + x, z * 4 + (x + s) % 4) for z in range(4) for x in range(4)]
        )
        for s in (1, 3, 2)
    ]


def around_z(a):
    return [a] + [
        lax.ppermute(
            a, "space", [(z * 4 + x, (z + s) % 4 * 4 + x) for z in range(4) for x in range(4)]
        )
        for s in (1, 3, 2)
    ]


def around_y(a):
    return [a] + [
        lax.ppermute(a, "ens", [(e, (e + 2 * s) % 8) for e in range(8)]) for s in (1, 3, 2)
    ]


def partner(a):
    return lax.ppermute(a, "ens", [(e, e ^ 1) for e in range(8)])


def total4(parts):
    return (parts[0] + parts[1]) + (parts[2] + parts[3])


def shards(u, k, pos, count, values, std, noise, params):
    spaces = lax.axis_size("space")
    ens_scale = math.sqrt(u.shape[0] * lax.axis_size("ens") - 1.0)
    last = jnp.stack([u[:, -1], k[:, -1]])
    head = jnp.stack([u[:, 0], k[:, 0]])
    lo = lax.ppermute(last, "space", [(i, i + 1) for i in range(spaces - 1)])
    hi = lax.ppermute(head, "space", [(i + 1, i) for i in range(spaces - 1)])
    states, partial, listed, found = stencil(pos, u, k)
    states, picked = faces(
        pos, listed, found, u, k, lo, hi, states.reshape(u.shape), partial, params
    )

    mine = around_y(picked)
    blocks = mine + [partner(a) for a in mine]

    core = (lax.axis_index("ens") % 2).astype(jnp.int32).reshape(1)
    sums = gram(count, core, blocks, noise, values, std, ens_scale)
    sums = total4(around_z(total4(around_x(sums))))
    other = partner(sums)
    inv = inverse(sums)
    return update(core, inv, sums, other, blocks, params.shape[1], ens_scale), states


def solution(mesh):
    in_specs = (
        P("ens", "space", None, None),
        P("ens", "space", None, None),
        P("space"),
        P("space"),
        P("space"),
        P("space"),
        P("ens", "space"),
        P("ens", "space"),
    )
    out_specs = (P("ens", "space"), P("ens", "space", None, None))
    return jax.shard_map(shards, mesh=mesh, in_specs=in_specs, out_specs=out_specs, check_vma=False)
```

time: 156 us -> 93.5 us (0.60)
  Pallas kernels: 89.1 us -> 45.9 us
  starting transfers between devices: 56.6 us -> 27.6 us
  waiting for transfers between devices: 4.52 us -> 16.3 us
  local copies, waits for them, and re-layouts: 3.78 us -> 1.91 us
    pallas_call x1, Pallas kernels: 32.5 us -> 8.81 us  [faces(): pl.pallas_call(faces_kernel, grid=(m // per, 2), in_specs=[pl.BlockSpec(m...]
    pallas_call x1, Pallas kernels: 37.7 us -> 26.1 us  [stencil(): pl.pallas_call(stencil_kernel, grid=(m // per,), in_specs=[pl.BlockSpec(m...]
    ppermute x9 -> x5, starting transfers between devices: 18 us -> 7.92 us  [partner(): return lax.ppermute(a, 'ens', [(e, e ^ 1) for e in range(8)])]
    ppermute x9 -> x3, starting transfers between devices: 12.7 us -> 4.37 us  [around_x(): lax.ppermute(a, 'space', [(z * 4 + x, z * 4 + (x + s) % 4) for z in range...]
    ppermute x9 -> x3, waiting for transfers between devices: 1.17 us -> 9.02 us  [around_x(): lax.ppermute(a, 'space', [(z * 4 + x, z * 4 + (x + s) % 4) for z in range...]
    pallas_call x2, Pallas kernels: 17 us -> 9.69 us  [the longest x1 5.77 us: update(): pl.pallas_call(lambda *refs: update_kernel(ens_scale, *refs), in_specs=[p...]
    ppermute x9 -> x3, starting transfers between devices: 12.1 us -> 5.32 us  [around_z(): lax.ppermute(a, 'space', [(z * 4 + x, (z + s) % 4 * 4 + x) for z in range...]
    ppermute x9 -> x3, waiting for transfers between devices: 2.39 us -> 5.79 us  [around_z(): lax.ppermute(a, 'space', [(z * 4 + x, (z + s) % 4 * 4 + x) for z in range...]
  transfers between devices with their start and end apart: 35 -> 16, of which waited for: 4 -> 7; matrix products, arithmetic and copies ran while one was open for 0% -> 0% of each run, Pallas kernels for 34% -> 32%
where the time goes in v2:
time: 93.5 us
  Pallas kernels  45.9 us (49%)
  starting transfers between devices  27.6 us (30%)
  waiting for transfers between devices  16.3 us (17%)
  local copies, waits for them, and re-layouts  1.91 us (2%)
  between operations  1.5 us (2%)
    pallas_call x1, Pallas kernels, stencil(): pl.pallas_call(stencil_kernel, grid=(m // per,), in_specs=[pl.BlockSpec(m...  26.1 us
    ppermute x3, waiting for transfers between devices, around_x(): lax.ppermute(a, 'space', [(z * 4 + x, z * 4 + (x + s) % 4) for z in range...  9.02 us
    pallas_call x1, Pallas kernels, faces(): pl.pallas_call(faces_kernel, grid=(m // per, 2), in_specs=[pl.BlockSpec(m...  8.81 us
    ppermute x5, starting transfers between devices, partner(): return lax.ppermute(a, 'ens', [(e, e ^ 1) for e in range(8)])  7.92 us
    ppermute x3, waiting for transfers between devices, around_z(): lax.ppermute(a, 'space', [(z * 4 + x, (z + s) % 4 * 4 + x) for z in range...  5.79 us
    pallas_call x1, Pallas kernels, update(): pl.pallas_call(lambda *refs: update_kernel(ens_scale, *refs), in_specs=[p...  5.77 us
    ppermute x3, starting transfers between devices, around_z(): lax.ppermute(a, 'space', [(z * 4 + x, (z + s) % 4 * 4 + x) for z in range...  5.32 us
    ppermute x3, starting transfers between devices, around_y(): lax.ppermute(a, 'ens', [(e, (e + 2 * s) % 8) for e in range(8)])  4.38 us
  transfers between devices with their start and end apart: 16, of which 7 were waited for; matrix products, arithmetic and copies ran while one was open for 0% of the time, Pallas kernels for 32%

profile of v2, /device:TPU:1, one launch (start us, length us, event | category | flops | bytes accessed | tf_op | source)
XLA Modules:
  0.0 93.5 jit_solution(11567519158028180335)
XLA Ops:
  0.6 0.0 copy-start
  0.6 0.0 copy-start.1
  0.6 0.0 copy-start.4
  0.7 1.9 %slice_bitcast_fusion = (bf16[1,32,64,128]{3,2,1,0:T(8,128)(2,1)S(1)}, bf16[1,32,64,128]{3,2,1,0:T(8,128)(2,1)S(1)}, bf16[1,32,64,128]{3,2,1,0:T(8,128)(2,1)S(1)}, bf16[1,32,64,128]{3,2,1,0:T(8,128)(2,1)S(1)}) fusion(bf16[32,8,64,128]{3,2,1,0:T(8,128)(2,1)} %k_ref.3, bf16[32,8,64,128]{3,2,1,0:T(8,128)(2,1)} %u_ref.3), kind=kLoop, calls=%fused_computation.2 | loop fusion | bytes 4194304 | tf_op jit(solution)/shard_map/stack;squeeze | solution.py:472
  2.5 0.1 pad_maximum_fusion
  2.6 4.3 %collective-permute-start = (bf16[2,32,64,128]{3,2,1,0:T(8,128)(2,1)S(1)}, bf16[2,32,64,128]{3,2,1,0:T(8,128)(2,1)S(1)}, u32[]{:S(2)}, u32[]{:S(2)}) collective-permute-start(bf16[2,32,64,128]{3,2,1,0:T(8,128)(2,1)S(1)} %pad_maximum_fusion), channel_id=1, source_target_pairs={{0,1},{1,2},{2,3},{3,4},{4,5},{5,6},{6,7},{7,8},{8,9},{9,10},{10,1... | collective-permute-start | bytes 3145736 | tf_op jit(solution)/shard_map/ppermute | solution.py:473
  6.9 0.1 pad_maximum_fusion.1
  7.0 0.0 copy-start.3
  7.0 1.3 %collective-permute-start.1 = (bf16[2,32,64,128]{3,2,1,0:T(8,128)(2,1)S(1)}, bf16[2,32,64,128]{3,2,1,0:T(8,128)(2,1)S(1)}, u32[]{:S(2)}, u32[]{:S(2)}) collective-permute-start(bf16[2,32,64,128]{3,2,1,0:T(8,128)(2,1)S(1)} %pad_maximum_fusion.1), channel_id=1, source_target_pairs={{1,0},{2,1},{3,2},{4,3},{5,4},{6,5},{7,6},{8,7},{9,8},{10,9},{11,1... | collective-permute-start | bytes 3145736 | tf_op jit(solution)/shard_map/ppermute | solution.py:474
  8.3 0.0 copy-done
  8.4 26.1 %shard_map.95 = (f32[16384,128]{1,0:T(8,128)}, f32[32,1024]{1,0:T(8,128)S(1)}, s32[1032]{0:T(1024)S(1)}, s32[1]{0:T(128)}) custom-call(s32[1024]{0:T(1024)S(1)} %copy-done.4, bf16[32,8,64,128]{3,2,1,0:T(8,128)(2,1)S(1)} %copy-done, bf16[32,8,64,128]{3,2,1,0:T(8,128)(2,1)S(1)} %copy-done.1), custom_call_target="tpu_custom_call" | custom-call | flops 83886080 | bytes 16777216 | tf_op jit(solution)/shard_map/pallas_call | solution.py:148
  34.4 0.0 collective-permute-done.lo_ref
  34.5 0.0 collective-permute-done.1.hi_ref
  34.5 0.0 copy-start.2
  34.5 0.0 copy-start.5
  34.5 0.0 copy-start.6
  34.5 8.8 %shard_map.96 = (f32[32,8,64,128]{3,2,1,0:T(8,128)}, f32[32,1152]{1,0:T(8,128)S(1)}) custom-call(s32[1024]{0:T(1024)S(1)} %copy-done.4, s32[1032]{0:T(1024)S(1)} %get-tuple-element.8.list_ref, s32[1]{0:T(128)} %get-tuple-element.9.count_ref, bf16[32,8,64,128]{3,2,1,0:T(8,128)(2,1)S(1)} %copy-done, ...), custom_call_target="tpu_custom_call", output_to_operand_aliasing={{0}: (7, {})} | custom-call | flops 2097152 | bytes 6291456 | tf_op jit(solution)/shard_map/pallas_call | solution.py:221
  43.3 1.3 %collective-permute-start.2 = (f32[32,1152]{1,0:T(8,128)S(1)}, f32[32,1152]{1,0:T(8,128)S(1)}, u32[]{:S(2)}, u32[]{:S(2)}) collective-permute-start(f32[32,1152]{1,0:T(8,128)S(1)} %get-tuple-element.12.refs_2_.refs_4_), channel_id=1, source_target_pairs={{0,32},{16,48},{32,64},{48,80},{64,96},{80,112},{96,0},{112,16},{1... | collective-permute-start | bytes 442376 | tf_op jit(solution)/shard_map/ppermute | solution.py:456
  44.6 1.4 %collective-permute-start.3 = (f32[32,1152]{1,0:T(8,128)S(1)}, f32[32,1152]{1,0:T(8,128)S(1)}, u32[]{:S(2)}, u32[]{:S(2)}) collective-permute-start(f32[32,1152]{1,0:T(8,128)S(1)} %get-tuple-element.12.refs_2_.refs_4_), channel_id=1, source_target_pairs={{0,96},{16,112},{32,0},{48,16},{64,32},{80,48},{96,64},{112,80},{1... | collective-permute-start | bytes 442376 | tf_op jit(solution)/shard_map/ppermute | solution.py:456
  46.1 1.6 %collective-permute-start.4 = (f32[32,1152]{1,0:T(8,128)S(1)}, f32[32,1152]{1,0:T(8,128)S(1)}, u32[]{:S(2)}, u32[]{:S(2)}) collective-permute-start(f32[32,1152]{1,0:T(8,128)S(1)} %get-tuple-element.12.refs_2_.refs_4_), channel_id=1, source_target_pairs={{0,64},{16,80},{32,96},{48,112},{64,0},{80,16},{96,32},{112,48},{1... | collective-permute-start | bytes 442376 | tf_op jit(solution)/shard_map/ppermute | solution.py:456
  47.7 1.8 %collective-permute-start.5 = (f32[32,1152]{1,0:T(8,128)S(1)}, f32[32,1152]{1,0:T(8,128)S(1)}, u32[]{:S(2)}, u32[]{:S(2)}) collective-permute-start(f32[32,1152]{1,0:T(8,128)S(1)} %get-tuple-element.12.refs_2_.refs_4_), channel_id=1, source_target_pairs={{0,16},{16,0},{32,48},{48,32},{64,80},{80,64},{96,112},{112,96},{1... | collective-permute-start | bytes 442376 | tf_op jit(solution)/shard_map/ppermute | solution.py:461
  49.5 0.0 collective-permute-done.2.refs_3_.refs_5_
  49.5 1.5 %collective-permute-start.6 = (f32[32,1152]{1,0:T(8,128)S(1)}, f32[32,1152]{1,0:T(8,128)S(1)}, u32[]{:S(2)}, u32[]{:S(2)}) collective-permute-start(f32[32,1152]{1,0:T(8,128)S(1)} %collective-permute-done.2.refs_3_.refs_5_), channel_id=1, source_target_pairs={{0,16},{16,0},{32,48},{48,32},{64,80},{80,64},{96,112},{112,96},{1... | collective-permute-start | bytes 442376 | tf_op jit(solution)/shard_map/ppermute | solution.py:461
  51.0 0.0 collective-permute-done.3.refs_4_.refs_6_
  51.0 1.2 %collective-permute-start.7 = (f32[32,1152]{1,0:T(8,128)S(1)}, f32[32,1152]{1,0:T(8,128)S(1)}, u32[]{:S(2)}, u32[]{:S(2)}) collective-permute-start(f32[32,1152]{1,0:T(8,128)S(1)} %collective-permute-done.3.refs_4_.refs_6_), channel_id=1, source_target_pairs={{0,16},{16,0},{32,48},{48,32},{64,80},{80,64},{96,112},{112,96},{1... | collective-permute-start | bytes 442376 | tf_op jit(solution)/shard_map/ppermute | solution.py:461
  52.3 1.2 %collective-permute-done.4.refs_5_.refs_7_ = f32[32,1152]{1,0:T(8,128)S(1)} collective-permute-done((f32[32,1152]{1,0:T(8,128)S(1)}, f32[32,1152]{1,0:T(8,128)S(1)}, u32[]{:S(2)}, u32[]{:S(2)}) %collective-permute-start.4) | collective-permute-done | bytes 147488 | tf_op jit(solution)/shard_map/ppermute | solution.py:456
  53.4 1.8 %collective-permute-start.8 = (f32[32,1152]{1,0:T(8,128)S(1)}, f32[32,1152]{1,0:T(8,128)S(1)}, u32[]{:S(2)}, u32[]{:S(2)}) collective-permute-start(f32[32,1152]{1,0:T(8,128)S(1)} %collective-permute-done.4.refs_5_.refs_7_), channel_id=1, source_target_pairs={{0,16},{16,0},{32,48},{48,32},{64,80},{80,64},{96,112},{112,96},{1... | collective-permute-start | bytes 442376 | tf_op jit(solution)/shard_map/ppermute | solution.py:461
  55.9 0.0 collective-permute-done.5.refs_6_.refs_8_
  55.9 0.0 collective-permute-done.6.refs_7_.refs_9_
  55.9 0.0 collective-permute-done.7.refs_8_.refs_10_
  55.9 0.3 collective-permute-done.8.refs_9_.refs_11_
  56.2 1.3 %shard_map.97 = f32[256,128]{1,0:T(8,128)S(1)} custom-call(s32[1]{0:T(128)S(6)} %copy.20.refs_0_, s32[1]{0:T(128)} %bitcast.refs_1_.refs_0_, f32[32,1152]{1,0:T(8,128)S(1)} %get-tuple-element.12.refs_2_.refs_4_, f32[32,1152]{1,0:T(8,128)S(1)} %collective-permute-done.2.refs_3_.refs_5_, f32[32,1152]{1,0:T(8,128)S(1)} %collective-permute-done.3.refs_4_.refs_6_, ...), custom_call_target="tpu_custom_call" | custom-call | tf_op jit(solution)/shard_map/pallas_call | solution.py:278
  57.6 3.7 %collective-permute-start.10 = (f32[256,128]{1,0:T(8,128)S(1)}, f32[256,128]{1,0:T(8,128)S(1)}, u32[]{:S(2)}, u32[]{:S(2)}) collective-permute-start(f32[256,128]{1,0:T(8,128)S(1)} %shard_map.97), channel_id=1, source_target_pairs={{0,3},{1,0},{2,1},{3,2},{4,7},{5,4},{6,5},{7,6},{8,11},{9,8},{10,9... | collective-permute-start | bytes 393224 | tf_op jit(solution)/shard_map/ppermute | solution.py:438
  61.2 0.6 collective-permute-start.11
  61.8 0.1 collective-permute-start.9
  61.9 4.5 %collective-permute-done.10 = f32[256,128]{1,0:T(8,128)S(1)} collective-permute-done((f32[256,128]{1,0:T(8,128)S(1)}, f32[256,128]{1,0:T(8,128)S(1)}, u32[]{:S(2)}, u32[]{:S(2)}) %collective-permute-start.10) | collective-permute-done | bytes 131104 | tf_op jit(solution)/shard_map/ppermute | solution.py:438
  66.4 0.7 collective-permute-done.11
  67.1 3.8 %collective-permute-done.9 = f32[256,128]{1,0:T(8,128)S(1)} collective-permute-done((f32[256,128]{1,0:T(8,128)S(1)}, f32[256,128]{1,0:T(8,128)S(1)}, u32[]{:S(2)}, u32[]{:S(2)}) %collective-permute-start.9) | collective-permute-done | bytes 131104 | tf_op jit(solution)/shard_map/ppermute | solution.py:438
  71.0 1.8 %collective-permute-start.12 = (f32[256,128]{1,0:T(8,128)S(1)}, f32[256,128]{1,0:T(8,128)S(1)}, u32[]{:S(2)}, u32[]{:S(2)}) collective-permute-start(f32[256,128]{1,0:T(8,128)S(1)} %add_add_fusion.1), channel_id=1, source_target_pairs={{0,4},{1,5},{2,6},{3,7},{4,8},{5,9},{6,10},{7,11},{8,12},{9,13},{1... | collective-permute-start | bytes 393224 | tf_op jit(solution)/shard_map/ppermute | solution.py:447
  72.8 2.3 %collective-permute-start.13 = (f32[256,128]{1,0:T(8,128)S(1)}, f32[256,128]{1,0:T(8,128)S(1)}, u32[]{:S(2)}, u32[]{:S(2)}) collective-permute-start(f32[256,128]{1,0:T(8,128)S(1)} %add_add_fusion.1), channel_id=1, source_target_pairs={{0,12},{1,13},{2,14},{3,15},{4,0},{5,1},{6,2},{7,3},{8,4},{9,5},{1... | collective-permute-start | bytes 393224 | tf_op jit(solution)/shard_map/ppermute | solution.py:447
  75.1 1.2 %collective-permute-start.14 = (f32[256,128]{1,0:T(8,128)S(1)}, f32[256,128]{1,0:T(8,128)S(1)}, u32[]{:S(2)}, u32[]{:S(2)}) collective-permute-start(f32[256,128]{1,0:T(8,128)S(1)} %add_add_fusion.1), channel_id=1, source_target_pairs={{0,8},{1,9},{2,10},{3,11},{4,12},{5,13},{6,14},{7,15},{8,0},{9,1},... | collective-permute-start | bytes 393224 | tf_op jit(solution)/shard_map/ppermute | solution.py:447
  76.3 2.1 %collective-permute-done.12 = f32[256,128]{1,0:T(8,128)S(1)} collective-permute-done((f32[256,128]{1,0:T(8,128)S(1)}, f32[256,128]{1,0:T(8,128)S(1)}, u32[]{:S(2)}, u32[]{:S(2)}) %collective-permute-start.12) | collective-permute-done | bytes 131104 | tf_op jit(solution)/shard_map/ppermute | solution.py:447
  78.5 0.0 collective-permute-done.13
  78.5 3.6 %collective-permute-done.14 = f32[256,128]{1,0:T(8,128)S(1)} collective-permute-done((f32[256,128]{1,0:T(8,128)S(1)}, f32[256,128]{1,0:T(8,128)S(1)}, u32[]{:S(2)}, u32[]{:S(2)}) %collective-permute-start.14) | collective-permute-done | bytes 131104 | tf_op jit(solution)/shard_map/ppermute | solution.py:447
  82.1 1.6 %collective-permute-start.15 = (f32[256,128]{1,0:T(8,128)S(1)}, f32[256,128]{1,0:T(8,128)S(1)}, u32[]{:S(2)}, u32[]{:S(2)}) collective-permute-start(f32[256,128]{1,0:T(8,128)S(1)} %add_add_fusion.sum_ref.refs_2_), channel_id=1, source_target_pairs={{0,16},{16,0},{32,48},{48,32},{64,80},{80,64},{96,112},{112,96},{1... | collective-permute-start | bytes 393224 | tf_op jit(solution)/shard_map/ppermute | solution.py:461
  83.8 3.9 %shard_map.98.refs_1_ = f32[128,128]{1,0:T(8,128)S(1)} custom-call(f32[256,128]{1,0:T(8,128)S(1)} %add_add_fusion.sum_ref.refs_2_), custom_call_target="tpu_custom_call" | custom-call | flops 4294967296 | bytes 1048576 | tf_op jit(solution)/shard_map/pallas_call | solution.py:391
  87.7 0.0 collective-permute-done.15.refs_3_
  87.7 5.8 %shard_map.99 = f32[32,128]{1,0:T(8,128)} custom-call(s32[1]{0:T(128)} %bitcast.refs_1_.refs_0_, f32[128,128]{1,0:T(8,128)S(1)} %shard_map.98.refs_1_, f32[256,128]{1,0:T(8,128)S(1)} %add_add_fusion.sum_ref.refs_2_, f32[256,128]{1,0:T(8,128)S(1)} %collective-permute-done.15.refs_3_, f32[32,1152]{1,0:T(8,128)S(1)} %get-tuple-element.12.refs_2_.refs_4_, ...), custom_call_target="tpu_custom_call" | custom-call | tf_op jit(solution)/shard_map/pallas_call | solution.py:427
  (8 shorter events, 0.1 us)
Async XLA Ops:
  0.6 7.7 %copy-start = (bf16[32,8,64,128]{3,2,1,0:T(8,128)(2,1)S(1)}, bf16[32,8,64,128]{3,2,1,0:T(8,128)(2,1)}, u32[]{:S(2)}) copy-start(bf16[32,8,64,128]{3,2,1,0:T(8,128)(2,1)} %u_ref.3) | copy-start | bytes 12582916
  0.6 7.7 %copy-start.1 = (bf16[32,8,64,128]{3,2,1,0:T(8,128)(2,1)S(1)}, bf16[32,8,64,128]{3,2,1,0:T(8,128)(2,1)}, u32[]{:S(2)}) copy-start(bf16[32,8,64,128]{3,2,1,0:T(8,128)(2,1)} %k_ref.3) | copy-start | bytes 12582916
  0.6 7.7 %copy-start.4 = (s32[1024]{0:T(1024)S(1)}, s32[1024]{0:T(1024)}, u32[]{:S(2)}) copy-start(s32[1024]{0:T(1024)} %pos_ref.3) | copy-start | bytes 12292
  2.6 31.8 %collective-permute-start = (bf16[2,32,64,128]{3,2,1,0:T(8,128)(2,1)S(1)}, bf16[2,32,64,128]{3,2,1,0:T(8,128)(2,1)S(1)}, u32[]{:S(2)}, u32[]{:S(2)}) collective-permute-start(bf16[2,32,64,128]{3,2,1,0:T(8,128)(2,1)S(1)} %pad_maximum_fusion), channel_id=1, source_target_pairs={{0,1},{1,2},{2,3},{3,4},{4,5},{5,6},{6,7},{7,8},{8,9},{9,10},{10,1... | collective-permute-start | bytes 3145736 | tf_op jit(solution)/shard_map/ppermute | solution.py:473
  7.0 27.4 %copy-start.3 = (f32[32,128]{1,0:T(8,128)S(1)}, f32[32,128]{1,0:T(8,128)}, u32[]{:S(2)}) copy-start(f32[32,128]{1,0:T(8,128)} %params_ref.1) | copy-start | bytes 49156
  7.0 27.4 %collective-permute-start.1 = (bf16[2,32,64,128]{3,2,1,0:T(8,128)(2,1)S(1)}, bf16[2,32,64,128]{3,2,1,0:T(8,128)(2,1)S(1)}, u32[]{:S(2)}, u32[]{:S(2)}) collective-permute-start(bf16[2,32,64,128]{3,2,1,0:T(8,128)(2,1)S(1)} %pad_maximum_fusion.1), channel_id=1, source_target_pairs={{1,0},{2,1},{3,2},{4,3},{5,4},{6,5},{7,6},{8,7},{9,8},{10,9},{11,1... | collective-permute-start | bytes 3145736 | tf_op jit(solution)/shard_map/ppermute | solution.py:474
  34.5 21.7 %copy-start.2 = (f32[32,1024]{1,0:T(8,128)S(1)}, f32[32,1024]{1,0:T(8,128)}, u32[]{:S(2)}) copy-start(f32[32,1024]{1,0:T(8,128)} %refs_10_.1) | copy-start | bytes 393220
  34.5 21.7 %copy-start.5 = (f32[1024]{0:T(1024)S(1)}, f32[1024]{0:T(1024)}, u32[]{:S(2)}) copy-start(f32[1024]{0:T(1024)} %param.12) | copy-start | bytes 12292
  34.5 21.7 %copy-start.6 = (f32[1024]{0:T(1024)S(1)}, f32[1024]{0:T(1024)}, u32[]{:S(2)}) copy-start(f32[1024]{0:T(1024)} %param.13) | copy-start | bytes 12292
  43.3 6.2 %collective-permute-start.2 = (f32[32,1152]{1,0:T(8,128)S(1)}, f32[32,1152]{1,0:T(8,128)S(1)}, u32[]{:S(2)}, u32[]{:S(2)}) collective-permute-start(f32[32,1152]{1,0:T(8,128)S(1)} %get-tuple-element.12.refs_2_.refs_4_), channel_id=1, source_target_pairs={{0,32},{16,48},{32,64},{48,80},{64,96},{80,112},{96,0},{112,16},{1... | collective-permute-start | bytes 442376 | tf_op jit(solution)/shard_map/ppermute | solution.py:456
  44.6 6.4 %collective-permute-start.3 = (f32[32,1152]{1,0:T(8,128)S(1)}, f32[32,1152]{1,0:T(8,128)S(1)}, u32[]{:S(2)}, u32[]{:S(2)}) collective-permute-start(f32[32,1152]{1,0:T(8,128)S(1)} %get-tuple-element.12.refs_2_.refs_4_), channel_id=1, source_target_pairs={{0,96},{16,112},{32,0},{48,16},{64,32},{80,48},{96,64},{112,80},{1... | collective-permute-start | bytes 442376 | tf_op jit(solution)/shard_map/ppermute | solution.py:456
  46.1 7.4 %collective-permute-start.4 = (f32[32,1152]{1,0:T(8,128)S(1)}, f32[32,1152]{1,0:T(8,128)S(1)}, u32[]{:S(2)}, u32[]{:S(2)}) collective-permute-start(f32[32,1152]{1,0:T(8,128)S(1)} %get-tuple-element.12.refs_2_.refs_4_), channel_id=1, source_target_pairs={{0,64},{16,80},{32,96},{48,112},{64,0},{80,16},{96,32},{112,48},{1... | collective-permute-start | bytes 442376 | tf_op jit(solution)/shard_map/ppermute | solution.py:456
  47.7 8.2 %collective-permute-start.5 = (f32[32,1152]{1,0:T(8,128)S(1)}, f32[32,1152]{1,0:T(8,128)S(1)}, u32[]{:S(2)}, u32[]{:S(2)}) collective-permute-start(f32[32,1152]{1,0:T(8,128)S(1)} %get-tuple-element.12.refs_2_.refs_4_), channel_id=1, source_target_pairs={{0,16},{16,0},{32,48},{48,32},{64,80},{80,64},{96,112},{112,96},{1... | collective-permute-start | bytes 442376 | tf_op jit(solution)/shard_map/ppermute | solution.py:461
  49.5 6.4 %collective-permute-start.6 = (f32[32,1152]{1,0:T(8,128)S(1)}, f32[32,1152]{1,0:T(8,128)S(1)}, u32[]{:S(2)}, u32[]{:S(2)}) collective-permute-start(f32[32,1152]{1,0:T(8,128)S(1)} %collective-permute-done.2.refs_3_.refs_5_), channel_id=1, source_target_pairs={{0,16},{16,0},{32,48},{48,32},{64,80},{80,64},{96,112},{112,96},{1... | collective-permute-start | bytes 442376 | tf_op jit(solution)/shard_map/ppermute | solution.py:461
  51.0 4.8 %collective-permute-start.7 = (f32[32,1152]{1,0:T(8,128)S(1)}, f32[32,1152]{1,0:T(8,128)S(1)}, u32[]{:S(2)}, u32[]{:S(2)}) collective-permute-start(f32[32,1152]{1,0:T(8,128)S(1)} %collective-permute-done.3.refs_4_.refs_6_), channel_id=1, source_target_pairs={{0,16},{16,0},{32,48},{48,32},{64,80},{80,64},{96,112},{112,96},{1... | collective-permute-start | bytes 442376 | tf_op jit(solution)/shard_map/ppermute | solution.py:461
  53.4 2.8 %collective-permute-start.8 = (f32[32,1152]{1,0:T(8,128)S(1)}, f32[32,1152]{1,0:T(8,128)S(1)}, u32[]{:S(2)}, u32[]{:S(2)}) collective-permute-start(f32[32,1152]{1,0:T(8,128)S(1)} %collective-permute-done.4.refs_5_.refs_7_), channel_id=1, source_target_pairs={{0,16},{16,0},{32,48},{48,32},{64,80},{80,64},{96,112},{112,96},{1... | collective-permute-start | bytes 442376 | tf_op jit(solution)/shard_map/ppermute | solution.py:461
  57.6 8.8 %collective-permute-start.10 = (f32[256,128]{1,0:T(8,128)S(1)}, f32[256,128]{1,0:T(8,128)S(1)}, u32[]{:S(2)}, u32[]{:S(2)}) collective-permute-start(f32[256,128]{1,0:T(8,128)S(1)} %shard_map.97), channel_id=1, source_target_pairs={{0,3},{1,0},{2,1},{3,2},{4,7},{5,4},{6,5},{7,6},{8,11},{9,8},{10,9... | collective-permute-start | bytes 393224 | tf_op jit(solution)/shard_map/ppermute | solution.py:438
  61.2 5.9 %collective-permute-start.11 = (f32[256,128]{1,0:T(8,128)S(1)}, f32[256,128]{1,0:T(8,128)S(1)}, u32[]{:S(2)}, u32[]{:S(2)}) collective-permute-start(f32[256,128]{1,0:T(8,128)S(1)} %shard_map.97), channel_id=1, source_target_pairs={{0,2},{1,3},{2,0},{3,1},{4,6},{5,7},{6,4},{7,5},{8,10},{9,11},{10,... | collective-permute-start | bytes 393224 | tf_op jit(solution)/shard_map/ppermute | solution.py:438
  61.8 9.1 %collective-permute-start.9 = (f32[256,128]{1,0:T(8,128)S(1)}, f32[256,128]{1,0:T(8,128)S(1)}, u32[]{:S(2)}, u32[]{:S(2)}) collective-permute-start(f32[256,128]{1,0:T(8,128)S(1)} %shard_map.97), channel_id=1, source_target_pairs={{0,1},{1,2},{2,3},{3,0},{4,5},{5,6},{6,7},{7,4},{8,9},{9,10},{10,1... | collective-permute-start | bytes 393224 | tf_op jit(solution)/shard_map/ppermute | solution.py:438
  71.0 7.5 %collective-permute-start.12 = (f32[256,128]{1,0:T(8,128)S(1)}, f32[256,128]{1,0:T(8,128)S(1)}, u32[]{:S(2)}, u32[]{:S(2)}) collective-permute-start(f32[256,128]{1,0:T(8,128)S(1)} %add_add_fusion.1), channel_id=1, source_target_pairs={{0,4},{1,5},{2,6},{3,7},{4,8},{5,9},{6,10},{7,11},{8,12},{9,13},{1... | collective-permute-start | bytes 393224 | tf_op jit(solution)/shard_map/ppermute | solution.py:447
  72.8 5.6 %collective-permute-start.13 = (f32[256,128]{1,0:T(8,128)S(1)}, f32[256,128]{1,0:T(8,128)S(1)}, u32[]{:S(2)}, u32[]{:S(2)}) collective-permute-start(f32[256,128]{1,0:T(8,128)S(1)} %add_add_fusion.1), channel_id=1, source_target_pairs={{0,12},{1,13},{2,14},{3,15},{4,0},{5,1},{6,2},{7,3},{8,4},{9,5},{1... | collective-permute-start | bytes 393224 | tf_op jit(solution)/shard_map/ppermute | solution.py:447
  75.1 7.0 %collective-permute-start.14 = (f32[256,128]{1,0:T(8,128)S(1)}, f32[256,128]{1,0:T(8,128)S(1)}, u32[]{:S(2)}, u32[]{:S(2)}) collective-permute-start(f32[256,128]{1,0:T(8,128)S(1)} %add_add_fusion.1), channel_id=1, source_target_pairs={{0,8},{1,9},{2,10},{3,11},{4,12},{5,13},{6,14},{7,15},{8,0},{9,1},... | collective-permute-start | bytes 393224 | tf_op jit(solution)/shard_map/ppermute | solution.py:447
  82.1 5.5 %collective-permute-start.15 = (f32[256,128]{1,0:T(8,128)S(1)}, f32[256,128]{1,0:T(8,128)S(1)}, u32[]{:S(2)}, u32[]{:S(2)}) collective-permute-start(f32[256,128]{1,0:T(8,128)S(1)} %add_add_fusion.sum_ref.refs_2_), channel_id=1, source_target_pairs={{0,16},{16,0},{32,48},{48,32},{64,80},{80,64},{96,112},{112,96},{1... | collective-permute-start | bytes 393224 | tf_op jit(solution)/shard_map/ppermute | solution.py:461

commit v3 on v2

--- a/solution.py
+++ b/solution.py
@@ -20,83 +20,59 @@
     return jnp.concatenate([a[1:], jnp.zeros_like(a[:1])], axis=0)
 
 
-PAD = 8
-
-
-def boundary(p, layers):
-    z = p >> 13
-    return (z == 0) | (z == layers - 1)
-
-
-def sample_all(pos_ref, src_ref, dst_ref, list_ref, count_ref, stride, layers):
-    members, slots = dst_ref.shape
-    groups = members // 8
-    lane = lax.broadcasted_iota(jnp.int32, (8, 128), 1)
-
-    def block(jb, found):
-        def chunk(jc, carry):
-            found, accs = carry[0], list(carry[1:])
-            for t in range(8):
-                j = jc * 8 + t
-                p = pos_ref[jb * 128 + j]
-                list_ref[found] = jb * 128 + j
-                found = found + boundary(p, layers).astype(jnp.int32)
-                here = lane == j
-                for g in range(groups):
-                    v = src_ref[pl.ds(g * 8 * stride + (p >> 7), 8, stride=stride), :]
-                    accs[g] = jnp.where(here, pltpu.roll(v, (j - p) & 127, 1), accs[g])
-            return (found, *accs)
-
-        start = (found,) + tuple(jnp.zeros((8, 128), F32) for _ in range(groups))
-        found, *accs = lax.fori_loop(0, 16, chunk, start)
-        at = pl.ds(pl.multiple_of(jb * 128, 128), 128)
-        for g in range(groups):
-            dst_ref[g * 8 : g * 8 + 8, at] = accs[g]
-        return found
-
-    count_ref[0] = lax.fori_loop(0, slots // 128, block, jnp.int32(0))
-
-
-def sample_listed(pos_ref, list_ref, count_ref, src_ref, dst_ref, stride, nx):
-    groups = dst_ref.shape[0] // 8
-    lane = lax.broadcasted_iota(jnp.int32, (8, 128), 1)
-    count, unroll = count_ref[0], 8
-
-    def chunk(c, _):
-        held = []
-        for t in range(unroll):
-            n = jnp.minimum(c * unroll + t, count - 1)
-            j = list_ref[n]
-            p = pos_ref[j]
-            row = ((p >> 15) & 1) * nx + ((p >> 7) & (nx - 1))
-            rolled = [
-                pltpu.roll(
-                    src_ref[pl.ds(g * 8 * stride + row, 8, stride=stride), :], (j - p) & 127, 1
-                )
-                for g in range(groups)
-            ]
-            held.append((j, rolled))
-        for j, rolled in held:
-            here = lane == (j & 127)
-            at = pl.ds(pl.multiple_of((j >> 7) * 128, 128), 128)
-            for g in range(groups):
-                pltpu.store(dst_ref.at[g * 8 : g * 8 + 8, at], rolled[g], mask=here)
-        return 0
-
-    lax.fori_loop(0, (count + unroll - 1) // unroll, chunk, 0)
-
-
-def stencil_kernel(
-    pos_ref, u_ref, k_ref, out_ref, picked_ref, list_ref, count_ref, state, sem
-):
+GROUP = 8
+
+
+def set_lanes(pos, lanes, layers, nx, ny):
+    slots = lanes.shape[1]
+    lane = lax.broadcasted_iota(jnp.int32, (ny, slots), 0)
+    for section, layer in enumerate(layers):
+        own = jnp.where(pos // (nx * ny) == layer, pos % ny, -1)
+        hot = jnp.where(lane == own, 1.0, 0.0).astype(jnp.bfloat16)
+        base = 2 * section * ny
+        lanes[base : base + ny] = hot
+        lanes[base + ny : base + 2 * ny] = hot
+
+
+def put(pair, rows, section, value):
+    ny = value.shape[1]
+    high = value.astype(jnp.bfloat16)
+    base = 2 * section * ny
+    pair[rows, base : base + ny] = high
+    pair[rows, base + ny : base + 2 * ny] = (value - high.astype(F32)).astype(jnp.bfloat16)
+
+
+def pick(pair, lanes, x, sums, base, nx, chunk=256):
+    slots = lanes.shape[1]
+    row = lax.broadcasted_iota(jnp.int32, (nx, chunk), 0)
+    for c in range(0, slots, chunk):
+        t = jnp.dot(pair[...], lanes[:, c : c + chunk], preferred_element_type=F32)
+        hit = row == x[:, c : c + chunk]
+        for b in range(GROUP):
+            part = jnp.where(hit, t[b * nx : (b + 1) * nx], 0.0)
+            at = pl.ds(pl.multiple_of(base + b * 8, 8), 8)
+            sums[at, c : c + chunk] = jnp.sum(part.reshape(nx // 8, 8, chunk), axis=0)
+
+
+def add_eights(sums):
+    m = sums.shape[0] // 8
+    member = lax.broadcasted_iota(jnp.int32, (m, 8 * m), 1) // 8
+    add = jnp.where(member == lax.broadcasted_iota(jnp.int32, (m, 8 * m), 0), 1.0, 0.0)
+    return contract(add, sums, ((1,), (0,)))
+
+
+def stencil_kernel(pos_ref, u_ref, k_ref, out_ref, picked_ref, lanes, pair, sums):
     i = pl.program_id(0)
     members, layers, nx, ny = u_ref.shape
     lane = lax.broadcasted_iota(jnp.int32, (nx, ny), 1)
     first_lane, last_lane = lane == 0, lane == ny - 1
     half = step_size * 0.5
 
+    @pl.when(i == 0)
+    def _():
+        set_lanes(pos_ref[...], lanes, range(layers), nx, ny)
+
     def member(b, _):
-        base = (i * members + b) * (layers * nx + PAD)
         u = u_ref[b, 0].astype(F32)
         k = k_ref[b, 0].astype(F32)
         below = None
@@ -117,81 +93,107 @@
                 below = (k + k_next) * (u_next - u)
                 acc = acc + below
                 u, k = u_next, k_next
-            state[pl.ds(pl.multiple_of(base + z * nx, 8), nx), :] = u_now + half * acc
+            value = u_now + half * acc
+            out_ref[b, z] = value
+            put(pair, pl.ds(pl.multiple_of(b * nx, nx), nx), z, value)
         return 0
 
     lax.fori_loop(0, members, member, 0)
-    rows = layers * nx
-
-    def push(m):
-        return pltpu.make_async_copy(
-            state.at[pl.ds(pl.multiple_of(m * (rows + PAD), 8), rows), :],
-            out_ref.at[pl.ds(pl.multiple_of(m * rows, 8), rows), :],
-            sem.at[m],
-        )
-
-    for b in range(members):
-        push(i * members + b).start()
+    pick(pair, lanes, pos_ref[...] // ny % nx, sums, i * members * 8, nx)
 
     @pl.when(i == pl.num_programs(0) - 1)
     def _():
-        sample_all(pos_ref, state, picked_ref, list_ref, count_ref, rows + PAD, layers)
-        for m in range(out_ref.shape[0] // rows):
-            push(m).wait()
+        picked_ref[...] = add_eights(sums[...])
 
 
 def stencil(pos, u, k):
     m, layers, nx, ny = u.shape
-    per = 4
+    per = GROUP
     block = pl.BlockSpec((per, layers, nx, ny), lambda i: (i, 0, 0, 0))
-    rows = m * layers * nx
+    slots = pos.shape[1]
     return pl.pallas_call(
         stencil_kernel,
         grid=(m // per,),
-        in_specs=[pl.BlockSpec(memory_space=pltpu.SMEM), block, block],
-        out_specs=[
-            pl.BlockSpec(memory_space=pl.ANY),
-            pl.BlockSpec((m, pos.shape[0]), lambda i: (0, 0)),
-            pl.BlockSpec(memory_space=pltpu.SMEM),
-            pl.BlockSpec(memory_space=pltpu.SMEM),
-        ],
+        in_specs=[pl.BlockSpec(pos.shape, lambda i: (0, 0)), block, block],
+        out_specs=[block, pl.BlockSpec((m, slots), lambda i: (0, 0))],
         out_shape=[
-            jax.ShapeDtypeStruct((rows, ny), F32),
-            jax.ShapeDtypeStruct((m, pos.shape[0]), F32),
-            jax.ShapeDtypeStruct((pos.shape[0] + 8,), jnp.int32),
-            jax.ShapeDtypeStruct((1,), jnp.int32),
+            jax.ShapeDtypeStruct(u.shape, F32),
+            jax.ShapeDtypeStruct((m, slots), F32),
         ],
         scratch_shapes=[
-            pltpu.VMEM((m * (layers * nx + PAD), ny), F32),
-            pltpu.SemaphoreType.DMA((m,)),
+            pltpu.VMEM((2 * layers * ny, slots), jnp.bfloat16),
+            pltpu.VMEM((per * nx, 2 * layers * ny), jnp.bfloat16),
+            pltpu.VMEM((8 * m, slots), F32),
         ],
-        compiler_params=pltpu.CompilerParams(vmem_limit_bytes=32 << 20),
+        compiler_params=pltpu.CompilerParams(vmem_limit_bytes=24 << 20),
         cost_estimate=pl.CostEstimate(
             flops=40 * u.size, bytes_accessed=8 * u.size, transcendentals=0
         ),
     )(pos, u, k)
 
 
-def faces_kernel(
-    pos_ref, list_ref, count_ref, u_ref, k_ref, lo_ref, hi_ref, in_ref, partial_ref, params_ref, out_ref, picked_ref, extra, found
+def face_flux(own, halo, b):
+    u, k = own[0, b].astype(F32), own[1, b].astype(F32)
+    return (step_size * 0.5) * ((k + halo[1, b].astype(F32)) * (halo[0, b].astype(F32) - u))
+
+
+def readings_kernel(
+    last_layer, pos_ref, head_ref, last_ref, lo_ref, hi_ref, partial_ref, params_ref, out_ref,
+    lanes, pair, sums
 ):
-    g, side = pl.program_id(0), pl.program_id(1)
-    members, _, nx, ny = u_ref.shape
-    half = step_size * 0.5
+    _, members, nx, ny = head_ref.shape
+    slots = partial_ref.shape[1]
+    set_lanes(pos_ref[...], lanes, (0, last_layer), nx, ny)
+    x = pos_ref[...] // ny % nx
+
+    def group(q, _):
+        def member(b, _):
+            rows = pl.ds(pl.multiple_of(b * nx, nx), nx)
+            put(pair, rows, 0, face_flux(head_ref, lo_ref, q * GROUP + b))
+            put(pair, rows, 1, face_flux(last_ref, hi_ref, q * GROUP + b))
+            return 0
+
+        lax.fori_loop(0, GROUP, member, 0, unroll=2)
+        pick(pair, lanes, x, sums, q * GROUP * 8, nx)
+        return 0
+
+    lax.fori_loop(0, members // GROUP, group, 0)
+    out_ref[:, :slots] = partial_ref[...] + add_eights(sums[...])
+    out_ref[:, slots:] = params_ref[...]
+
+
+def readings(pos, head, last, lo, hi, partial, params, layers):
+    _, m, nx, ny = head.shape
+    slots = pos.shape[1]
+    vmem = pl.BlockSpec(memory_space=pltpu.VMEM)
+    return pl.pallas_call(
+        lambda *refs: readings_kernel(layers - 1, *refs),
+        in_specs=[vmem] * 7,
+        out_specs=vmem,
+        out_shape=jax.ShapeDtypeStruct((m, slots + params.shape[1]), F32),
+        scratch_shapes=[
+            pltpu.VMEM((4 * ny, slots), jnp.bfloat16),
+            pltpu.VMEM((GROUP * nx, 4 * ny), jnp.bfloat16),
+            pltpu.VMEM((8 * m, slots), F32),
+        ],
+        compiler_params=pltpu.CompilerParams(vmem_limit_bytes=8 << 20),
+        cost_estimate=pl.CostEstimate(
+            flops=8 * m * nx * ny, bytes_accessed=8 << 20, transcendentals=0
+        ),
+    )(pos, head, last, lo, hi, partial, params)
+
+
+def faces_kernel(u_ref, k_ref, lo_ref, hi_ref, in_ref, out_ref):
+    side = pl.program_id(1)
 
     def apply(halo):
         def member(b, _):
-            u = u_ref[b, 0].astype(F32)
-            k = k_ref[b, 0].astype(F32)
-            un = halo[0, b].astype(F32)
-            kn = halo[1, b].astype(F32)
-            d = half * ((k + kn) * (un - u))
-            out_ref[b, 0] = in_ref[b, 0] + d
-            at = (g * members + b) * (2 * nx + PAD) + side * nx
-            extra[pl.ds(pl.multiple_of(at, 8), nx), :] = d
+            u, k = u_ref[b, 0].astype(F32), k_ref[b, 0].astype(F32)
+            flux = (k + halo[1, b].astype(F32)) * (halo[0, b].astype(F32) - u)
+            out_ref[b, 0] = in_ref[b, 0] + (step_size * 0.5) * flux
             return 0
 
-        lax.fori_loop(0, members, member, 0)
+        lax.fori_loop(0, in_ref.shape[0], member, 0)
 
     @pl.when(side == 0)
     def _():
@@ -201,42 +203,24 @@
     def _():
         apply(hi_ref)
 
-    @pl.when((g == pl.num_programs(0) - 1) & (side == 1))
-    def _():
-        found[...] = jnp.zeros_like(found)
-        sample_listed(pos_ref, list_ref, count_ref, extra, found, 2 * nx + PAD, nx)
-        slots = found.shape[1]
-        picked_ref[:, :slots] = partial_ref[...] + found[...]
-        picked_ref[:, slots:] = params_ref[...]
-
-
-def faces(pos, listed, count, u, k, lo, hi, states, partial, params):
-    m, layers, nx, ny = u.shape
+
+def faces(u, k, lo, hi, states):
+    m, layers, nx, ny = states.shape
     per = 16
     face = pl.BlockSpec((per, 1, nx, ny), lambda g, s: (g, s * (layers - 1), 0, 0))
     halo = pl.BlockSpec((2, per, nx, ny), lambda g, s: (0, g, 0, 0))
-    flat = pl.BlockSpec(partial.shape, lambda g, s: (0, 0))
-    small = pl.BlockSpec(params.shape, lambda g, s: (0, 0))
-    both = (m, partial.shape[1] + params.shape[1])
     return pl.pallas_call(
         faces_kernel,
         grid=(m // per, 2),
-        in_specs=[pl.BlockSpec(memory_space=pltpu.SMEM)] * 3 + [face, face, halo, halo, face, flat, small],
-        out_specs=[face, pl.BlockSpec(both, lambda g, s: (0, 0))],
-        out_shape=[
-            jax.ShapeDtypeStruct(states.shape, F32),
-            jax.ShapeDtypeStruct(both, F32),
-        ],
-        scratch_shapes=[
-            pltpu.VMEM((m * (2 * nx + PAD), ny), F32),
-            pltpu.VMEM(partial.shape, F32),
-        ],
-        input_output_aliases={7: 0},
-        compiler_params=pltpu.CompilerParams(vmem_limit_bytes=32 << 20),
+        in_specs=[face, face, halo, halo, face],
+        out_specs=face,
+        out_shape=jax.ShapeDtypeStruct(states.shape, F32),
+        input_output_aliases={4: 0},
+        compiler_params=pltpu.CompilerParams(vmem_limit_bytes=58 << 20),
         cost_estimate=pl.CostEstimate(
             flops=8 * m * nx * ny, bytes_accessed=24 * m * nx * ny, transcendentals=0
         ),
-    )(pos, listed, count, u, k, lo, hi, states, partial, params)
+    )(u, k, lo, hi, states)
 
 
 def contract(a, b, dims):
@@ -244,7 +228,7 @@
 
 
 def gram_kernel(scale, count_ref, core_ref, *refs):
-    blocks, (noise, values, std, sum_ref) = refs[:8], refs[8:]
+    blocks, (noise, values, std, sum_ref, anomaly_ref) = refs[:8], refs[8:]
     rows = blocks[0].shape[0]
     n = 4 * rows
     slots = noise.shape[1]
@@ -265,6 +249,9 @@
     on_second = contract(
         jnp.concatenate([first[n // 2 :], misfit], axis=0), second, ((1,), (1,))
     )
+    params = jnp.concatenate([b[:, slots:] for b in blocks], axis=0)
+    mean = jnp.sum(params, axis=0, keepdims=True) * (1.0 / (2 * n))
+    anomaly_ref[...] = (params - mean) * (1.0 / scale)
     is_first = core_ref[0] == 0
     sum_ref[:n] = on_first[:n]
     sum_ref[n : n + n // 2] = jnp.where(is_first, on_first[n : n + n // 2], on_second[: n // 2])
@@ -278,8 +265,11 @@
     return pl.pallas_call(
         lambda *refs: gram_kernel(ens_scale, *refs),
         in_specs=[pl.BlockSpec(memory_space=pltpu.SMEM)] * 2 + [vmem] * 11,
-        out_specs=vmem,
-        out_shape=jax.ShapeDtypeStruct((8 * rows, 4 * rows), F32),
+        out_specs=[vmem, vmem],
+        out_shape=[
+            jax.ShapeDtypeStruct((8 * rows, 4 * rows), F32),
+            jax.ShapeDtypeStruct((8 * rows, blocks[0].shape[1] - noise.shape[1]), F32),
+        ],
         compiler_params=pltpu.CompilerParams(vmem_limit_bytes=16 << 20),
     )(count, core, *blocks, noise, values.reshape(1, -1), std.reshape(1, -1))
 
@@ -398,13 +388,10 @@
     )(sums)
 
 
-def update_kernel(scale, core_ref, inv_ref, sum_ref, other_ref, *refs):
-    blocks, out_ref = refs[:8], refs[8]
+def update_kernel(core_ref, inv_ref, sum_ref, other_ref, anomaly_ref, params_ref, out_ref):
     n = inv_ref.shape[0]
-    half, rows = n // 2, blocks[0].shape[0]
-    width = out_ref.shape[1]
-    params = jnp.concatenate([b[:, -width:] for b in blocks], axis=0)
-    anomaly = (params - jnp.sum(params, axis=0, keepdims=True) * (1.0 / (2 * n))) * (1.0 / scale)
+    half, rows = n // 2, params_ref.shape[0]
+    anomaly = anomaly_ref[...]
     is_first = core_ref[0] == 0
     mine, theirs = sum_ref[n : n + half], other_ref[n : n + half]
     product = jnp.concatenate(
@@ -417,20 +404,20 @@
     x_second = contract(second, anomaly[n:] - down[:, n:], ((1,), (0,)))
     x_first = right[:, n:] - contract(right[:, :n], x_second, ((1,), (0,)))
     cross_first, cross_second = sum_ref[n + half : n + half + rows], sum_ref[n + half + rows :]
-    out_ref[...] = params[:rows] + (
+    out_ref[...] = params_ref[...] + (
         contract(cross_first, x_first, ((1,), (0,))) + contract(cross_second, x_second, ((1,), (0,)))
     )
 
 
-def update(core, inv, sums, other, blocks, width, ens_scale):
+def update(core, inv, sums, other, anomaly, params):
     vmem = pl.BlockSpec(memory_space=pltpu.VMEM)
     return pl.pallas_call(
-        lambda *refs: update_kernel(ens_scale, *refs),
-        in_specs=[pl.BlockSpec(memory_space=pltpu.SMEM)] + [vmem] * 11,
+        update_kernel,
+        in_specs=[pl.BlockSpec(memory_space=pltpu.SMEM)] + [vmem] * 5,
         out_specs=vmem,
-        out_shape=jax.ShapeDtypeStruct((blocks[0].shape[0], width), F32),
-        compiler_params=pltpu.CompilerParams(vmem_limit_bytes=16 << 20),
-    )(core, inv, sums, other, *blocks)
+        out_shape=jax.ShapeDtypeStruct(params.shape, F32),
+        compiler_params=pltpu.CompilerParams(vmem_limit_bytes=8 << 20),
+    )(core, inv, sums, other, anomaly, params)
 
 
 def around_x(a):
@@ -472,20 +459,21 @@
     head = jnp.stack([u[:, 0], k[:, 0]])
     lo = lax.ppermute(last, "space", [(i, i + 1) for i in range(spaces - 1)])
     hi = lax.ppermute(head, "space", [(i + 1, i) for i in range(spaces - 1)])
-    states, partial, listed, found = stencil(pos, u, k)
-    states, picked = faces(
-        pos, listed, found, u, k, lo, hi, states.reshape(u.shape), partial, params
-    )
-
+    cells = pos.reshape(1, -1)
+    states, partial = stencil(cells, u, k)
+    picked = readings(cells, head, last, lo, hi, partial, params, u.shape[1])
     mine = around_y(picked)
     blocks = mine + [partner(a) for a in mine]
 
     core = (lax.axis_index("ens") % 2).astype(jnp.int32).reshape(1)
-    sums = gram(count, core, blocks, noise, values, std, ens_scale)
-    sums = total4(around_z(total4(around_x(sums))))
+    sums, anomaly = gram(count, core, blocks, noise, values, std, ens_scale)
+    lo, hi, sums = lax.optimization_barrier((lo, hi, sums))
+    states = faces(u, k, lo, hi, states)
+    sums, states = lax.optimization_barrier((total4(around_x(sums)), states))
+    sums = total4(around_z(sums))
     other = partner(sums)
     inv = inverse(sums)
-    return update(core, inv, sums, other, blocks, params.shape[1], ens_scale), states
+    return update(core, inv, sums, other, anomaly, params), states
 
 
 def solution(mesh):

time: 93.5 us -> 86.2 us (0.922)
  waiting for transfers between devices: 16.3 us -> 6.69 us
  starting transfers between devices: 27.6 us -> 31.5 us
  Pallas kernels: 45.9 us -> 44.2 us
    ppermute x3, waiting for transfers between devices: 9.02 us -> 0.92 us  [around_x(): lax.ppermute(a, 'space', [(z * 4 + x, z * 4 + (x + s) % 4) for z in range...]
    ppermute x5, starting transfers between devices: 7.92 us -> 11 us  [partner(): return lax.ppermute(a, 'ens', [(e, e ^ 1) for e in range(8)])]
    pallas_call x3 -> x4, Pallas kernels: 40.6 us -> 38.9 us  [the longest x1 23.3 us: stencil(): pl.pallas_call(stencil_kernel, grid=(m // per,), in_specs=[pl.BlockSpec(p...]
    ppermute x3, waiting for transfers between devices: 5.79 us -> 4.48 us  [around_z(): lax.ppermute(a, 'space', [(z * 4 + x, (z + s) % 4 * 4 + x) for z in range...]
    ppermute x3, waiting for transfers between devices: 1.18 us -> 0.01 us  [around_y(): lax.ppermute(a, 'ens', [(e, (e + 2 * s) % 8) for e in range(8)])]
    ppermute x3, starting transfers between devices: 4.37 us -> 5.53 us  [around_x(): lax.ppermute(a, 'space', [(z * 4 + x, z * 4 + (x + s) % 4) for z in range...]
    ppermute x1, waiting for transfers between devices: 0.01 us -> 0.94 us  [shards(): hi = lax.ppermute(head, 'space', [(i + 1, i) for i in range(spaces - 1)])]
  transfers between devices with their start and end apart: 16 -> 16, of which waited for: 7 -> 6; matrix products, arithmetic and copies ran while one was open for 0% -> 0% of each run, Pallas kernels for 32% -> 38%
where the time goes in v3:
time: 86.2 us; the launch traced here: 86 us
  Pallas kernels  44.2 us (51%)
  starting transfers between devices  31.5 us (37%)
  waiting for transfers between devices  6.69 us (8%)
  local copies, waits for them, and re-layouts  1.94 us (2%)
  between operations  1.47 us (2%)
    pallas_call x1, Pallas kernels, stencil(): pl.pallas_call(stencil_kernel, grid=(m // per,), in_specs=[pl.BlockSpec(p...  23.3 us
    ppermute x5, starting transfers between devices, partner(): return lax.ppermute(a, 'ens', [(e, e ^ 1) for e in range(8)])  11 us
    pallas_call x1, Pallas kernels, update(): pl.pallas_call(update_kernel, in_specs=[pl.BlockSpec(memory_space=pltpu.S...  5.77 us
    ppermute x3, starting transfers between devices, around_x(): lax.ppermute(a, 'space', [(z * 4 + x, z * 4 + (x + s) % 4) for z in range...  5.53 us
    pallas_call x1, Pallas kernels, faces(): pl.pallas_call(faces_kernel, grid=(m // per, 2), in_specs=[face, face, ha...  5.17 us
    ppermute x3, starting transfers between devices, around_z(): lax.ppermute(a, 'space', [(z * 4 + x, (z + s) % 4 * 4 + x) for z in range...  4.85 us
    pallas_call x1, Pallas kernels, readings(): pl.pallas_call(lambda *refs: readings_kernel(layers - 1, *refs), in_specs...  4.68 us
    ppermute x3, waiting for transfers between devices, around_z(): lax.ppermute(a, 'space', [(z * 4 + x, (z + s) % 4 * 4 + x) for z in range...  4.48 us
  transfers between devices with their start and end apart: 16, of which 6 were waited for; matrix products, arithmetic and copies ran while one was open for 0% of the time, Pallas kernels for 38%

profile of v3, /device:TPU:1, one launch (start us, length us, event | category | flops | bytes accessed | tf_op | source)
XLA Modules:
  0.0 86.0 jit_solution(16043264006611339819)
XLA Ops:
  0.6 0.0 copy-start
  0.6 0.0 copy-start.1
  0.7 0.0 copy-start.6
  0.7 1.9 %slice_bitcast_fusion = (bf16[1,32,64,128]{3,2,1,0:T(8,128)(2,1)S(1)}, bf16[1,32,64,128]{3,2,1,0:T(8,128)(2,1)S(1)}, bf16[1,32,64,128]{3,2,1,0:T(8,128)(2,1)S(1)}, bf16[1,32,64,128]{3,2,1,0:T(8,128)(2,1)S(1)}) fusion(bf16[32,8,64,128]{3,2,1,0:T(8,128)(2,1)} %k_ref.3, bf16[32,8,64,128]{3,2,1,0:T(8,128)(2,1)} %u_ref.3), kind=kLoop, calls=%fused_computation.2 | loop fusion | bytes 4194304 | tf_op jit(solution)/shard_map/stack;squeeze | solution.py:459
  2.6 0.1 pad_maximum_fusion.refs_2_
  2.7 4.3 %collective-permute-start = (bf16[2,32,64,128]{3,2,1,0:T(8,128)(2,1)S(1)}, bf16[2,32,64,128]{3,2,1,0:T(8,128)(2,1)S(1)}, u32[]{:S(2)}, u32[]{:S(2)}) collective-permute-start(bf16[2,32,64,128]{3,2,1,0:T(8,128)(2,1)S(1)} %pad_maximum_fusion.refs_2_), channel_id=1, source_target_pairs={{0,1},{1,2},{2,3},{3,4},{4,5},{5,6},{6,7},{7,8},{8,9},{9,10},{10,1... | collective-permute-start | bytes 3145736 | tf_op jit(solution)/shard_map/ppermute | solution.py:460
  7.0 0.1 pad_maximum_fusion.1.refs_1_
  7.1 1.3 %collective-permute-start.1 = (bf16[2,32,64,128]{3,2,1,0:T(8,128)(2,1)S(1)}, bf16[2,32,64,128]{3,2,1,0:T(8,128)(2,1)S(1)}, u32[]{:S(2)}, u32[]{:S(2)}) collective-permute-start(bf16[2,32,64,128]{3,2,1,0:T(8,128)(2,1)S(1)} %pad_maximum_fusion.1.refs_1_), channel_id=1, source_target_pairs={{1,0},{2,1},{3,2},{4,3},{5,4},{6,5},{7,6},{8,7},{9,8},{10,9},{11,1... | collective-permute-start | bytes 3145736 | tf_op jit(solution)/shard_map/ppermute | solution.py:461
  8.4 0.0 copy-done
  8.4 0.0 copy-start.5
  8.4 23.3 %shard_map.95 = (f32[32,8,64,128]{3,2,1,0:T(8,128)}, f32[32,1024]{1,0:T(8,128)S(1)}) custom-call(s32[1,1024]{1,0:T(1,128)S(1)} %bitcast.20, bf16[32,8,64,128]{3,2,1,0:T(8,128)(2,1)S(1)} %copy-done.1, bf16[32,8,64,128]{3,2,1,0:T(8,128)(2,1)S(1)} %copy-done), custom_call_target="tpu_custom_call" | custom-call | flops 83886080 | bytes 16777216 | tf_op jit(solution)/shard_map/pallas_call | solution.py:114
  31.7 0.0 collective-permute-done.refs_3_.lo_ref
  31.7 0.9 %collective-permute-done.1.refs_4_.hi_ref = bf16[2,32,64,128]{3,2,1,0:T(8,128)(2,1)S(1)} collective-permute-done((bf16[2,32,64,128]{3,2,1,0:T(8,128)(2,1)S(1)}, bf16[2,32,64,128]{3,2,1,0:T(8,128)(2,1)S(1)}, u32[]{:S(2)}, u32[]{:S(2)}) %collective-permute-start.1) | collective-permute-done | bytes 1048608 | tf_op jit(solution)/shard_map/ppermute | solution.py:461
  32.7 4.7 %shard_map.96.refs_2_ = f32[32,1152]{1,0:T(8,128)S(1)} custom-call(s32[1,1024]{1,0:T(1,128)S(1)} %bitcast.21, bf16[2,32,64,128]{3,2,1,0:T(8,128)(2,1)S(1)} %pad_maximum_fusion.1.refs_1_, bf16[2,32,64,128]{3,2,1,0:T(8,128)(2,1)S(1)} %pad_maximum_fusion.refs_2_, bf16[2,32,64,128]{3,2,1,0:T(8,128)(2,1)S(1)} %collective-permute-done.refs_3_.lo_ref, ...), custom_call_target="tpu_custom_call" | custom-call | flops 2097152 | bytes 8388608 | tf_op jit(solution)/shard_map/pallas_call | solution.py:169
  37.4 3.0 %collective-permute-start.4 = (f32[32,1152]{1,0:T(8,128)S(1)}, f32[32,1152]{1,0:T(8,128)S(1)}, u32[]{:S(2)}, u32[]{:S(2)}) collective-permute-start(f32[32,1152]{1,0:T(8,128)S(1)} %shard_map.96.refs_2_), channel_id=1, source_target_pairs={{0,64},{16,80},{32,96},{48,112},{64,0},{80,16},{96,32},{112,48},{1... | collective-permute-start | bytes 442376 | tf_op jit(solution)/shard_map/ppermute | solution.py:443
  40.4 0.8 collective-permute-start.3
  41.1 0.7 collective-permute-start.2
  41.8 2.7 %collective-permute-start.5 = (f32[32,1152]{1,0:T(8,128)S(1)}, f32[32,1152]{1,0:T(8,128)S(1)}, u32[]{:S(2)}, u32[]{:S(2)}) collective-permute-start(f32[32,1152]{1,0:T(8,128)S(1)} %shard_map.96.refs_2_), channel_id=1, source_target_pairs={{0,16},{16,0},{32,48},{48,32},{64,80},{80,64},{96,112},{112,96},{1... | collective-permute-start | bytes 442376 | tf_op jit(solution)/shard_map/ppermute | solution.py:448
  44.5 0.0 collective-permute-done.4.refs_5_
  44.5 2.9 %collective-permute-start.8 = (f32[32,1152]{1,0:T(8,128)S(1)}, f32[32,1152]{1,0:T(8,128)S(1)}, u32[]{:S(2)}, u32[]{:S(2)}) collective-permute-start(f32[32,1152]{1,0:T(8,128)S(1)} %collective-permute-done.4.refs_5_), channel_id=1, source_target_pairs={{0,16},{16,0},{32,48},{48,32},{64,80},{80,64},{96,112},{112,96},{1... | collective-permute-start | bytes 442376 | tf_op jit(solution)/shard_map/ppermute | solution.py:448
  47.4 0.0 collective-permute-done.3.refs_4_
  47.4 1.3 %collective-permute-start.7 = (f32[32,1152]{1,0:T(8,128)S(1)}, f32[32,1152]{1,0:T(8,128)S(1)}, u32[]{:S(2)}, u32[]{:S(2)}) collective-permute-start(f32[32,1152]{1,0:T(8,128)S(1)} %collective-permute-done.3.refs_4_), channel_id=1, source_target_pairs={{0,16},{16,0},{32,48},{48,32},{64,80},{80,64},{96,112},{112,96},{1... | collective-permute-start | bytes 442376 | tf_op jit(solution)/shard_map/ppermute | solution.py:448
  48.7 0.0 collective-permute-done.2.refs_3_
  48.7 1.2 %collective-permute-start.6 = (f32[32,1152]{1,0:T(8,128)S(1)}, f32[32,1152]{1,0:T(8,128)S(1)}, u32[]{:S(2)}, u32[]{:S(2)}) collective-permute-start(f32[32,1152]{1,0:T(8,128)S(1)} %collective-permute-done.2.refs_3_), channel_id=1, source_target_pairs={{0,16},{16,0},{32,48},{48,32},{64,80},{80,64},{96,112},{112,96},{1... | collective-permute-start | bytes 442376 | tf_op jit(solution)/shard_map/ppermute | solution.py:448
  50.6 0.0 collective-permute-done.5.refs_6_
  50.6 0.0 collective-permute-done.8.refs_9_
  50.6 0.0 collective-permute-done.7.refs_8_
  50.6 0.3 collective-permute-done.6.refs_7_
  50.9 0.0 copy-done.4
  50.9 0.0 copy-done.8
  50.9 1.3 %shard_map.97 = (f32[256,128]{1,0:T(8,128)S(1)}, f32[256,128]{1,0:T(8,128)S(1)}) custom-call(s32[1]{0:T(128)S(6)} %copy.20.refs_0_, s32[1]{0:T(128)} %bitcast.refs_1_.core_ref, f32[32,1152]{1,0:T(8,128)S(1)} %shard_map.96.refs_2_, f32[32,1152]{1,0:T(8,128)S(1)} %collective-permute-done.2.refs_3_, f32[32,1152]{1,0:T(8,128)S(1)} %collective-permute-done.3.refs_4_, ...), custom_call_target="tpu_custom_call" | custom-call | tf_op jit(solution)/shard_map/pallas_call | solution.py:265
  52.3 2.6 %collective-permute-start.11 = (f32[256,128]{1,0:T(8,128)S(1)}, f32[256,128]{1,0:T(8,128)S(1)}, u32[]{:S(2)}, u32[]{:S(2)}) collective-permute-start(f32[256,128]{1,0:T(8,128)S(1)} %get-tuple-element.13), channel_id=1, source_target_pairs={{0,2},{1,3},{2,0},{3,1},{4,6},{5,7},{6,4},{7,5},{8,10},{9,11},{10,... | collective-permute-start | bytes 393224 | tf_op jit(solution)/shard_map/ppermute | solution.py:425
  54.8 2.5 %collective-permute-start.10 = (f32[256,128]{1,0:T(8,128)S(1)}, f32[256,128]{1,0:T(8,128)S(1)}, u32[]{:S(2)}, u32[]{:S(2)}) collective-permute-start(f32[256,128]{1,0:T(8,128)S(1)} %get-tuple-element.13), channel_id=1, source_target_pairs={{0,3},{1,0},{2,1},{3,2},{4,7},{5,4},{6,5},{7,6},{8,11},{9,8},{10,9... | collective-permute-start | bytes 393224 | tf_op jit(solution)/shard_map/ppermute | solution.py:425
  57.3 0.5 collective-permute-start.9
  57.8 5.2 %shard_map.98 = f32[32,8,64,128]{3,2,1,0:T(8,128)} custom-call(bf16[32,8,64,128]{3,2,1,0:T(8,128)(2,1)} %u_ref.3, bf16[32,8,64,128]{3,2,1,0:T(8,128)(2,1)} %k_ref.3, bf16[2,32,64,128]{3,2,1,0:T(8,128)(2,1)} %copy-done.2, bf16[2,32,64,128]{3,2,1,0:T(8,128)(2,1)} %copy-done.3, f32[32,8,64,128]{3,2,1,0:T(8,128)} %get-tuple-element.16.in_ref), custom_call_target="tpu_custom_call", output_to_operand_aliasing={{}: (4, {})} | custom-call | flops 2097152 | bytes 6291456 | tf_op jit(solution)/shard_map/pallas_call | solution.py:212
  63.0 0.0 collective-permute-done.11
  63.0 0.9 %collective-permute-done.10 = f32[256,128]{1,0:T(8,128)S(1)} collective-permute-done((f32[256,128]{1,0:T(8,128)S(1)}, f32[256,128]{1,0:T(8,128)S(1)}, u32[]{:S(2)}, u32[]{:S(2)}) %collective-permute-start.10) | collective-permute-done | bytes 131104 | tf_op jit(solution)/shard_map/ppermute | solution.py:425
  63.9 0.0 collective-permute-done.9
  63.9 3.4 %collective-permute-start.14 = (f32[256,128]{1,0:T(8,128)S(1)}, f32[256,128]{1,0:T(8,128)S(1)}, u32[]{:S(2)}, u32[]{:S(2)}) collective-permute-start(f32[256,128]{1,0:T(8,128)S(1)} %add_add_fusion.1), channel_id=1, source_target_pairs={{0,8},{1,9},{2,10},{3,11},{4,12},{5,13},{6,14},{7,15},{8,0},{9,1},... | collective-permute-start | bytes 393224 | tf_op jit(solution)/shard_map/ppermute | solution.py:434
  67.3 0.7 collective-permute-start.13
  68.0 0.7 collective-permute-start.12
  68.8 0.9 %collective-permute-done.14 = f32[256,128]{1,0:T(8,128)S(1)} collective-permute-done((f32[256,128]{1,0:T(8,128)S(1)}, f32[256,128]{1,0:T(8,128)S(1)}, u32[]{:S(2)}, u32[]{:S(2)}) %collective-permute-start.14) | collective-permute-done | bytes 131104 | tf_op jit(solution)/shard_map/ppermute | solution.py:434
  69.7 2.8 %collective-permute-done.13 = f32[256,128]{1,0:T(8,128)S(1)} collective-permute-done((f32[256,128]{1,0:T(8,128)S(1)}, f32[256,128]{1,0:T(8,128)S(1)}, u32[]{:S(2)}, u32[]{:S(2)}) %collective-permute-start.13) | collective-permute-done | bytes 131104 | tf_op jit(solution)/shard_map/ppermute | solution.py:434
  72.4 0.8 collective-permute-done.12
  73.3 3.0 %collective-permute-start.15 = (f32[256,128]{1,0:T(8,128)S(1)}, f32[256,128]{1,0:T(8,128)S(1)}, u32[]{:S(2)}, u32[]{:S(2)}) collective-permute-start(f32[256,128]{1,0:T(8,128)S(1)} %add_add_fusion.sum_ref), channel_id=1, source_target_pairs={{0,16},{16,0},{32,48},{48,32},{64,80},{80,64},{96,112},{112,96},{1... | collective-permute-start | bytes 393224 | tf_op jit(solution)/shard_map/ppermute | solution.py:448
  76.3 3.9 %shard_map.99.inv_ref = f32[128,128]{1,0:T(8,128)S(1)} custom-call(f32[256,128]{1,0:T(8,128)S(1)} %add_add_fusion.sum_ref), custom_call_target="tpu_custom_call" | custom-call | flops 4294967296 | bytes 1048576 | tf_op jit(solution)/shard_map/pallas_call | solution.py:381
  80.2 0.0 collective-permute-done.15.other_ref
  80.2 5.8 %shard_map.100 = f32[32,128]{1,0:T(8,128)} custom-call(s32[1]{0:T(128)} %bitcast.refs_1_.core_ref, f32[128,128]{1,0:T(8,128)S(1)} %shard_map.99.inv_ref, f32[256,128]{1,0:T(8,128)S(1)} %add_add_fusion.sum_ref, f32[256,128]{1,0:T(8,128)S(1)} %collective-permute-done.15.other_ref, f32[256,128]{1,0:T(8,128)S(1)} %get-tuple-element.18.anomaly_ref, ...), custom_call_target="tpu_custom_call" | custom-call | tf_op jit(solution)/shard_map/pallas_call | solution.py:414
  (13 shorter events, 0.1 us)
Async XLA Ops:
  0.6 7.7 %copy-start = (bf16[32,8,64,128]{3,2,1,0:T(8,128)(2,1)S(1)}, bf16[32,8,64,128]{3,2,1,0:T(8,128)(2,1)}, u32[]{:S(2)}) copy-start(bf16[32,8,64,128]{3,2,1,0:T(8,128)(2,1)} %k_ref.3) | copy-start | bytes 12582916
  0.6 7.7 %copy-start.1 = (bf16[32,8,64,128]{3,2,1,0:T(8,128)(2,1)S(1)}, bf16[32,8,64,128]{3,2,1,0:T(8,128)(2,1)}, u32[]{:S(2)}) copy-start(bf16[32,8,64,128]{3,2,1,0:T(8,128)(2,1)} %u_ref.3) | copy-start | bytes 12582916
  0.7 7.7 %copy-start.6 = (s32[1024]{0:T(1024)S(1)}, s32[1024]{0:T(1024)}, u32[]{:S(2)}) copy-start(s32[1024]{0:T(1024)} %param.10) | copy-start | bytes 12292
  2.7 29.0 %collective-permute-start = (bf16[2,32,64,128]{3,2,1,0:T(8,128)(2,1)S(1)}, bf16[2,32,64,128]{3,2,1,0:T(8,128)(2,1)S(1)}, u32[]{:S(2)}, u32[]{:S(2)}) collective-permute-start(bf16[2,32,64,128]{3,2,1,0:T(8,128)(2,1)S(1)} %pad_maximum_fusion.refs_2_), channel_id=1, source_target_pairs={{0,1},{1,2},{2,3},{3,4},{4,5},{5,6},{6,7},{7,8},{8,9},{9,10},{10,1... | collective-permute-start | bytes 3145736 | tf_op jit(solution)/shard_map/ppermute | solution.py:460
  7.1 25.6 %collective-permute-start.1 = (bf16[2,32,64,128]{3,2,1,0:T(8,128)(2,1)S(1)}, bf16[2,32,64,128]{3,2,1,0:T(8,128)(2,1)S(1)}, u32[]{:S(2)}, u32[]{:S(2)}) collective-permute-start(bf16[2,32,64,128]{3,2,1,0:T(8,128)(2,1)S(1)} %pad_maximum_fusion.1.refs_1_), channel_id=1, source_target_pairs={{1,0},{2,1},{3,2},{4,3},{5,4},{6,5},{7,6},{8,7},{9,8},{10,9},{11,1... | collective-permute-start | bytes 3145736 | tf_op jit(solution)/shard_map/ppermute | solution.py:461
  8.4 24.3 %copy-start.5 = (f32[32,128]{1,0:T(8,128)S(1)}, f32[32,128]{1,0:T(8,128)}, u32[]{:S(2)}) copy-start(f32[32,128]{1,0:T(8,128)} %params_ref.1) | copy-start | bytes 49156
  31.7 19.2 %copy-start.4 = (f32[32,1024]{1,0:T(8,128)S(1)}, f32[32,1024]{1,0:T(8,128)}, u32[]{:S(2)}) copy-start(f32[32,1024]{1,0:T(8,128)} %refs_10_.1) | copy-start | bytes 393220
  31.7 19.2 %copy-start.7 = (f32[1024]{0:T(1024)S(1)}, f32[1024]{0:T(1024)}, u32[]{:S(2)}) copy-start(f32[1024]{0:T(1024)} %param.12) | copy-start | bytes 12292
  31.7 19.2 %copy-start.8 = (f32[1024]{0:T(1024)S(1)}, f32[1024]{0:T(1024)}, u32[]{:S(2)}) copy-start(f32[1024]{0:T(1024)} %param.13) | copy-start | bytes 12292
  31.7 26.1 %copy-start.2 = (bf16[2,32,64,128]{3,2,1,0:T(8,128)(2,1)}, bf16[2,32,64,128]{3,2,1,0:T(8,128)(2,1)S(1)}, u32[]{:S(2)}) copy-start(bf16[2,32,64,128]{3,2,1,0:T(8,128)(2,1)S(1)} %collective-permute-done.refs_3_.lo_ref) | copy-start | bytes 3145732
  32.7 25.1 %copy-start.3 = (bf16[2,32,64,128]{3,2,1,0:T(8,128)(2,1)}, bf16[2,32,64,128]{3,2,1,0:T(8,128)(2,1)S(1)}, u32[]{:S(2)}) copy-start(bf16[2,32,64,128]{3,2,1,0:T(8,128)(2,1)S(1)} %collective-permute-done.1.refs_4_.hi_ref) | copy-start | bytes 3145732
  37.4 7.2 %collective-permute-start.4 = (f32[32,1152]{1,0:T(8,128)S(1)}, f32[32,1152]{1,0:T(8,128)S(1)}, u32[]{:S(2)}, u32[]{:S(2)}) collective-permute-start(f32[32,1152]{1,0:T(8,128)S(1)} %shard_map.96.refs_2_), channel_id=1, source_target_pairs={{0,64},{16,80},{32,96},{48,112},{64,0},{80,16},{96,32},{112,48},{1... | collective-permute-start | bytes 442376 | tf_op jit(solution)/shard_map/ppermute | solution.py:443
  40.4 7.1 %collective-permute-start.3 = (f32[32,1152]{1,0:T(8,128)S(1)}, f32[32,1152]{1,0:T(8,128)S(1)}, u32[]{:S(2)}, u32[]{:S(2)}) collective-permute-start(f32[32,1152]{1,0:T(8,128)S(1)} %shard_map.96.refs_2_), channel_id=1, source_target_pairs={{0,96},{16,112},{32,0},{48,16},{64,32},{80,48},{96,64},{112,80},{1... | collective-permute-start | bytes 442376 | tf_op jit(solution)/shard_map/ppermute | solution.py:443
  41.1 7.6 %collective-permute-start.2 = (f32[32,1152]{1,0:T(8,128)S(1)}, f32[32,1152]{1,0:T(8,128)S(1)}, u32[]{:S(2)}, u32[]{:S(2)}) collective-permute-start(f32[32,1152]{1,0:T(8,128)S(1)} %shard_map.96.refs_2_), channel_id=1, source_target_pairs={{0,32},{16,48},{32,64},{48,80},{64,96},{80,112},{96,0},{112,16},{1... | collective-permute-start | bytes 442376 | tf_op jit(solution)/shard_map/ppermute | solution.py:443
  41.8 8.7 %collective-permute-start.5 = (f32[32,1152]{1,0:T(8,128)S(1)}, f32[32,1152]{1,0:T(8,128)S(1)}, u32[]{:S(2)}, u32[]{:S(2)}) collective-permute-start(f32[32,1152]{1,0:T(8,128)S(1)} %shard_map.96.refs_2_), channel_id=1, source_target_pairs={{0,16},{16,0},{32,48},{48,32},{64,80},{80,64},{96,112},{112,96},{1... | collective-permute-start | bytes 442376 | tf_op jit(solution)/shard_map/ppermute | solution.py:448
  44.5 6.0 %collective-permute-start.8 = (f32[32,1152]{1,0:T(8,128)S(1)}, f32[32,1152]{1,0:T(8,128)S(1)}, u32[]{:S(2)}, u32[]{:S(2)}) collective-permute-start(f32[32,1152]{1,0:T(8,128)S(1)} %collective-permute-done.4.refs_5_), channel_id=1, source_target_pairs={{0,16},{16,0},{32,48},{48,32},{64,80},{80,64},{96,112},{112,96},{1... | collective-permute-start | bytes 442376 | tf_op jit(solution)/shard_map/ppermute | solution.py:448
  47.4 3.1 %collective-permute-start.7 = (f32[32,1152]{1,0:T(8,128)S(1)}, f32[32,1152]{1,0:T(8,128)S(1)}, u32[]{:S(2)}, u32[]{:S(2)}) collective-permute-start(f32[32,1152]{1,0:T(8,128)S(1)} %collective-permute-done.3.refs_4_), channel_id=1, source_target_pairs={{0,16},{16,0},{32,48},{48,32},{64,80},{80,64},{96,112},{112,96},{1... | collective-permute-start | bytes 442376 | tf_op jit(solution)/shard_map/ppermute | solution.py:448
  48.7 2.2 %collective-permute-start.6 = (f32[32,1152]{1,0:T(8,128)S(1)}, f32[32,1152]{1,0:T(8,128)S(1)}, u32[]{:S(2)}, u32[]{:S(2)}) collective-permute-start(f32[32,1152]{1,0:T(8,128)S(1)} %collective-permute-done.2.refs_3_), channel_id=1, source_target_pairs={{0,16},{16,0},{32,48},{48,32},{64,80},{80,64},{96,112},{112,96},{1... | collective-permute-start | bytes 442376 | tf_op jit(solution)/shard_map/ppermute | solution.py:448
  52.3 10.7 %collective-permute-start.11 = (f32[256,128]{1,0:T(8,128)S(1)}, f32[256,128]{1,0:T(8,128)S(1)}, u32[]{:S(2)}, u32[]{:S(2)}) collective-permute-start(f32[256,128]{1,0:T(8,128)S(1)} %get-tuple-element.13), channel_id=1, source_target_pairs={{0,2},{1,3},{2,0},{3,1},{4,6},{5,7},{6,4},{7,5},{8,10},{9,11},{10,... | collective-permute-start | bytes 393224 | tf_op jit(solution)/shard_map/ppermute | solution.py:425
  54.8 9.1 %collective-permute-start.10 = (f32[256,128]{1,0:T(8,128)S(1)}, f32[256,128]{1,0:T(8,128)S(1)}, u32[]{:S(2)}, u32[]{:S(2)}) collective-permute-start(f32[256,128]{1,0:T(8,128)S(1)} %get-tuple-element.13), channel_id=1, source_target_pairs={{0,3},{1,0},{2,1},{3,2},{4,7},{5,4},{6,5},{7,6},{8,11},{9,8},{10,9... | collective-permute-start | bytes 393224 | tf_op jit(solution)/shard_map/ppermute | solution.py:425
  57.3 6.6 %collective-permute-start.9 = (f32[256,128]{1,0:T(8,128)S(1)}, f32[256,128]{1,0:T(8,128)S(1)}, u32[]{:S(2)}, u32[]{:S(2)}) collective-permute-start(f32[256,128]{1,0:T(8,128)S(1)} %get-tuple-element.13), channel_id=1, source_target_pairs={{0,1},{1,2},{2,3},{3,0},{4,5},{5,6},{6,7},{7,4},{8,9},{9,10},{10,1... | collective-permute-start | bytes 393224 | tf_op jit(solution)/shard_map/ppermute | solution.py:425
  63.9 5.7 %collective-permute-start.14 = (f32[256,128]{1,0:T(8,128)S(1)}, f32[256,128]{1,0:T(8,128)S(1)}, u32[]{:S(2)}, u32[]{:S(2)}) collective-permute-start(f32[256,128]{1,0:T(8,128)S(1)} %add_add_fusion.1), channel_id=1, source_target_pairs={{0,8},{1,9},{2,10},{3,11},{4,12},{5,13},{6,14},{7,15},{8,0},{9,1},... | collective-permute-start | bytes 393224 | tf_op jit(solution)/shard_map/ppermute | solution.py:434
  67.3 5.1 %collective-permute-start.13 = (f32[256,128]{1,0:T(8,128)S(1)}, f32[256,128]{1,0:T(8,128)S(1)}, u32[]{:S(2)}, u32[]{:S(2)}) collective-permute-start(f32[256,128]{1,0:T(8,128)S(1)} %add_add_fusion.1), channel_id=1, source_target_pairs={{0,12},{1,13},{2,14},{3,15},{4,0},{5,1},{6,2},{7,3},{8,4},{9,5},{1... | collective-permute-start | bytes 393224 | tf_op jit(solution)/shard_map/ppermute | solution.py:434
  68.0 5.2 %collective-permute-start.12 = (f32[256,128]{1,0:T(8,128)S(1)}, f32[256,128]{1,0:T(8,128)S(1)}, u32[]{:S(2)}, u32[]{:S(2)}) collective-permute-start(f32[256,128]{1,0:T(8,128)S(1)} %add_add_fusion.1), channel_id=1, source_target_pairs={{0,4},{1,5},{2,6},{3,7},{4,8},{5,9},{6,10},{7,11},{8,12},{9,13},{1... | collective-permute-start | bytes 393224 | tf_op jit(solution)/shard_map/ppermute | solution.py:434
  73.3 6.9 %collective-permute-start.15 = (f32[256,128]{1,0:T(8,128)S(1)}, f32[256,128]{1,0:T(8,128)S(1)}, u32[]{:S(2)}, u32[]{:S(2)}) collective-permute-start(f32[256,128]{1,0:T(8,128)S(1)} %add_add_fusion.sum_ref), channel_id=1, source_target_pairs={{0,16},{16,0},{32,48},{48,32},{64,80},{80,64},{96,112},{112,96},{1... | collective-permute-start | bytes 393224 | tf_op jit(solution)/shard_map/ppermute | solution.py:448

commit v4 on v3

--- a/solution.py
+++ b/solution.py
@@ -48,7 +48,7 @@
     for c in range(0, slots, chunk):
         t = jnp.dot(pair[...], lanes[:, c : c + chunk], preferred_element_type=F32)
         hit = row == x[:, c : c + chunk]
-        for b in range(GROUP):
+        for b in range(pair.shape[0] // nx):
             part = jnp.where(hit, t[b * nx : (b + 1) * nx], 0.0)
             at = pl.ds(pl.multiple_of(base + b * 8, 8), 8)
             sums[at, c : c + chunk] = jnp.sum(part.reshape(nx // 8, 8, chunk), axis=0)
@@ -142,22 +142,22 @@
     lanes, pair, sums
 ):
     _, members, nx, ny = head_ref.shape
-    slots = partial_ref.shape[1]
+    slots, per = partial_ref.shape[1], pair.shape[0] // nx
     set_lanes(pos_ref[...], lanes, (0, last_layer), nx, ny)
     x = pos_ref[...] // ny % nx
 
     def group(q, _):
         def member(b, _):
             rows = pl.ds(pl.multiple_of(b * nx, nx), nx)
-            put(pair, rows, 0, face_flux(head_ref, lo_ref, q * GROUP + b))
-            put(pair, rows, 1, face_flux(last_ref, hi_ref, q * GROUP + b))
+            put(pair, rows, 0, face_flux(head_ref, lo_ref, q * per + b))
+            put(pair, rows, 1, face_flux(last_ref, hi_ref, q * per + b))
             return 0
 
-        lax.fori_loop(0, GROUP, member, 0, unroll=2)
-        pick(pair, lanes, x, sums, q * GROUP * 8, nx)
+        lax.fori_loop(0, per, member, 0, unroll=4)
+        pick(pair, lanes, x, sums, q * per * 8, nx)
         return 0
 
-    lax.fori_loop(0, members // GROUP, group, 0)
+    lax.fori_loop(0, members // per, group, 0)
     out_ref[:, :slots] = partial_ref[...] + add_eights(sums[...])
     out_ref[:, slots:] = params_ref[...]
 
@@ -173,54 +173,42 @@
         out_shape=jax.ShapeDtypeStruct((m, slots + params.shape[1]), F32),
         scratch_shapes=[
             pltpu.VMEM((4 * ny, slots), jnp.bfloat16),
-            pltpu.VMEM((GROUP * nx, 4 * ny), jnp.bfloat16),
+            pltpu.VMEM((2 * GROUP * nx, 4 * ny), jnp.bfloat16),
             pltpu.VMEM((8 * m, slots), F32),
         ],
-        compiler_params=pltpu.CompilerParams(vmem_limit_bytes=8 << 20),
+        compiler_params=pltpu.CompilerParams(vmem_limit_bytes=10 << 20),
         cost_estimate=pl.CostEstimate(
             flops=8 * m * nx * ny, bytes_accessed=8 << 20, transcendentals=0
         ),
     )(pos, head, last, lo, hi, partial, params)
 
 
-def faces_kernel(u_ref, k_ref, lo_ref, hi_ref, in_ref, out_ref):
-    side = pl.program_id(1)
-
-    def apply(halo):
-        def member(b, _):
-            u, k = u_ref[b, 0].astype(F32), k_ref[b, 0].astype(F32)
-            flux = (k + halo[1, b].astype(F32)) * (halo[0, b].astype(F32) - u)
-            out_ref[b, 0] = in_ref[b, 0] + (step_size * 0.5) * flux
-            return 0
-
-        lax.fori_loop(0, in_ref.shape[0], member, 0)
-
-    @pl.when(side == 0)
-    def _():
-        apply(lo_ref)
-
-    @pl.when(side == 1)
-    def _():
-        apply(hi_ref)
-
-
-def faces(u, k, lo, hi, states):
-    m, layers, nx, ny = states.shape
+def face_kernel(u_ref, k_ref, halo_ref, in_ref, out_ref):
+    def member(b, _):
+        u, k = u_ref[b, 0].astype(F32), k_ref[b, 0].astype(F32)
+        flux = (k + halo_ref[1, b].astype(F32)) * (halo_ref[0, b].astype(F32) - u)
+        out_ref[b, 0] = in_ref[b, 0] + (step_size * 0.5) * flux
+        return 0
+
+    lax.fori_loop(0, in_ref.shape[0], member, 0)
+
+
+def add_face(u, k, halo, states, layer):
+    m, _, nx, ny = states.shape
     per = 16
-    face = pl.BlockSpec((per, 1, nx, ny), lambda g, s: (g, s * (layers - 1), 0, 0))
-    halo = pl.BlockSpec((2, per, nx, ny), lambda g, s: (0, g, 0, 0))
-    return pl.pallas_call(
-        faces_kernel,
-        grid=(m // per, 2),
-        in_specs=[face, face, halo, halo, face],
+    face = pl.BlockSpec((per, 1, nx, ny), lambda g: (g, layer, 0, 0))
+    return pl.pallas_call(
+        face_kernel,
+        grid=(m // per,),
+        in_specs=[face, face, pl.BlockSpec((2, per, nx, ny), lambda g: (0, g, 0, 0)), face],
         out_specs=face,
         out_shape=jax.ShapeDtypeStruct(states.shape, F32),
-        input_output_aliases={4: 0},
+        input_output_aliases={3: 0},
         compiler_params=pltpu.CompilerParams(vmem_limit_bytes=58 << 20),
         cost_estimate=pl.CostEstimate(
-            flops=8 * m * nx * ny, bytes_accessed=24 * m * nx * ny, transcendentals=0
+            flops=4 * m * nx * ny, bytes_accessed=16 * m * nx * ny, transcendentals=0
         ),
-    )(u, k, lo, hi, states)
+    )(u, k, halo, states)
 
 
 def contract(a, b, dims):
@@ -253,10 +241,17 @@
     mean = jnp.sum(params, axis=0, keepdims=True) * (1.0 / (2 * n))
     anomaly_ref[...] = (params - mean) * (1.0 / scale)
     is_first = core_ref[0] == 0
-    sum_ref[:n] = on_first[:n]
-    sum_ref[n : n + n // 2] = jnp.where(is_first, on_first[n : n + n // 2], on_second[: n // 2])
-    sum_ref[n + n // 2 : n + n // 2 + rows] = on_first[n + n // 2 :]
-    sum_ref[n + n // 2 + rows :] = on_second[n // 2 :]
+    half = n // 2
+    left = lax.broadcasted_iota(jnp.int32, (half, n), 1) < half
+    sum_ref[:half] = jnp.where(left, on_first[:half], on_first[half:n])
+    turned = pltpu.roll(on_first[:half], half, 1)
+    sum_ref[half : half + half // 2] = jnp.where(
+        left[: half // 2], turned[: half // 2], on_first[half // 2 : half]
+    )
+    at = half + half // 2
+    sum_ref[at : at + half] = jnp.where(is_first, on_first[n : n + half], on_second[:half])
+    sum_ref[at + half : at + half + rows] = on_first[n + half :]
+    sum_ref[at + half + rows :] = on_second[half:]
 
 
 def gram(count, core, blocks, noise, values, std, ens_scale):
@@ -267,7 +262,7 @@
         in_specs=[pl.BlockSpec(memory_space=pltpu.SMEM)] * 2 + [vmem] * 11,
         out_specs=[vmem, vmem],
         out_shape=[
-            jax.ShapeDtypeStruct((8 * rows, 4 * rows), F32),
+            jax.ShapeDtypeStruct((7 * rows, 4 * rows), F32),
             jax.ShapeDtypeStruct((8 * rows, blocks[0].shape[1] - noise.shape[1]), F32),
         ],
         compiler_params=pltpu.CompilerParams(vmem_limit_bytes=16 << 20),
@@ -348,18 +343,24 @@
     return jnp.concatenate(tiles, axis=0)
 
 
-def spd_inverse(p):
-    n = p.shape[0]
-    if n <= 64:
-        return pivoted_inverse(p)
-    h = n // 2
-    corner, side = p[:h, :h], p[:h, h:]
-    first = spd_inverse(corner)
+def spd_inverse(corner, side, rest):
+    first = pivoted_inverse(corner)
     ahead = contract(first, side, ((1,), (0,)))
-    second = spd_inverse(p[h:, h:] - contract(side, ahead, ((0,), (0,))))
+    second = pivoted_inverse(rest - contract(side, ahead, ((0,), (0,))))
     mixed = contract(ahead, second, ((1,), (0,)))
     top = jnp.concatenate([first + contract(mixed, ahead, ((1,), (1,))), -mixed], axis=1)
     return jnp.concatenate([top, jnp.concatenate([-mixed.T, second], axis=1)], axis=0)
+
+
+def square(sum_ref):
+    h = sum_ref.shape[1] // 2
+    pair, side = sum_ref[:h], sum_ref[h : h + h // 2]
+    eye = identity(h)
+    return (
+        pair[:, :h] + eye,
+        jnp.concatenate([side[:, :h], side[:, h:]], axis=0),
+        pair[:, h:] + eye,
+    )
 
 
 def identity(n):
@@ -371,8 +372,7 @@
 
 
 def inverse_kernel(sum_ref, out_ref):
-    n = out_ref.shape[0]
-    out_ref[...] = spd_inverse(sum_ref[:n] + identity(n))
+    out_ref[...] = spd_inverse(*square(sum_ref))
 
 
 def inverse(sums):
@@ -393,17 +393,22 @@
     half, rows = n // 2, params_ref.shape[0]
     anomaly = anomaly_ref[...]
     is_first = core_ref[0] == 0
-    mine, theirs = sum_ref[n : n + half], other_ref[n : n + half]
+    at = half + half // 2
+    mine, theirs = sum_ref[at : at + half], other_ref[at : at + half]
     product = jnp.concatenate(
         [jnp.where(is_first, mine, theirs), jnp.where(is_first, theirs, mine)], axis=0
     )
     fs = jnp.where(is_first, product.T, product)
     right = contract(inv_ref[...], jnp.concatenate([fs, anomaly[:n]], axis=1), ((1,), (0,)))
     down = contract(fs, right, ((0,), (0,)))
-    second = spd_inverse(other_ref[:n] + identity(n) - down[:, :n])
+    corner, side, rest = square(other_ref)
+    second = spd_inverse(
+        corner - down[:half, :half], side - down[:half, half:n], rest - down[half:, half:n]
+    )
     x_second = contract(second, anomaly[n:] - down[:, n:], ((1,), (0,)))
     x_first = right[:, n:] - contract(right[:, :n], x_second, ((1,), (0,)))
-    cross_first, cross_second = sum_ref[n + half : n + half + rows], sum_ref[n + half + rows :]
+    at = at + half
+    cross_first, cross_second = sum_ref[at : at + rows], sum_ref[at + rows :]
     out_ref[...] = params_ref[...] + (
         contract(cross_first, x_first, ((1,), (0,))) + contract(cross_second, x_second, ((1,), (0,)))
     )
@@ -467,10 +472,12 @@
 
     core = (lax.axis_index("ens") % 2).astype(jnp.int32).reshape(1)
     sums, anomaly = gram(count, core, blocks, noise, values, std, ens_scale)
-    lo, hi, sums = lax.optimization_barrier((lo, hi, sums))
-    states = faces(u, k, lo, hi, states)
-    sums, states = lax.optimization_barrier((total4(around_x(sums)), states))
-    sums = total4(around_z(sums))
+    lo, sums = lax.optimization_barrier((lo, sums))
+    states = add_face(u, k, lo, states, 0)
+    sums, states, hi = lax.optimization_barrier((total4(around_x(sums)), states, hi))
+    parts = around_z(sums)
+    states = add_face(u, k, hi, states, u.shape[1] - 1)
+    sums, states = lax.optimization_barrier((total4(parts), states))
     other = partner(sums)
     inv = inverse(sums)
     return update(core, inv, sums, other, anomaly, params), states

time: 86.2 us -> 84.8 us (0.984)
  waiting for transfers between devices: 6.69 us -> 4.99 us
    ppermute x3, waiting for transfers between devices: 4.48 us -> 1.22 us  [around_z(): lax.ppermute(a, 'space', [(z * 4 + x, (z + s) % 4 * 4 + x) for z in range...]
    ppermute x3, waiting for transfers between devices: 0.92 us -> 2.49 us  [around_x(): lax.ppermute(a, 'space', [(z * 4 + x, z * 4 + (x + s) % 4) for z in range...]
    pallas_call x1 -> x2, Pallas kernels: 5.17 us -> 5.79 us  [add_face(): pl.pallas_call(face_kernel, grid=(m // per,), in_specs=[face, face, pl.Bl...]
  transfers between devices with their start and end apart: 16 -> 16, of which waited for: 6 -> 5; matrix products, arithmetic and copies ran while one was open for 0% -> 0% of each run, Pallas kernels for 38% -> 39%
where the time goes in v4:
time: 84.8 us; the launch traced here: 84.6 us
  Pallas kernels  44.3 us (52%)
  starting transfers between devices  31.6 us (37%)
  waiting for transfers between devices  4.99 us (6%)
  local copies, waits for them, and re-layouts  1.94 us (2%)
  between operations  1.47 us (2%)
    pallas_call x1, Pallas kernels, stencil(): pl.pallas_call(stencil_kernel, grid=(m // per,), in_specs=[pl.BlockSpec(p...  23.3 us
    ppermute x5, starting transfers between devices, partner(): return lax.ppermute(a, 'ens', [(e, e ^ 1) for e in range(8)])  11.2 us
    pallas_call x2, Pallas kernels, add_face(): pl.pallas_call(face_kernel, grid=(m // per,), in_specs=[face, face, pl.Bl...  5.79 us
    pallas_call x1, Pallas kernels, update(): pl.pallas_call(update_kernel, in_specs=[pl.BlockSpec(memory_space=pltpu.S...  5.77 us
    ppermute x3, starting transfers between devices, around_x(): lax.ppermute(a, 'space', [(z * 4 + x, z * 4 + (x + s) % 4) for z in range...  5.52 us
    ppermute x3, starting transfers between devices, around_z(): lax.ppermute(a, 'space', [(z * 4 + x, (z + s) % 4 * 4 + x) for z in range...  4.85 us
    ppermute x3, starting transfers between devices, around_y(): lax.ppermute(a, 'ens', [(e, (e + 2 * s) % 8) for e in range(8)])  4.46 us
    ppermute x1, starting transfers between devices, shards(): lo = lax.ppermute(last, 'space', [(i, i + 1) for i in range(spaces - 1)])  4.27 us
  transfers between devices with their start and end apart: 16, of which 5 were waited for; matrix products, arithmetic and copies ran while one was open for 0% of the time, Pallas kernels for 39%

profile of v4, /device:TPU:1, one launch (start us, length us, event | category | flops | bytes accessed | tf_op | source)
XLA Modules:
  0.0 84.6 jit_solution(9286616576997084708)
XLA Ops:
  0.6 0.0 copy-start
  0.6 0.0 copy-start.1
  0.7 0.0 copy-start.6
  0.7 1.9 %slice_bitcast_fusion = (bf16[1,32,64,128]{3,2,1,0:T(8,128)(2,1)S(1)}, bf16[1,32,64,128]{3,2,1,0:T(8,128)(2,1)S(1)}, bf16[1,32,64,128]{3,2,1,0:T(8,128)(2,1)S(1)}, bf16[1,32,64,128]{3,2,1,0:T(8,128)(2,1)S(1)}) fusion(bf16[32,8,64,128]{3,2,1,0:T(8,128)(2,1)} %k_ref.5, bf16[32,8,64,128]{3,2,1,0:T(8,128)(2,1)} %u_ref.5), kind=kLoop, calls=%fused_computation.2 | loop fusion | bytes 4194304 | tf_op jit(solution)/shard_map/stack;squeeze | solution.py:464
  2.6 0.1 pad_maximum_fusion.refs_2_
  2.7 4.3 %collective-permute-start = (bf16[2,32,64,128]{3,2,1,0:T(8,128)(2,1)S(1)}, bf16[2,32,64,128]{3,2,1,0:T(8,128)(2,1)S(1)}, u32[]{:S(2)}, u32[]{:S(2)}) collective-permute-start(bf16[2,32,64,128]{3,2,1,0:T(8,128)(2,1)S(1)} %pad_maximum_fusion.refs_2_), channel_id=1, source_target_pairs={{0,1},{1,2},{2,3},{3,4},{4,5},{5,6},{6,7},{7,8},{8,9},{9,10},{10,1... | collective-permute-start | bytes 3145736 | tf_op jit(solution)/shard_map/ppermute | solution.py:465
  7.0 0.1 pad_maximum_fusion.1.refs_1_
  7.1 1.3 %collective-permute-start.1 = (bf16[2,32,64,128]{3,2,1,0:T(8,128)(2,1)S(1)}, bf16[2,32,64,128]{3,2,1,0:T(8,128)(2,1)S(1)}, u32[]{:S(2)}, u32[]{:S(2)}) collective-permute-start(bf16[2,32,64,128]{3,2,1,0:T(8,128)(2,1)S(1)} %pad_maximum_fusion.1.refs_1_), channel_id=1, source_target_pairs={{1,0},{2,1},{3,2},{4,3},{5,4},{6,5},{7,6},{8,7},{9,8},{10,9},{11,1... | collective-permute-start | bytes 3145736 | tf_op jit(solution)/shard_map/ppermute | solution.py:466
  8.4 0.0 copy-done
  8.4 0.0 copy-start.5
  8.4 23.3 %shard_map.95 = (f32[32,8,64,128]{3,2,1,0:T(8,128)}, f32[32,1024]{1,0:T(8,128)S(1)}) custom-call(s32[1,1024]{1,0:T(1,128)S(1)} %bitcast.20, bf16[32,8,64,128]{3,2,1,0:T(8,128)(2,1)S(1)} %copy-done.1, bf16[32,8,64,128]{3,2,1,0:T(8,128)(2,1)S(1)} %copy-done), custom_call_target="tpu_custom_call" | custom-call | flops 83886080 | bytes 16777216 | tf_op jit(solution)/shard_map/pallas_call | solution.py:114
  31.7 0.0 collective-permute-done.refs_3_.halo_ref
  31.7 0.9 %collective-permute-done.1.refs_4_.halo_ref = bf16[2,32,64,128]{3,2,1,0:T(8,128)(2,1)S(1)} collective-permute-done((bf16[2,32,64,128]{3,2,1,0:T(8,128)(2,1)S(1)}, bf16[2,32,64,128]{3,2,1,0:T(8,128)(2,1)S(1)}, u32[]{:S(2)}, u32[]{:S(2)}) %collective-permute-start.1) | collective-permute-done | bytes 1048608 | tf_op jit(solution)/shard_map/ppermute | solution.py:466
  32.7 4.2 %shard_map.96.refs_2_ = f32[32,1152]{1,0:T(8,128)S(1)} custom-call(s32[1,1024]{1,0:T(1,128)S(1)} %bitcast.21, bf16[2,32,64,128]{3,2,1,0:T(8,128)(2,1)S(1)} %pad_maximum_fusion.1.refs_1_, bf16[2,32,64,128]{3,2,1,0:T(8,128)(2,1)S(1)} %pad_maximum_fusion.refs_2_, bf16[2,32,64,128]{3,2,1,0:T(8,128)(2,1)S(1)} %collective-permute-done.refs_3_.halo_ref, ...), custom_call_target="tpu_custom_call" | custom-call | flops 2097152 | bytes 8388608 | tf_op jit(solution)/shard_map/pallas_call | solution.py:169
  36.9 3.0 %collective-permute-start.4 = (f32[32,1152]{1,0:T(8,128)S(1)}, f32[32,1152]{1,0:T(8,128)S(1)}, u32[]{:S(2)}, u32[]{:S(2)}) collective-permute-start(f32[32,1152]{1,0:T(8,128)S(1)} %shard_map.96.refs_2_), channel_id=1, source_target_pairs={{0,64},{16,80},{32,96},{48,112},{64,0},{80,16},{96,32},{112,48},{1... | collective-permute-start | bytes 442376 | tf_op jit(solution)/shard_map/ppermute | solution.py:448
  39.9 0.8 collective-permute-start.3
  40.6 0.7 collective-permute-start.2
  41.3 2.7 %collective-permute-start.5 = (f32[32,1152]{1,0:T(8,128)S(1)}, f32[32,1152]{1,0:T(8,128)S(1)}, u32[]{:S(2)}, u32[]{:S(2)}) collective-permute-start(f32[32,1152]{1,0:T(8,128)S(1)} %shard_map.96.refs_2_), channel_id=1, source_target_pairs={{0,16},{16,0},{32,48},{48,32},{64,80},{80,64},{96,112},{112,96},{1... | collective-permute-start | bytes 442376 | tf_op jit(solution)/shard_map/ppermute | solution.py:453
  44.0 0.0 collective-permute-done.4.refs_5_
  44.0 2.9 %collective-permute-start.8 = (f32[32,1152]{1,0:T(8,128)S(1)}, f32[32,1152]{1,0:T(8,128)S(1)}, u32[]{:S(2)}, u32[]{:S(2)}) collective-permute-start(f32[32,1152]{1,0:T(8,128)S(1)} %collective-permute-done.4.refs_5_), channel_id=1, source_target_pairs={{0,16},{16,0},{32,48},{48,32},{64,80},{80,64},{96,112},{112,96},{1... | collective-permute-start | bytes 442376 | tf_op jit(solution)/shard_map/ppermute | solution.py:453
  46.9 0.0 collective-permute-done.3.refs_4_
  46.9 1.3 %collective-permute-start.7 = (f32[32,1152]{1,0:T(8,128)S(1)}, f32[32,1152]{1,0:T(8,128)S(1)}, u32[]{:S(2)}, u32[]{:S(2)}) collective-permute-start(f32[32,1152]{1,0:T(8,128)S(1)} %collective-permute-done.3.refs_4_), channel_id=1, source_target_pairs={{0,16},{16,0},{32,48},{48,32},{64,80},{80,64},{96,112},{112,96},{1... | collective-permute-start | bytes 442376 | tf_op jit(solution)/shard_map/ppermute | solution.py:453
  48.2 0.0 collective-permute-done.2.refs_3_
  48.2 1.2 %collective-permute-start.6 = (f32[32,1152]{1,0:T(8,128)S(1)}, f32[32,1152]{1,0:T(8,128)S(1)}, u32[]{:S(2)}, u32[]{:S(2)}) collective-permute-start(f32[32,1152]{1,0:T(8,128)S(1)} %collective-permute-done.2.refs_3_), channel_id=1, source_target_pairs={{0,16},{16,0},{32,48},{48,32},{64,80},{80,64},{96,112},{112,96},{1... | collective-permute-start | bytes 442376 | tf_op jit(solution)/shard_map/ppermute | solution.py:453
  50.1 0.0 collective-permute-done.5.refs_6_
  50.1 0.0 collective-permute-done.8.refs_9_
  50.1 0.0 collective-permute-done.7.refs_8_
  50.1 0.3 collective-permute-done.6.refs_7_
  50.4 0.0 copy-done.7
  50.4 1.4 %shard_map.97 = (f32[224,128]{1,0:T(8,128)S(1)}, f32[256,128]{1,0:T(8,128)S(1)}) custom-call(s32[1]{0:T(128)S(6)} %copy.22.refs_0_, s32[1]{0:T(128)} %bitcast.refs_1_.core_ref, f32[32,1152]{1,0:T(8,128)S(1)} %shard_map.96.refs_2_, f32[32,1152]{1,0:T(8,128)S(1)} %collective-permute-done.2.refs_3_, f32[32,1152]{1,0:T(8,128)S(1)} %collective-permute-done.3.refs_4_, ...), custom_call_target="tpu_custom_call" | custom-call | tf_op jit(solution)/shard_map/pallas_call | solution.py:260
  51.8 2.6 %collective-permute-start.11 = (f32[224,128]{1,0:T(8,128)S(1)}, f32[224,128]{1,0:T(8,128)S(1)}, u32[]{:S(2)}, u32[]{:S(2)}) collective-permute-start(f32[224,128]{1,0:T(8,128)S(1)} %get-tuple-element.15), channel_id=1, source_target_pairs={{0,2},{1,3},{2,0},{3,1},{4,6},{5,7},{6,4},{7,5},{8,10},{9,11},{10,... | collective-permute-start | bytes 344072 | tf_op jit(solution)/shard_map/ppermute | solution.py:430
  54.3 2.5 %collective-permute-start.10 = (f32[224,128]{1,0:T(8,128)S(1)}, f32[224,128]{1,0:T(8,128)S(1)}, u32[]{:S(2)}, u32[]{:S(2)}) collective-permute-start(f32[224,128]{1,0:T(8,128)S(1)} %get-tuple-element.15), channel_id=1, source_target_pairs={{0,3},{1,0},{2,1},{3,2},{4,7},{5,4},{6,5},{7,6},{8,11},{9,8},{10,9... | collective-permute-start | bytes 344072 | tf_op jit(solution)/shard_map/ppermute | solution.py:430
  56.8 0.5 collective-permute-start.9
  57.3 2.9 %shard_map.98.in_ref = f32[32,8,64,128]{3,2,1,0:T(8,128)} custom-call(bf16[32,8,64,128]{3,2,1,0:T(8,128)(2,1)} %u_ref.5, bf16[32,8,64,128]{3,2,1,0:T(8,128)(2,1)} %k_ref.5, bf16[2,32,64,128]{3,2,1,0:T(8,128)(2,1)} %copy-done.3, f32[32,8,64,128]{3,2,1,0:T(8,128)} %get-tuple-element.17.in_ref), custom_call_target="tpu_custom_call", output_to_operand_aliasing={{}: (3, {})} | custom-call | flops 1048576 | bytes 4194304 | tf_op jit(solution)/shard_map/pallas_call | solution.py:200
  60.2 0.0 collective-permute-done.11
  60.2 2.5 %collective-permute-done.10 = f32[224,128]{1,0:T(8,128)S(1)} collective-permute-done((f32[224,128]{1,0:T(8,128)S(1)}, f32[224,128]{1,0:T(8,128)S(1)}, u32[]{:S(2)}, u32[]{:S(2)}) %collective-permute-start.10) | collective-permute-done | bytes 114720 | tf_op jit(solution)/shard_map/ppermute | solution.py:430
  62.7 0.0 collective-permute-done.9
  62.7 3.4 %collective-permute-start.14 = (f32[224,128]{1,0:T(8,128)S(1)}, f32[224,128]{1,0:T(8,128)S(1)}, u32[]{:S(2)}, u32[]{:S(2)}) collective-permute-start(f32[224,128]{1,0:T(8,128)S(1)} %add_add_fusion.1), channel_id=1, source_target_pairs={{0,8},{1,9},{2,10},{3,11},{4,12},{5,13},{6,14},{7,15},{8,0},{9,1},... | collective-permute-start | bytes 344072 | tf_op jit(solution)/shard_map/ppermute | solution.py:439
  66.1 0.7 collective-permute-start.13
  66.8 0.7 collective-permute-start.12
  67.6 2.9 %shard_map.99 = f32[32,8,64,128]{3,2,1,0:T(8,128)} custom-call(bf16[32,8,64,128]{3,2,1,0:T(8,128)(2,1)} %u_ref.5, bf16[32,8,64,128]{3,2,1,0:T(8,128)(2,1)} %k_ref.5, bf16[2,32,64,128]{3,2,1,0:T(8,128)(2,1)} %copy-done.2, f32[32,8,64,128]{3,2,1,0:T(8,128)} %shard_map.98.in_ref), custom_call_target="tpu_custom_call", output_to_operand_aliasing={{}: (3, {})} | custom-call | flops 1048576 | bytes 4194304 | tf_op jit(solution)/shard_map/pallas_call | solution.py:200
  70.5 0.0 collective-permute-done.14
  70.5 0.3 collective-permute-done.13
  70.8 0.9 %collective-permute-done.12 = f32[224,128]{1,0:T(8,128)S(1)} collective-permute-done((f32[224,128]{1,0:T(8,128)S(1)}, f32[224,128]{1,0:T(8,128)S(1)}, u32[]{:S(2)}, u32[]{:S(2)}) %collective-permute-start.12) | collective-permute-done | bytes 114720 | tf_op jit(solution)/shard_map/ppermute | solution.py:439
  71.7 3.2 %collective-permute-start.15 = (f32[224,128]{1,0:T(8,128)S(1)}, f32[224,128]{1,0:T(8,128)S(1)}, u32[]{:S(2)}, u32[]{:S(2)}) collective-permute-start(f32[224,128]{1,0:T(8,128)S(1)} %add_add_fusion.sum_ref), channel_id=1, source_target_pairs={{0,16},{16,0},{32,48},{48,32},{64,80},{80,64},{96,112},{112,96},{1... | collective-permute-start | bytes 344072 | tf_op jit(solution)/shard_map/ppermute | solution.py:453
  74.9 3.9 %shard_map.100.inv_ref = f32[128,128]{1,0:T(8,128)S(1)} custom-call(f32[224,128]{1,0:T(8,128)S(1)} %add_add_fusion.sum_ref), custom_call_target="tpu_custom_call" | custom-call | flops 4294967296 | bytes 1048576 | tf_op jit(solution)/shard_map/pallas_call | solution.py:381
  78.8 0.0 collective-permute-done.15.other_ref
  78.8 5.8 %shard_map.101 = f32[32,128]{1,0:T(8,128)} custom-call(s32[1]{0:T(128)} %bitcast.refs_1_.core_ref, f32[128,128]{1,0:T(8,128)S(1)} %shard_map.100.inv_ref, f32[224,128]{1,0:T(8,128)S(1)} %add_add_fusion.sum_ref, f32[224,128]{1,0:T(8,128)S(1)} %collective-permute-done.15.other_ref, f32[256,128]{1,0:T(8,128)S(1)} %get-tuple-element.22.anomaly_ref, ...), custom_call_target="tpu_custom_call" | custom-call | tf_op jit(solution)/shard_map/pallas_call | solution.py:419
  (14 shorter events, 0.1 us)
Async XLA Ops:
  0.6 7.7 %copy-start = (bf16[32,8,64,128]{3,2,1,0:T(8,128)(2,1)S(1)}, bf16[32,8,64,128]{3,2,1,0:T(8,128)(2,1)}, u32[]{:S(2)}) copy-start(bf16[32,8,64,128]{3,2,1,0:T(8,128)(2,1)} %k_ref.5) | copy-start | bytes 12582916
  0.6 7.7 %copy-start.1 = (bf16[32,8,64,128]{3,2,1,0:T(8,128)(2,1)S(1)}, bf16[32,8,64,128]{3,2,1,0:T(8,128)(2,1)}, u32[]{:S(2)}) copy-start(bf16[32,8,64,128]{3,2,1,0:T(8,128)(2,1)} %u_ref.5) | copy-start | bytes 12582916
  0.7 7.7 %copy-start.6 = (s32[1024]{0:T(1024)S(1)}, s32[1024]{0:T(1024)}, u32[]{:S(2)}) copy-start(s32[1024]{0:T(1024)} %param.10) | copy-start | bytes 12292
  2.7 29.0 %collective-permute-start = (bf16[2,32,64,128]{3,2,1,0:T(8,128)(2,1)S(1)}, bf16[2,32,64,128]{3,2,1,0:T(8,128)(2,1)S(1)}, u32[]{:S(2)}, u32[]{:S(2)}) collective-permute-start(bf16[2,32,64,128]{3,2,1,0:T(8,128)(2,1)S(1)} %pad_maximum_fusion.refs_2_), channel_id=1, source_target_pairs={{0,1},{1,2},{2,3},{3,4},{4,5},{5,6},{6,7},{7,8},{8,9},{9,10},{10,1... | collective-permute-start | bytes 3145736 | tf_op jit(solution)/shard_map/ppermute | solution.py:465
  7.1 25.6 %collective-permute-start.1 = (bf16[2,32,64,128]{3,2,1,0:T(8,128)(2,1)S(1)}, bf16[2,32,64,128]{3,2,1,0:T(8,128)(2,1)S(1)}, u32[]{:S(2)}, u32[]{:S(2)}) collective-permute-start(bf16[2,32,64,128]{3,2,1,0:T(8,128)(2,1)S(1)} %pad_maximum_fusion.1.refs_1_), channel_id=1, source_target_pairs={{1,0},{2,1},{3,2},{4,3},{5,4},{6,5},{7,6},{8,7},{9,8},{10,9},{11,1... | collective-permute-start | bytes 3145736 | tf_op jit(solution)/shard_map/ppermute | solution.py:466
  8.4 24.3 %copy-start.5 = (f32[32,128]{1,0:T(8,128)S(1)}, f32[32,128]{1,0:T(8,128)}, u32[]{:S(2)}) copy-start(f32[32,128]{1,0:T(8,128)} %params_ref.1) | copy-start | bytes 49156
  31.7 18.7 %copy-start.4 = (f32[32,1024]{1,0:T(8,128)S(1)}, f32[32,1024]{1,0:T(8,128)}, u32[]{:S(2)}) copy-start(f32[32,1024]{1,0:T(8,128)} %refs_10_.1) | copy-start | bytes 393220
  31.7 18.7 %copy-start.7 = (f32[1024]{0:T(1024)S(1)}, f32[1024]{0:T(1024)}, u32[]{:S(2)}) copy-start(f32[1024]{0:T(1024)} %param.12) | copy-start | bytes 12292
  31.7 18.7 %copy-start.8 = (f32[1024]{0:T(1024)S(1)}, f32[1024]{0:T(1024)}, u32[]{:S(2)}) copy-start(f32[1024]{0:T(1024)} %param.13) | copy-start | bytes 12292
  31.7 25.6 %copy-start.3 = (bf16[2,32,64,128]{3,2,1,0:T(8,128)(2,1)}, bf16[2,32,64,128]{3,2,1,0:T(8,128)(2,1)S(1)}, u32[]{:S(2)}) copy-start(bf16[2,32,64,128]{3,2,1,0:T(8,128)(2,1)S(1)} %collective-permute-done.refs_3_.halo_ref) | copy-start | bytes 3145732
  32.7 27.5 %copy-start.2 = (bf16[2,32,64,128]{3,2,1,0:T(8,128)(2,1)}, bf16[2,32,64,128]{3,2,1,0:T(8,128)(2,1)S(1)}, u32[]{:S(2)}) copy-start(bf16[2,32,64,128]{3,2,1,0:T(8,128)(2,1)S(1)} %collective-permute-done.1.refs_4_.halo_ref) | copy-start | bytes 3145732
  36.9 7.2 %collective-permute-start.4 = (f32[32,1152]{1,0:T(8,128)S(1)}, f32[32,1152]{1,0:T(8,128)S(1)}, u32[]{:S(2)}, u32[]{:S(2)}) collective-permute-start(f32[32,1152]{1,0:T(8,128)S(1)} %shard_map.96.refs_2_), channel_id=1, source_target_pairs={{0,64},{16,80},{32,96},{48,112},{64,0},{80,16},{96,32},{112,48},{1... | collective-permute-start | bytes 442376 | tf_op jit(solution)/shard_map/ppermute | solution.py:448
  39.9 7.1 %collective-permute-start.3 = (f32[32,1152]{1,0:T(8,128)S(1)}, f32[32,1152]{1,0:T(8,128)S(1)}, u32[]{:S(2)}, u32[]{:S(2)}) collective-permute-start(f32[32,1152]{1,0:T(8,128)S(1)} %shard_map.96.refs_2_), channel_id=1, source_target_pairs={{0,96},{16,112},{32,0},{48,16},{64,32},{80,48},{96,64},{112,80},{1... | collective-permute-start | bytes 442376 | tf_op jit(solution)/shard_map/ppermute | solution.py:448
  40.6 7.6 %collective-permute-start.2 = (f32[32,1152]{1,0:T(8,128)S(1)}, f32[32,1152]{1,0:T(8,128)S(1)}, u32[]{:S(2)}, u32[]{:S(2)}) collective-permute-start(f32[32,1152]{1,0:T(8,128)S(1)} %shard_map.96.refs_2_), channel_id=1, source_target_pairs={{0,32},{16,48},{32,64},{48,80},{64,96},{80,112},{96,0},{112,16},{1... | collective-permute-start | bytes 442376 | tf_op jit(solution)/shard_map/ppermute | solution.py:448
  41.3 8.7 %collective-permute-start.5 = (f32[32,1152]{1,0:T(8,128)S(1)}, f32[32,1152]{1,0:T(8,128)S(1)}, u32[]{:S(2)}, u32[]{:S(2)}) collective-permute-start(f32[32,1152]{1,0:T(8,128)S(1)} %shard_map.96.refs_2_), channel_id=1, source_target_pairs={{0,16},{16,0},{32,48},{48,32},{64,80},{80,64},{96,112},{112,96},{1... | collective-permute-start | bytes 442376 | tf_op jit(solution)/shard_map/ppermute | solution.py:453
  44.0 6.0 %collective-permute-start.8 = (f32[32,1152]{1,0:T(8,128)S(1)}, f32[32,1152]{1,0:T(8,128)S(1)}, u32[]{:S(2)}, u32[]{:S(2)}) collective-permute-start(f32[32,1152]{1,0:T(8,128)S(1)} %collective-permute-done.4.refs_5_), channel_id=1, source_target_pairs={{0,16},{16,0},{32,48},{48,32},{64,80},{80,64},{96,112},{112,96},{1... | collective-permute-start | bytes 442376 | tf_op jit(solution)/shard_map/ppermute | solution.py:453
  46.9 3.1 %collective-permute-start.7 = (f32[32,1152]{1,0:T(8,128)S(1)}, f32[32,1152]{1,0:T(8,128)S(1)}, u32[]{:S(2)}, u32[]{:S(2)}) collective-permute-start(f32[32,1152]{1,0:T(8,128)S(1)} %collective-permute-done.3.refs_4_), channel_id=1, source_target_pairs={{0,16},{16,0},{32,48},{48,32},{64,80},{80,64},{96,112},{112,96},{1... | collective-permute-start | bytes 442376 | tf_op jit(solution)/shard_map/ppermute | solution.py:453
  48.2 2.2 %collective-permute-start.6 = (f32[32,1152]{1,0:T(8,128)S(1)}, f32[32,1152]{1,0:T(8,128)S(1)}, u32[]{:S(2)}, u32[]{:S(2)}) collective-permute-start(f32[32,1152]{1,0:T(8,128)S(1)} %collective-permute-done.2.refs_3_), channel_id=1, source_target_pairs={{0,16},{16,0},{32,48},{48,32},{64,80},{80,64},{96,112},{112,96},{1... | collective-permute-start | bytes 442376 | tf_op jit(solution)/shard_map/ppermute | solution.py:453
  51.8 8.4 %collective-permute-start.11 = (f32[224,128]{1,0:T(8,128)S(1)}, f32[224,128]{1,0:T(8,128)S(1)}, u32[]{:S(2)}, u32[]{:S(2)}) collective-permute-start(f32[224,128]{1,0:T(8,128)S(1)} %get-tuple-element.15), channel_id=1, source_target_pairs={{0,2},{1,3},{2,0},{3,1},{4,6},{5,7},{6,4},{7,5},{8,10},{9,11},{10,... | collective-permute-start | bytes 344072 | tf_op jit(solution)/shard_map/ppermute | solution.py:430
  54.3 8.4 %collective-permute-start.10 = (f32[224,128]{1,0:T(8,128)S(1)}, f32[224,128]{1,0:T(8,128)S(1)}, u32[]{:S(2)}, u32[]{:S(2)}) collective-permute-start(f32[224,128]{1,0:T(8,128)S(1)} %get-tuple-element.15), channel_id=1, source_target_pairs={{0,3},{1,0},{2,1},{3,2},{4,7},{5,4},{6,5},{7,6},{8,11},{9,8},{10,9... | collective-permute-start | bytes 344072 | tf_op jit(solution)/shard_map/ppermute | solution.py:430
  56.8 5.9 %collective-permute-start.9 = (f32[224,128]{1,0:T(8,128)S(1)}, f32[224,128]{1,0:T(8,128)S(1)}, u32[]{:S(2)}, u32[]{:S(2)}) collective-permute-start(f32[224,128]{1,0:T(8,128)S(1)} %get-tuple-element.15), channel_id=1, source_target_pairs={{0,1},{1,2},{2,3},{3,0},{4,5},{5,6},{6,7},{7,4},{8,9},{9,10},{10,1... | collective-permute-start | bytes 344072 | tf_op jit(solution)/shard_map/ppermute | solution.py:430
  62.7 7.7 %collective-permute-start.14 = (f32[224,128]{1,0:T(8,128)S(1)}, f32[224,128]{1,0:T(8,128)S(1)}, u32[]{:S(2)}, u32[]{:S(2)}) collective-permute-start(f32[224,128]{1,0:T(8,128)S(1)} %add_add_fusion.1), channel_id=1, source_target_pairs={{0,8},{1,9},{2,10},{3,11},{4,12},{5,13},{6,14},{7,15},{8,0},{9,1},... | collective-permute-start | bytes 344072 | tf_op jit(solution)/shard_map/ppermute | solution.py:439
  66.1 4.7 %collective-permute-start.13 = (f32[224,128]{1,0:T(8,128)S(1)}, f32[224,128]{1,0:T(8,128)S(1)}, u32[]{:S(2)}, u32[]{:S(2)}) collective-permute-start(f32[224,128]{1,0:T(8,128)S(1)} %add_add_fusion.1), channel_id=1, source_target_pairs={{0,12},{1,13},{2,14},{3,15},{4,0},{5,1},{6,2},{7,3},{8,4},{9,5},{1... | collective-permute-start | bytes 344072 | tf_op jit(solution)/shard_map/ppermute | solution.py:439
  66.8 4.9 %collective-permute-start.12 = (f32[224,128]{1,0:T(8,128)S(1)}, f32[224,128]{1,0:T(8,128)S(1)}, u32[]{:S(2)}, u32[]{:S(2)}) collective-permute-start(f32[224,128]{1,0:T(8,128)S(1)} %add_add_fusion.1), channel_id=1, source_target_pairs={{0,4},{1,5},{2,6},{3,7},{4,8},{5,9},{6,10},{7,11},{8,12},{9,13},{1... | collective-permute-start | bytes 344072 | tf_op jit(solution)/shard_map/ppermute | solution.py:439
  71.7 7.1 %collective-permute-start.15 = (f32[224,128]{1,0:T(8,128)S(1)}, f32[224,128]{1,0:T(8,128)S(1)}, u32[]{:S(2)}, u32[]{:S(2)}) collective-permute-start(f32[224,128]{1,0:T(8,128)S(1)} %add_add_fusion.sum_ref), channel_id=1, source_target_pairs={{0,16},{16,0},{32,48},{48,32},{64,80},{80,64},{96,112},{112,96},{1... | collective-permute-start | bytes 344072 | tf_op jit(solution)/shard_map/ppermute | solution.py:453

commit v5 on v4

--- a/solution.py
+++ b/solution.py
@@ -474,8 +474,8 @@
     sums, anomaly = gram(count, core, blocks, noise, values, std, ens_scale)
     lo, sums = lax.optimization_barrier((lo, sums))
     states = add_face(u, k, lo, states, 0)
-    sums, states, hi = lax.optimization_barrier((total4(around_x(sums)), states, hi))
-    parts = around_z(sums)
+    sums, states, hi = lax.optimization_barrier((total4(around_z(sums)), states, hi))
+    parts = around_x(sums)
     states = add_face(u, k, hi, states, u.shape[1] - 1)
     sums, states = lax.optimization_barrier((total4(parts), states))
     other = partner(sums)

time: 84.8 us -> 84.3 us (level)
    ppermute x3, starting transfers between devices: 5.52 us -> 3.28 us  [around_x(): lax.ppermute(a, 'space', [(z * 4 + x, z * 4 + (x + s) % 4) for z in range...]
    ppermute x3, starting transfers between devices: 4.85 us -> 6.53 us  [around_z(): lax.ppermute(a, 'space', [(z * 4 + x, (z + s) % 4 * 4 + x) for z in range...]
where the time goes in v5:
time: 84.3 us; the launch traced here: 84.1 us
  Pallas kernels  44.3 us (53%)
  starting transfers between devices  31 us (37%)
  waiting for transfers between devices  5.24 us (6%)
  local copies, waits for them, and re-layouts  1.94 us (2%)
  between operations  1.47 us (2%)
    pallas_call x1, Pallas kernels, stencil(): pl.pallas_call(stencil_kernel, grid=(m // per,), in_specs=[pl.BlockSpec(p...  23.3 us
    ppermute x5, starting transfers between devices, partner(): return lax.ppermute(a, 'ens', [(e, e ^ 1) for e in range(8)])  11.1 us
    ppermute x3, starting transfers between devices, around_z(): lax.ppermute(a, 'space', [(z * 4 + x, (z + s) % 4 * 4 + x) for z in range...  6.53 us
    pallas_call x2, Pallas kernels, add_face(): pl.pallas_call(face_kernel, grid=(m // per,), in_specs=[face, face, pl.Bl...  5.79 us
    pallas_call x1, Pallas kernels, update(): pl.pallas_call(update_kernel, in_specs=[pl.BlockSpec(memory_space=pltpu.S...  5.77 us
    ppermute x3, starting transfers between devices, around_y(): lax.ppermute(a, 'ens', [(e, (e + 2 * s) % 8) for e in range(8)])  4.46 us
    ppermute x1, starting transfers between devices, shards(): lo = lax.ppermute(last, 'space', [(i, i + 1) for i in range(spaces - 1)])  4.27 us
    pallas_call x1, Pallas kernels, readings(): pl.pallas_call(lambda *refs: readings_kernel(layers - 1, *refs), in_specs...  4.17 us
  transfers between devices with their start and end apart: 16, of which 5 were waited for; matrix products, arithmetic and copies ran while one was open for 0% of the time, Pallas kernels for 39%

profile of v5, /device:TPU:1, one launch (start us, length us, event | category | flops | bytes accessed | tf_op | source)
XLA Modules:
  0.0 84.1 jit_solution(4334177238763871581)
XLA Ops:
  0.6 0.0 copy-start
  0.6 0.0 copy-start.1
  0.7 0.0 copy-start.6
  0.7 1.9 %slice_bitcast_fusion = (bf16[1,32,64,128]{3,2,1,0:T(8,128)(2,1)S(1)}, bf16[1,32,64,128]{3,2,1,0:T(8,128)(2,1)S(1)}, bf16[1,32,64,128]{3,2,1,0:T(8,128)(2,1)S(1)}, bf16[1,32,64,128]{3,2,1,0:T(8,128)(2,1)S(1)}) fusion(bf16[32,8,64,128]{3,2,1,0:T(8,128)(2,1)} %k_ref.5, bf16[32,8,64,128]{3,2,1,0:T(8,128)(2,1)} %u_ref.5), kind=kLoop, calls=%fused_computation.2 | loop fusion | bytes 4194304 | tf_op jit(solution)/shard_map/stack;squeeze | solution.py:464
  2.6 0.1 pad_maximum_fusion.refs_2_
  2.7 4.3 %collective-permute-start = (bf16[2,32,64,128]{3,2,1,0:T(8,128)(2,1)S(1)}, bf16[2,32,64,128]{3,2,1,0:T(8,128)(2,1)S(1)}, u32[]{:S(2)}, u32[]{:S(2)}) collective-permute-start(bf16[2,32,64,128]{3,2,1,0:T(8,128)(2,1)S(1)} %pad_maximum_fusion.refs_2_), channel_id=1, source_target_pairs={{0,1},{1,2},{2,3},{3,4},{4,5},{5,6},{6,7},{7,8},{8,9},{9,10},{10,1... | collective-permute-start | bytes 3145736 | tf_op jit(solution)/shard_map/ppermute | solution.py:465
  7.0 0.1 pad_maximum_fusion.1.refs_1_
  7.1 1.3 %collective-permute-start.1 = (bf16[2,32,64,128]{3,2,1,0:T(8,128)(2,1)S(1)}, bf16[2,32,64,128]{3,2,1,0:T(8,128)(2,1)S(1)}, u32[]{:S(2)}, u32[]{:S(2)}) collective-permute-start(bf16[2,32,64,128]{3,2,1,0:T(8,128)(2,1)S(1)} %pad_maximum_fusion.1.refs_1_), channel_id=1, source_target_pairs={{1,0},{2,1},{3,2},{4,3},{5,4},{6,5},{7,6},{8,7},{9,8},{10,9},{11,1... | collective-permute-start | bytes 3145736 | tf_op jit(solution)/shard_map/ppermute | solution.py:466
  8.4 0.0 copy-done
  8.4 0.0 copy-done.1
  8.4 0.0 copy-start.5
  8.4 23.3 %shard_map.95 = (f32[32,8,64,128]{3,2,1,0:T(8,128)}, f32[32,1024]{1,0:T(8,128)S(1)}) custom-call(s32[1,1024]{1,0:T(1,128)S(1)} %bitcast.20, bf16[32,8,64,128]{3,2,1,0:T(8,128)(2,1)S(1)} %copy-done.1, bf16[32,8,64,128]{3,2,1,0:T(8,128)(2,1)S(1)} %copy-done), custom_call_target="tpu_custom_call" | custom-call | flops 83886080 | bytes 16777216 | tf_op jit(solution)/shard_map/pallas_call | solution.py:114
  31.7 0.0 collective-permute-done.refs_3_.halo_ref
  31.7 0.9 %collective-permute-done.1.refs_4_.halo_ref = bf16[2,32,64,128]{3,2,1,0:T(8,128)(2,1)S(1)} collective-permute-done((bf16[2,32,64,128]{3,2,1,0:T(8,128)(2,1)S(1)}, bf16[2,32,64,128]{3,2,1,0:T(8,128)(2,1)S(1)}, u32[]{:S(2)}, u32[]{:S(2)}) %collective-permute-start.1) | collective-permute-done | bytes 1048608 | tf_op jit(solution)/shard_map/ppermute | solution.py:466
  32.7 4.2 %shard_map.96.refs_2_ = f32[32,1152]{1,0:T(8,128)S(1)} custom-call(s32[1,1024]{1,0:T(1,128)S(1)} %bitcast.21, bf16[2,32,64,128]{3,2,1,0:T(8,128)(2,1)S(1)} %pad_maximum_fusion.1.refs_1_, bf16[2,32,64,128]{3,2,1,0:T(8,128)(2,1)S(1)} %pad_maximum_fusion.refs_2_, bf16[2,32,64,128]{3,2,1,0:T(8,128)(2,1)S(1)} %collective-permute-done.refs_3_.halo_ref, ...), custom_call_target="tpu_custom_call" | custom-call | flops 2097152 | bytes 8388608 | tf_op jit(solution)/shard_map/pallas_call | solution.py:169
  36.9 3.0 %collective-permute-start.4 = (f32[32,1152]{1,0:T(8,128)S(1)}, f32[32,1152]{1,0:T(8,128)S(1)}, u32[]{:S(2)}, u32[]{:S(2)}) collective-permute-start(f32[32,1152]{1,0:T(8,128)S(1)} %shard_map.96.refs_2_), channel_id=1, source_target_pairs={{0,64},{16,80},{32,96},{48,112},{64,0},{80,16},{96,32},{112,48},{1... | collective-permute-start | bytes 442376 | tf_op jit(solution)/shard_map/ppermute | solution.py:448
  39.9 0.8 collective-permute-start.3
  40.6 0.7 collective-permute-start.2
  41.3 2.7 %collective-permute-start.5 = (f32[32,1152]{1,0:T(8,128)S(1)}, f32[32,1152]{1,0:T(8,128)S(1)}, u32[]{:S(2)}, u32[]{:S(2)}) collective-permute-start(f32[32,1152]{1,0:T(8,128)S(1)} %shard_map.96.refs_2_), channel_id=1, source_target_pairs={{0,16},{16,0},{32,48},{48,32},{64,80},{80,64},{96,112},{112,96},{1... | collective-permute-start | bytes 442376 | tf_op jit(solution)/shard_map/ppermute | solution.py:453
  44.0 0.0 collective-permute-done.4.refs_5_
  44.0 2.9 %collective-permute-start.8 = (f32[32,1152]{1,0:T(8,128)S(1)}, f32[32,1152]{1,0:T(8,128)S(1)}, u32[]{:S(2)}, u32[]{:S(2)}) collective-permute-start(f32[32,1152]{1,0:T(8,128)S(1)} %collective-permute-done.4.refs_5_), channel_id=1, source_target_pairs={{0,16},{16,0},{32,48},{48,32},{64,80},{80,64},{96,112},{112,96},{1... | collective-permute-start | bytes 442376 | tf_op jit(solution)/shard_map/ppermute | solution.py:453
  46.9 0.0 collective-permute-done.3.refs_4_
  46.9 1.3 %collective-permute-start.7 = (f32[32,1152]{1,0:T(8,128)S(1)}, f32[32,1152]{1,0:T(8,128)S(1)}, u32[]{:S(2)}, u32[]{:S(2)}) collective-permute-start(f32[32,1152]{1,0:T(8,128)S(1)} %collective-permute-done.3.refs_4_), channel_id=1, source_target_pairs={{0,16},{16,0},{32,48},{48,32},{64,80},{80,64},{96,112},{112,96},{1... | collective-permute-start | bytes 442376 | tf_op jit(solution)/shard_map/ppermute | solution.py:453
  48.2 0.0 collective-permute-done.2.refs_3_
  48.2 1.2 %collective-permute-start.6 = (f32[32,1152]{1,0:T(8,128)S(1)}, f32[32,1152]{1,0:T(8,128)S(1)}, u32[]{:S(2)}, u32[]{:S(2)}) collective-permute-start(f32[32,1152]{1,0:T(8,128)S(1)} %collective-permute-done.2.refs_3_), channel_id=1, source_target_pairs={{0,16},{16,0},{32,48},{48,32},{64,80},{80,64},{96,112},{112,96},{1... | collective-permute-start | bytes 442376 | tf_op jit(solution)/shard_map/ppermute | solution.py:453
  50.1 0.0 collective-permute-done.5.refs_6_
  50.1 0.0 collective-permute-done.8.refs_9_
  50.1 0.0 collective-permute-done.7.refs_8_
  50.1 0.3 collective-permute-done.6.refs_7_
  50.4 1.4 %shard_map.97 = (f32[224,128]{1,0:T(8,128)S(1)}, f32[256,128]{1,0:T(8,128)S(1)}) custom-call(s32[1]{0:T(128)S(6)} %copy.22.refs_0_, s32[1]{0:T(128)} %bitcast.refs_1_.core_ref, f32[32,1152]{1,0:T(8,128)S(1)} %shard_map.96.refs_2_, f32[32,1152]{1,0:T(8,128)S(1)} %collective-permute-done.2.refs_3_, f32[32,1152]{1,0:T(8,128)S(1)} %collective-permute-done.3.refs_4_, ...), custom_call_target="tpu_custom_call" | custom-call | tf_op jit(solution)/shard_map/pallas_call | solution.py:260
  51.8 5.1 %collective-permute-start.11 = (f32[224,128]{1,0:T(8,128)S(1)}, f32[224,128]{1,0:T(8,128)S(1)}, u32[]{:S(2)}, u32[]{:S(2)}) collective-permute-start(f32[224,128]{1,0:T(8,128)S(1)} %get-tuple-element.15), channel_id=1, source_target_pairs={{0,8},{1,9},{2,10},{3,11},{4,12},{5,13},{6,14},{7,15},{8,0},{9,1},... | collective-permute-start | bytes 344072 | tf_op jit(solution)/shard_map/ppermute | solution.py:439
  56.8 0.4 collective-permute-start.10
  57.3 1.0 %collective-permute-start.9 = (f32[224,128]{1,0:T(8,128)S(1)}, f32[224,128]{1,0:T(8,128)S(1)}, u32[]{:S(2)}, u32[]{:S(2)}) collective-permute-start(f32[224,128]{1,0:T(8,128)S(1)} %get-tuple-element.15), channel_id=1, source_target_pairs={{0,4},{1,5},{2,6},{3,7},{4,8},{5,9},{6,10},{7,11},{8,12},{9,13},{1... | collective-permute-start | bytes 344072 | tf_op jit(solution)/shard_map/ppermute | solution.py:439
  58.3 2.9 %shard_map.98.in_ref = f32[32,8,64,128]{3,2,1,0:T(8,128)} custom-call(bf16[32,8,64,128]{3,2,1,0:T(8,128)(2,1)} %u_ref.5, bf16[32,8,64,128]{3,2,1,0:T(8,128)(2,1)} %k_ref.5, bf16[2,32,64,128]{3,2,1,0:T(8,128)(2,1)} %copy-done.3, f32[32,8,64,128]{3,2,1,0:T(8,128)} %get-tuple-element.17.in_ref), custom_call_target="tpu_custom_call", output_to_operand_aliasing={{}: (3, {})} | custom-call | flops 1048576 | bytes 4194304 | tf_op jit(solution)/shard_map/pallas_call | solution.py:200
  61.2 0.0 collective-permute-done.11
  61.2 1.8 %collective-permute-done.10 = f32[224,128]{1,0:T(8,128)S(1)} collective-permute-done((f32[224,128]{1,0:T(8,128)S(1)}, f32[224,128]{1,0:T(8,128)S(1)}, u32[]{:S(2)}, u32[]{:S(2)}) %collective-permute-start.10) | collective-permute-done | bytes 114720 | tf_op jit(solution)/shard_map/ppermute | solution.py:439
  63.0 0.0 collective-permute-done.9
  63.0 1.0 %collective-permute-start.14 = (f32[224,128]{1,0:T(8,128)S(1)}, f32[224,128]{1,0:T(8,128)S(1)}, u32[]{:S(2)}, u32[]{:S(2)}) collective-permute-start(f32[224,128]{1,0:T(8,128)S(1)} %add_add_fusion.1), channel_id=1, source_target_pairs={{0,2},{1,3},{2,0},{3,1},{4,6},{5,7},{6,4},{7,5},{8,10},{9,11},{10,... | collective-permute-start | bytes 344072 | tf_op jit(solution)/shard_map/ppermute | solution.py:430
  64.0 1.7 %collective-permute-start.13 = (f32[224,128]{1,0:T(8,128)S(1)}, f32[224,128]{1,0:T(8,128)S(1)}, u32[]{:S(2)}, u32[]{:S(2)}) collective-permute-start(f32[224,128]{1,0:T(8,128)S(1)} %add_add_fusion.1), channel_id=1, source_target_pairs={{0,3},{1,0},{2,1},{3,2},{4,7},{5,4},{6,5},{7,6},{8,11},{9,8},{10,9... | collective-permute-start | bytes 344072 | tf_op jit(solution)/shard_map/ppermute | solution.py:430
  65.8 0.5 collective-permute-start.12
  66.3 2.9 %shard_map.99 = f32[32,8,64,128]{3,2,1,0:T(8,128)} custom-call(bf16[32,8,64,128]{3,2,1,0:T(8,128)(2,1)} %u_ref.5, bf16[32,8,64,128]{3,2,1,0:T(8,128)(2,1)} %k_ref.5, bf16[2,32,64,128]{3,2,1,0:T(8,128)(2,1)} %copy-done.2, f32[32,8,64,128]{3,2,1,0:T(8,128)} %shard_map.98.in_ref), custom_call_target="tpu_custom_call", output_to_operand_aliasing={{}: (3, {})} | custom-call | flops 1048576 | bytes 4194304 | tf_op jit(solution)/shard_map/pallas_call | solution.py:200
  69.2 0.0 collective-permute-done.14
  69.2 0.8 %collective-permute-done.13 = f32[224,128]{1,0:T(8,128)S(1)} collective-permute-done((f32[224,128]{1,0:T(8,128)S(1)}, f32[224,128]{1,0:T(8,128)S(1)}, u32[]{:S(2)}, u32[]{:S(2)}) %collective-permute-start.13) | collective-permute-done | bytes 114720 | tf_op jit(solution)/shard_map/ppermute | solution.py:430
  70.0 1.3 %collective-permute-done.12 = f32[224,128]{1,0:T(8,128)S(1)} collective-permute-done((f32[224,128]{1,0:T(8,128)S(1)}, f32[224,128]{1,0:T(8,128)S(1)}, u32[]{:S(2)}, u32[]{:S(2)}) %collective-permute-start.12) | collective-permute-done | bytes 114720 | tf_op jit(solution)/shard_map/ppermute | solution.py:430
  71.4 3.0 %collective-permute-start.15 = (f32[224,128]{1,0:T(8,128)S(1)}, f32[224,128]{1,0:T(8,128)S(1)}, u32[]{:S(2)}, u32[]{:S(2)}) collective-permute-start(f32[224,128]{1,0:T(8,128)S(1)} %add_add_fusion.sum_ref), channel_id=1, source_target_pairs={{0,16},{16,0},{32,48},{48,32},{64,80},{80,64},{96,112},{112,96},{1... | collective-permute-start | bytes 344072 | tf_op jit(solution)/shard_map/ppermute | solution.py:453
  74.4 3.9 %shard_map.100.inv_ref = f32[128,128]{1,0:T(8,128)S(1)} custom-call(f32[224,128]{1,0:T(8,128)S(1)} %add_add_fusion.sum_ref), custom_call_target="tpu_custom_call" | custom-call | flops 4294967296 | bytes 1048576 | tf_op jit(solution)/shard_map/pallas_call | solution.py:381
  78.4 0.0 collective-permute-done.15.other_ref
  78.4 5.8 %shard_map.101 = f32[32,128]{1,0:T(8,128)} custom-call(s32[1]{0:T(128)} %bitcast.refs_1_.core_ref, f32[128,128]{1,0:T(8,128)S(1)} %shard_map.100.inv_ref, f32[224,128]{1,0:T(8,128)S(1)} %add_add_fusion.sum_ref, f32[224,128]{1,0:T(8,128)S(1)} %collective-permute-done.15.other_ref, f32[256,128]{1,0:T(8,128)S(1)} %get-tuple-element.22.anomaly_ref, ...), custom_call_target="tpu_custom_call" | custom-call | tf_op jit(solution)/shard_map/pallas_call | solution.py:419
  (14 shorter events, 0.1 us)
Async XLA Ops:
  0.6 7.7 %copy-start = (bf16[32,8,64,128]{3,2,1,0:T(8,128)(2,1)S(1)}, bf16[32,8,64,128]{3,2,1,0:T(8,128)(2,1)}, u32[]{:S(2)}) copy-start(bf16[32,8,64,128]{3,2,1,0:T(8,128)(2,1)} %k_ref.5) | copy-start | bytes 12582916
  0.6 7.7 %copy-start.1 = (bf16[32,8,64,128]{3,2,1,0:T(8,128)(2,1)S(1)}, bf16[32,8,64,128]{3,2,1,0:T(8,128)(2,1)}, u32[]{:S(2)}) copy-start(bf16[32,8,64,128]{3,2,1,0:T(8,128)(2,1)} %u_ref.5) | copy-start | bytes 12582916
  0.7 7.7 %copy-start.6 = (s32[1024]{0:T(1024)S(1)}, s32[1024]{0:T(1024)}, u32[]{:S(2)}) copy-start(s32[1024]{0:T(1024)} %param.10) | copy-start | bytes 12292
  2.7 29.0 %collective-permute-start = (bf16[2,32,64,128]{3,2,1,0:T(8,128)(2,1)S(1)}, bf16[2,32,64,128]{3,2,1,0:T(8,128)(2,1)S(1)}, u32[]{:S(2)}, u32[]{:S(2)}) collective-permute-start(bf16[2,32,64,128]{3,2,1,0:T(8,128)(2,1)S(1)} %pad_maximum_fusion.refs_2_), channel_id=1, source_target_pairs={{0,1},{1,2},{2,3},{3,4},{4,5},{5,6},{6,7},{7,8},{8,9},{9,10},{10,1... | collective-permute-start | bytes 3145736 | tf_op jit(solution)/shard_map/ppermute | solution.py:465
  7.1 25.6 %collective-permute-start.1 = (bf16[2,32,64,128]{3,2,1,0:T(8,128)(2,1)S(1)}, bf16[2,32,64,128]{3,2,1,0:T(8,128)(2,1)S(1)}, u32[]{:S(2)}, u32[]{:S(2)}) collective-permute-start(bf16[2,32,64,128]{3,2,1,0:T(8,128)(2,1)S(1)} %pad_maximum_fusion.1.refs_1_), channel_id=1, source_target_pairs={{1,0},{2,1},{3,2},{4,3},{5,4},{6,5},{7,6},{8,7},{9,8},{10,9},{11,1... | collective-permute-start | bytes 3145736 | tf_op jit(solution)/shard_map/ppermute | solution.py:466
  8.4 24.3 %copy-start.5 = (f32[32,128]{1,0:T(8,128)S(1)}, f32[32,128]{1,0:T(8,128)}, u32[]{:S(2)}) copy-start(f32[32,128]{1,0:T(8,128)} %params_ref.1) | copy-start | bytes 49156
  31.7 18.7 %copy-start.4 = (f32[32,1024]{1,0:T(8,128)S(1)}, f32[32,1024]{1,0:T(8,128)}, u32[]{:S(2)}) copy-start(f32[32,1024]{1,0:T(8,128)} %refs_10_.1) | copy-start | bytes 393220
  31.7 18.7 %copy-start.7 = (f32[1024]{0:T(1024)S(1)}, f32[1024]{0:T(1024)}, u32[]{:S(2)}) copy-start(f32[1024]{0:T(1024)} %param.12) | copy-start | bytes 12292
  31.7 18.7 %copy-start.8 = (f32[1024]{0:T(1024)S(1)}, f32[1024]{0:T(1024)}, u32[]{:S(2)}) copy-start(f32[1024]{0:T(1024)} %param.13) | copy-start | bytes 12292
  31.7 26.6 %copy-start.3 = (bf16[2,32,64,128]{3,2,1,0:T(8,128)(2,1)}, bf16[2,32,64,128]{3,2,1,0:T(8,128)(2,1)S(1)}, u32[]{:S(2)}) copy-start(bf16[2,32,64,128]{3,2,1,0:T(8,128)(2,1)S(1)} %collective-permute-done.refs_3_.halo_ref) | copy-start | bytes 3145732
  32.7 28.5 %copy-start.2 = (bf16[2,32,64,128]{3,2,1,0:T(8,128)(2,1)}, bf16[2,32,64,128]{3,2,1,0:T(8,128)(2,1)S(1)}, u32[]{:S(2)}) copy-start(bf16[2,32,64,128]{3,2,1,0:T(8,128)(2,1)S(1)} %collective-permute-done.1.refs_4_.halo_ref) | copy-start | bytes 3145732
  36.9 7.2 %collective-permute-start.4 = (f32[32,1152]{1,0:T(8,128)S(1)}, f32[32,1152]{1,0:T(8,128)S(1)}, u32[]{:S(2)}, u32[]{:S(2)}) collective-permute-start(f32[32,1152]{1,0:T(8,128)S(1)} %shard_map.96.refs_2_), channel_id=1, source_target_pairs={{0,64},{16,80},{32,96},{48,112},{64,0},{80,16},{96,32},{112,48},{1... | collective-permute-start | bytes 442376 | tf_op jit(solution)/shard_map/ppermute | solution.py:448
  39.9 7.1 %collective-permute-start.3 = (f32[32,1152]{1,0:T(8,128)S(1)}, f32[32,1152]{1,0:T(8,128)S(1)}, u32[]{:S(2)}, u32[]{:S(2)}) collective-permute-start(f32[32,1152]{1,0:T(8,128)S(1)} %shard_map.96.refs_2_), channel_id=1, source_target_pairs={{0,96},{16,112},{32,0},{48,16},{64,32},{80,48},{96,64},{112,80},{1... | collective-permute-start | bytes 442376 | tf_op jit(solution)/shard_map/ppermute | solution.py:448
  40.6 7.6 %collective-permute-start.2 = (f32[32,1152]{1,0:T(8,128)S(1)}, f32[32,1152]{1,0:T(8,128)S(1)}, u32[]{:S(2)}, u32[]{:S(2)}) collective-permute-start(f32[32,1152]{1,0:T(8,128)S(1)} %shard_map.96.refs_2_), channel_id=1, source_target_pairs={{0,32},{16,48},{32,64},{48,80},{64,96},{80,112},{96,0},{112,16},{1... | collective-permute-start | bytes 442376 | tf_op jit(solution)/shard_map/ppermute | solution.py:448
  41.3 8.7 %collective-permute-start.5 = (f32[32,1152]{1,0:T(8,128)S(1)}, f32[32,1152]{1,0:T(8,128)S(1)}, u32[]{:S(2)}, u32[]{:S(2)}) collective-permute-start(f32[32,1152]{1,0:T(8,128)S(1)} %shard_map.96.refs_2_), channel_id=1, source_target_pairs={{0,16},{16,0},{32,48},{48,32},{64,80},{80,64},{96,112},{112,96},{1... | collective-permute-start | bytes 442376 | tf_op jit(solution)/shard_map/ppermute | solution.py:453
  44.0 6.0 %collective-permute-start.8 = (f32[32,1152]{1,0:T(8,128)S(1)}, f32[32,1152]{1,0:T(8,128)S(1)}, u32[]{:S(2)}, u32[]{:S(2)}) collective-permute-start(f32[32,1152]{1,0:T(8,128)S(1)} %collective-permute-done.4.refs_5_), channel_id=1, source_target_pairs={{0,16},{16,0},{32,48},{48,32},{64,80},{80,64},{96,112},{112,96},{1... | collective-permute-start | bytes 442376 | tf_op jit(solution)/shard_map/ppermute | solution.py:453
  46.9 3.1 %collective-permute-start.7 = (f32[32,1152]{1,0:T(8,128)S(1)}, f32[32,1152]{1,0:T(8,128)S(1)}, u32[]{:S(2)}, u32[]{:S(2)}) collective-permute-start(f32[32,1152]{1,0:T(8,128)S(1)} %collective-permute-done.3.refs_4_), channel_id=1, source_target_pairs={{0,16},{16,0},{32,48},{48,32},{64,80},{80,64},{96,112},{112,96},{1... | collective-permute-start | bytes 442376 | tf_op jit(solution)/shard_map/ppermute | solution.py:453
  48.2 2.2 %collective-permute-start.6 = (f32[32,1152]{1,0:T(8,128)S(1)}, f32[32,1152]{1,0:T(8,128)S(1)}, u32[]{:S(2)}, u32[]{:S(2)}) collective-permute-start(f32[32,1152]{1,0:T(8,128)S(1)} %collective-permute-done.2.refs_3_), channel_id=1, source_target_pairs={{0,16},{16,0},{32,48},{48,32},{64,80},{80,64},{96,112},{112,96},{1... | collective-permute-start | bytes 442376 | tf_op jit(solution)/shard_map/ppermute | solution.py:453
  51.8 9.4 %collective-permute-start.11 = (f32[224,128]{1,0:T(8,128)S(1)}, f32[224,128]{1,0:T(8,128)S(1)}, u32[]{:S(2)}, u32[]{:S(2)}) collective-permute-start(f32[224,128]{1,0:T(8,128)S(1)} %get-tuple-element.15), channel_id=1, source_target_pairs={{0,8},{1,9},{2,10},{3,11},{4,12},{5,13},{6,14},{7,15},{8,0},{9,1},... | collective-permute-start | bytes 344072 | tf_op jit(solution)/shard_map/ppermute | solution.py:439
  56.8 6.1 %collective-permute-start.10 = (f32[224,128]{1,0:T(8,128)S(1)}, f32[224,128]{1,0:T(8,128)S(1)}, u32[]{:S(2)}, u32[]{:S(2)}) collective-permute-start(f32[224,128]{1,0:T(8,128)S(1)} %get-tuple-element.15), channel_id=1, source_target_pairs={{0,12},{1,13},{2,14},{3,15},{4,0},{5,1},{6,2},{7,3},{8,4},{9,5},{1... | collective-permute-start | bytes 344072 | tf_op jit(solution)/shard_map/ppermute | solution.py:439
  57.3 5.7 %collective-permute-start.9 = (f32[224,128]{1,0:T(8,128)S(1)}, f32[224,128]{1,0:T(8,128)S(1)}, u32[]{:S(2)}, u32[]{:S(2)}) collective-permute-start(f32[224,128]{1,0:T(8,128)S(1)} %get-tuple-element.15), channel_id=1, source_target_pairs={{0,4},{1,5},{2,6},{3,7},{4,8},{5,9},{6,10},{7,11},{8,12},{9,13},{1... | collective-permute-start | bytes 344072 | tf_op jit(solution)/shard_map/ppermute | solution.py:439
  63.0 6.2 %collective-permute-start.14 = (f32[224,128]{1,0:T(8,128)S(1)}, f32[224,128]{1,0:T(8,128)S(1)}, u32[]{:S(2)}, u32[]{:S(2)}) collective-permute-start(f32[224,128]{1,0:T(8,128)S(1)} %add_add_fusion.1), channel_id=1, source_target_pairs={{0,2},{1,3},{2,0},{3,1},{4,6},{5,7},{6,4},{7,5},{8,10},{9,11},{10,... | collective-permute-start | bytes 344072 | tf_op jit(solution)/shard_map/ppermute | solution.py:430
  64.0 6.0 %collective-permute-start.13 = (f32[224,128]{1,0:T(8,128)S(1)}, f32[224,128]{1,0:T(8,128)S(1)}, u32[]{:S(2)}, u32[]{:S(2)}) collective-permute-start(f32[224,128]{1,0:T(8,128)S(1)} %add_add_fusion.1), channel_id=1, source_target_pairs={{0,3},{1,0},{2,1},{3,2},{4,7},{5,4},{6,5},{7,6},{8,11},{9,8},{10,9... | collective-permute-start | bytes 344072 | tf_op jit(solution)/shard_map/ppermute | solution.py:430
  65.8 5.6 %collective-permute-start.12 = (f32[224,128]{1,0:T(8,128)S(1)}, f32[224,128]{1,0:T(8,128)S(1)}, u32[]{:S(2)}, u32[]{:S(2)}) collective-permute-start(f32[224,128]{1,0:T(8,128)S(1)} %add_add_fusion.1), channel_id=1, source_target_pairs={{0,1},{1,2},{2,3},{3,0},{4,5},{5,6},{6,7},{7,4},{8,9},{9,10},{10,1... | collective-permute-start | bytes 344072 | tf_op jit(solution)/shard_map/ppermute | solution.py:430
  71.4 7.0 %collective-permute-start.15 = (f32[224,128]{1,0:T(8,128)S(1)}, f32[224,128]{1,0:T(8,128)S(1)}, u32[]{:S(2)}, u32[]{:S(2)}) collective-permute-start(f32[224,128]{1,0:T(8,128)S(1)} %add_add_fusion.sum_ref), channel_id=1, source_target_pairs={{0,16},{16,0},{32,48},{48,32},{64,80},{80,64},{96,112},{112,96},{1... | collective-permute-start | bytes 344072 | tf_op jit(solution)/shard_map/ppermute | solution.py:453
